TPU v7x, 128 devices: a whole 4x4x4 slice. The times are simulated.
128 devices in a mesh: inp: 4 (over y), tm: 32 (over x, z, core).
Axes of the slice: x: 4, y: 4, z: 4, core: 2. Of those that a mesh axis runs over, the one named last changes fastest.
Arguments:
- voltages: bfloat16 [1024, 128, 2048], P('inp', 'tm'), may hold values from -6 to 6
- window: float32 [4, 2048], replicated, may hold values from -0.0625 to 0.0625
Outputs:
- visibilities: float32 [512, 1024, 1024], P('tm', 'inp')
All inputs are finite; a program needn't handle non-finite values.
Results may differ from a plain program's by a relative error of at most 0.0051.
Values may be sent and summed in bfloat16 or wider, within the bound.
No kernel may reach another device: no remote copies, remote signals or barrier semaphores. Data moves between devices by JAX's collectives and lax.ppermute only.
A program may use at most 128 MiB of HBM per device.

v0:
```python
import math

import jax
import jax.numpy as jnp
from jax import lax
from jax.sharding import PartitionSpec as P

TAPS = 4
CH_DEV = 16
CH_FIRST = 512


def shifted(block, axis, distance):
    devices = range(lax.axis_size(axis))
    route = [(i - distance, i) for i in devices if i - distance in devices]
    return lax.ppermute(block, axis, route)


def tables(window, frame, chan_total):
    index = jnp.arange(frame, dtype=jnp.int32)
    bins = CH_FIRST + jnp.arange(chan_total, dtype=jnp.int32)
    phase = index[:, None] * bins[None, :] % frame
    angle = 2.0 * math.pi / frame * phase.astype(jnp.float32)
    table = jnp.concatenate([jnp.cos(angle), -jnp.sin(angle)], axis=1)
    return (window[:, :, None] * table[None, :, :]).astype(jnp.bfloat16)


def correlate(mine, other, row_ids, scale):
    chans, rows, _, times = mine.shape
    cols = other.shape[1]
    left = mine.reshape(chans, rows, 2 * times)
    flipped = jnp.concatenate([mine[:, :, 1, :], -mine[:, :, 0, :]], axis=2)
    right = other.reshape(chans, cols, 2 * times)
    re_plane = jnp.einsum("cik,cjk->cij", left, right, preferred_element_type=jnp.float32)
    im_plane = jnp.einsum("cik,cjk->cij", flipped, right, preferred_element_type=jnp.float32)
    col_ids = jnp.arange(cols, dtype=jnp.int32)
    upper = row_ids[:, None] <= col_ids[None, :]
    return jnp.where(upper[None, :, :], re_plane, im_plane) * scale


def body(voltages, window):
    inputs_dev, frames_dev, frame = voltages.shape
    chan_total = CH_DEV * lax.axis_size("tm")
    filt = tables(window, frame, chan_total)
    hold = TAPS - 1
    width = 2 * chan_total
    earlier = shifted(voltages[:, frames_dev - hold :, :], "tm", 1)
    joined = jnp.concatenate([earlier, voltages], axis=1)
    spectra = jnp.zeros((inputs_dev * frames_dev, width), jnp.float32)
    for tap in range(TAPS):
        frames = joined[:, hold - tap : hold - tap + frames_dev, :].reshape(-1, frame)
        spectra = spectra + jnp.dot(frames, filt[tap], preferred_element_type=jnp.float32)
    spectra = spectra.reshape(inputs_dev, frames_dev, width)
    rounded = spectra.astype(jnp.bfloat16).reshape(inputs_dev, frames_dev, 2, chan_total)
    turned = rounded.transpose(3, 0, 2, 1)
    row_ids = lax.axis_index("inp") * inputs_dev + jnp.arange(inputs_dev, dtype=jnp.int32)
    local = lax.all_to_all(turned, "tm", split_axis=0, concat_axis=3, tiled=True)
    scale = 1.0 / local.shape[3]
    return correlate(local, lax.all_gather(local, "inp", axis=1, tiled=True), row_ids, scale)


def solution(mesh):
    in_specs = (P("inp", "tm", None), P())
    out_specs = P("tm", "inp", None)
    return jax.shard_map(body, mesh=mesh, in_specs=in_specs, out_specs=out_specs, check_vma=False)
```

profile of v0, /device:TPU:2, one launch (start us, length us, event | category | flops | bytes accessed | tf_op | source)
XLA Modules:
  0.0 322.2 jit_solution(7198452374038717355)
XLA Ops:
  6.5 0.0 all-gather.2.cloned.1.call-start
  6.5 4.7 %slice.31 = bf16[256,3,2048]{2,1,0:T(4,128)(2,1)S(1)} slice(bf16[256,4,2048]{2,1,0:T(4,128)(2,1)} %param.2), slice={[0:256], [1:4], [0:2048]} | slice | bytes 6291456 | tf_op jit(solution)/shard_map/slice | solution.py:47
  11.2 2.3 copy.61
  13.5 2.1 collective-permute-start
  15.6 16.5 %fusion.20 = (f32[2048,512]{1,0:T(8,128)S(1)}, f32[2048,512]{1,0:T(8,128)S(1)}) fusion(s32[512]{0:T(512)S(1)} %iota_add_fusion), kind=kLoop, calls=%fused_computation.37 | loop fusion | flops 15728640 | bytes 8390656 | tf_op jit(solution)/shard_map/cos | solution.py:24
  32.2 4.6 %pad_maximum_fusion = f32[2048,1024]{1,0:T(8,128)} fusion(f32[2048,512]{1,0:T(8,128)S(1)} %get-tuple-element.11, f32[2048,512]{1,0:T(8,128)S(1)} %get-tuple-element.10), kind=kLoop, calls=%fused_computation.6 | loop fusion | flops 2097152 | bytes 16777216 | tf_op jit(solution)/shard_map/concatenate | solution.py:24
  36.8 0.0 copy-start.4
  36.8 6.9 %reshape.53 = bf16[1024,2048]{1,0:T(8,128)(2,1)} reshape(bf16[256,4,2048]{2,1,0:T(4,128)(2,1)} %param.2) | data formatting | bytes 8388608 | tf_op jit(solution)/shard_map/reshape | solution.py:51
  43.7 0.0 copy-done.4
  43.7 0.0 copy-start.3
  43.7 7.0 %multiply_convert_fusion = bf16[4,2048,1024]{2,1,0:T(8,128)(2,1)S(1)} fusion(f32[2048,1024]{1,0:T(8,128)} %pad_maximum_fusion, f32[4,2048]{1,0:T(4,128)S(1)} %copy-done.4), kind=kLoop, calls=%fused_computation | loop fusion | flops 16777216 | bytes 25198592 | tf_op jit(solution)/shard_map/convert_element_type | solution.py:25
  50.7 0.0 copy-start.2
  50.7 6.2 %copy-done.2 = bf16[4,2048,1024]{2,1,0:T(8,128)(2,1)} copy-done((bf16[4,2048,1024]{2,1,0:T(8,128)(2,1)}, bf16[4,2048,1024]{2,1,0:T(8,128)(2,1)S(1)}, u32[]{:S(2)}) %copy-start.2) | copy-done | bytes 16777240
  56.9 0.0 copy-done.3
  56.9 6.5 %fusion.8 = f32[1024,1024]{1,0:T(8,128)} fusion(bf16[1024,2048]{1,0:T(8,128)(2,1)S(1)} %copy-done.3, bf16[4,2048,1024]{2,1,0:T(8,128)(2,1)S(1)} %multiply_convert_fusion), kind=kOutput, calls=%fused_computation.23 | convolution fusion | flops 4294967296 | bytes 12582912 | tf_op jit(solution)/shard_map/dot_general | solution.py:52
  63.4 0.0 copy-start
  63.4 0.0 collective-permute-done
  63.4 4.7 %copy.44 = bf16[256,3,2048]{2,1,0:T(4,128)(2,1)S(1)} copy(bf16[256,3,2048]{2,0,1:T(8,128)(2,1)} %collective-permute-done) | data formatting | bytes 6291456 | tf_op jit(solution)/shard_map/ppermute | solution.py:16
  68.1 0.0 copy-done
  68.1 14.1 %fusion.4 = (bf16[256,4,2048]{2,1,0:T(4,128)(2,1)}, bf16[256,4,2048]{2,1,0:T(4,128)(2,1)}, bf16[256,4,2048]{2,1,0:T(4,128)(2,1)}) fusion(bf16[256,3,2048]{2,1,0:T(4,128)(2,1)S(1)} %copy.44, bf16[256,4,2048]{2,1,0:T(4,128)(2,1)S(1)} %copy-done), kind=kLoop, calls=%fused_computation.14 | loop fusion | flops 25165824 | bytes 19922944 | tf_op jit(solution)/shard_map/concatenate | solution.py:48
  82.3 6.9 %reshape.54 = bf16[1024,2048]{1,0:T(8,128)(2,1)} reshape(bf16[256,4,2048]{2,1,0:T(4,128)(2,1)} %get-tuple-element.5) | data formatting | bytes 8388608 | tf_op jit(solution)/shard_map/reshape | solution.py:51
  89.2 10.0 %fusion.7 = f32[1024,1024]{0,1:T(8,128)} fusion(bf16[1024,2048]{1,0:T(8,128)(2,1)} %reshape.54, bf16[4,2048,1024]{2,1,0:T(8,128)(2,1)} %copy-done.2), kind=kOutput, calls=%fused_computation.21 | convolution fusion | flops 4294967296 | bytes 12582912 | tf_op jit(solution)/shard_map/dot_general | solution.py:52
  99.2 7.0 %reshape.55 = bf16[1024,2048]{1,0:T(8,128)(2,1)} reshape(bf16[256,4,2048]{2,1,0:T(4,128)(2,1)} %get-tuple-element.7) | data formatting | bytes 8388608 | tf_op jit(solution)/shard_map/reshape | solution.py:51
  106.2 10.0 %fusion.6 = f32[1024,1024]{0,1:T(8,128)} fusion(bf16[1024,2048]{1,0:T(8,128)(2,1)} %reshape.55, bf16[4,2048,1024]{2,1,0:T(8,128)(2,1)} %copy-done.2), kind=kOutput, calls=%fused_computation.19 | convolution fusion | flops 4294967296 | bytes 12582912 | tf_op jit(solution)/shard_map/dot_general | solution.py:52
  116.2 6.9 %reshape.56 = bf16[1024,2048]{1,0:T(8,128)(2,1)} reshape(bf16[256,4,2048]{2,1,0:T(4,128)(2,1)} %get-tuple-element.6) | data formatting | bytes 8388608 | tf_op jit(solution)/shard_map/reshape | solution.py:51
  123.1 13.3 %fusion.11 = bf16[1024,1024]{0,1:T(8,128)(2,1)} fusion(f32[1024,1024]{0,1:T(8,128)} %fusion.6, f32[1024,1024]{0,1:T(8,128)} %fusion.7, f32[1024,1024]{1,0:T(8,128)} %fusion.8, bf16[1024,2048]{1,0:T(8,128)(2,1)} %reshape.56, bf16[4,2048,1024]{2,1,0:T(8,128)(2,1)} %copy-done.2), kind=kOutput, calls=%fused_computation.27 | convolution fusion | flops 4299161600 | bytes 23068672 | tf_op jit(solution)/shard_map/dot_general | solution.py:52
  136.3 2.9 copy.48
  139.2 2.8 convert_element_type.18
  141.9 5.5 %copy.49 = bf16[512,256,2,4]{1,3,2,0:T(4,128)(2,1)S(1)} copy(bf16[512,256,2,4]{0,2,3,1:T(2,128)(2,1)} %bitcast.42) | data formatting | bytes 4194304 | tf_op jit(solution)/shard_map/transpose | solution.py:55
  147.5 35.3 %all_to_all.18 = bf16[512,256,2,4]{1,3,2,0:T(4,128)(2,1)S(1)} all-to-all(bf16[512,256,2,4]{1,3,2,0:T(4,128)(2,1)S(1)} %copy.49), channel_id=1, replica_groups=mesh['inp'=4,'tm'=32] {'tm'}, dimensions={0} | all-to-all | bytes 4194304 | tf_op jit(solution)/shard_map/all_to_all | solution.py:57
  182.8 0.4 copy.50
  183.2 1.6 copy.51
  184.8 0.0 all-gather.2.cloned.1.call-update
  184.9 0.2 iota_compare_fusion
  185.1 1.7 fusion.22
  186.8 1.0 copy.63
  187.8 1.0 copy.62
  188.8 1.1 negate_bitcast_fusion
  189.9 82.9 %all-gather.2.cloned.1.call-done = bf16[16,1024,2,128]{1,0,3,2:T(8,128)(2,1)} async-done(((bf16[16,256,2,128]{1,0,3,2:T(8,128)(2,1)}), bf16[16,1024,2,128]{1,0,3,2:T(8,128)(2,1)}) %all-gather.2.cloned.1.call-update) | async-done | bytes 8388624 | tf_op jit(solution)/shard_map/all_gather | solution.py:59
  272.8 0.0 copy-start.1
  272.8 12.6 %copy.60 = bf16[16,1024,256]{2,1,0:T(8,128)(2,1)} copy(bf16[16,1024,256]{1,0,2:T(8,128)(2,1)} %bitcast.41) | data formatting | bytes 16777216 | tf_op jit(solution)/shard_map/reshape | solution.py:33
  285.3 0.0 copy-done.1
  285.4 12.6 %fusion.18 = f32[16,256,1024]{2,1,0:T(8,128)} fusion(bf16[16,1024,256]{2,1,0:T(8,128)(2,1)} %copy.60, bf16[16,256,256]{1,0,2:T(8,128)(2,1)S(1)} %bitcast.40), kind=kOutput, calls=%fused_computation.35 | convolution fusion | flops 2147483648 | bytes 27262976 | tf_op jit(solution)/shard_map/cik,cjk->cij/dot_general | solution.py:34
  297.9 17.2 %select_multiply_fusion = f32[16,256,1024]{2,1,0:T(8,128)} fusion(f32[16,256,1024]{2,1,0:T(8,128)} %fusion.18, bf16[16,1024,256]{2,1,0:T(8,128)(2,1)} %copy.60, pred[256,1024]{1,0:T(8,128)(4,1)S(1)} %iota_compare_fusion, bf16[16,256,128]{2,1,0:T(8,128)(2,1)} %negate_bitcast_fusion, bf16[16,256,128]{2,1,0:T(8,128)(2,1)S(1)} %bitcast.44), kind=kOutput, calls=%fused_computation.1 | convolution fusion | flops 2160066560 | bytes 44302336 | tf_op jit(solution)/shard_map/cik,cjk->cij/dot_general | solution.py:35
  (2 shorter events, 0.0 us)
Async XLA Ops:
  6.5 266.3 %all-gather.2.cloned.1.call-start = ((), (), s32[]{:S(2)}) async-start(), calls=%async_computation.1 | async-start | bytes 10485760 | tf_op jit(solution)/shard_map/all_gather | solution.py:59
  13.5 49.9 %collective-permute-start = (bf16[256,3,2048]{2,0,1:T(8,128)(2,1)S(1)}, bf16[256,3,2048]{2,0,1:T(8,128)(2,1)}, u32[]{:S(2)}, u32[]{:S(2)}) collective-permute-start(bf16[256,3,2048]{2,0,1:T(8,128)(2,1)S(1)} %copy.61), channel_id=1, source_target_pairs={{0,1},{1,2},{2,3},{3,4},{4,5},{5,6},{6,7},{7,8},{8,9},{9,10},{10,1... | collective-permute-start | bytes 9437192 | tf_op jit(solution)/shard_map/ppermute | solution.py:16
  36.8 6.9 %copy-start.4 = (f32[4,2048]{1,0:T(4,128)S(1)}, f32[4,2048]{1,0:T(4,128)}, u32[]{:S(2)}) copy-start(f32[4,2048]{1,0:T(4,128)} %param.3) | copy-start | bytes 98308
  43.7 13.1 %copy-start.3 = (bf16[1024,2048]{1,0:T(8,128)(2,1)S(1)}, bf16[1024,2048]{1,0:T(8,128)(2,1)}, u32[]{:S(2)}) copy-start(bf16[1024,2048]{1,0:T(8,128)(2,1)} %reshape.53) | copy-start | bytes 12582916
  50.7 6.2 %copy-start.2 = (bf16[4,2048,1024]{2,1,0:T(8,128)(2,1)}, bf16[4,2048,1024]{2,1,0:T(8,128)(2,1)S(1)}, u32[]{:S(2)}) copy-start(bf16[4,2048,1024]{2,1,0:T(8,128)(2,1)S(1)} %multiply_convert_fusion) | copy-start | bytes 50331652
  63.4 4.7 %copy-start = (bf16[256,4,2048]{2,1,0:T(4,128)(2,1)S(1)}, bf16[256,4,2048]{2,1,0:T(4,128)(2,1)}, u32[]{:S(2)}) copy-start(bf16[256,4,2048]{2,1,0:T(4,128)(2,1)} %param.2) | copy-start | bytes 12582916
  272.8 12.6 %copy-start.1 = (bf16[16,256,2,32,4]{1,0,4,3,2:T(8,128)(2,1)S(1)}, bf16[16,256,2,32,4]{1,0,4,3,2:T(8,128)(2,1)}, u32[]{:S(2)}) copy-start(bf16[16,256,2,32,4]{1,0,4,3,2:T(8,128)(2,1)} %copy.51) | copy-start | bytes 6291460
Sparse Core Ops, SparseCore 0:
  185.0 87.7 all-gather.1
where the time goes:
time: 328 us; the launch traced here: 322 us
  waiting for transfers between devices  82.9 us (25%)
  local copies, waits for them, and re-layouts  75 us (23%)
  matrix products  69.5 us (21%)
  other arithmetic  43.6 us (13%)
  blocking collectives  35.3 us (11%)
  between operations  13.8 us (4%)
    all_gather x1, waiting for transfers between devices, body(): lax.all_gather(local, 'inp', axis=1, tiled=True)  82.9 us
    dot_general x4, matrix products, body(): jnp.dot(frames, filt[tap], preferred_element_type=jnp.float32)  39.7 us
    all_to_all x1, blocking collectives, body(): lax.all_to_all(turned, 'tm', split_axis=0, concat_axis=3, tiled=True)  35.3 us
    reshape x4, local copies, waits for them, and re-layouts, body(): frames = joined[:, hold - tap:hold - tap + frames_dev, :].reshape(-1, frame)  27.7 us
    dot_general x1, matrix products, correlate(): jnp.einsum('cik,cjk->cij', flipped, right, preferred_element_type=jnp.flo...  17.2 us
    cos x1, other arithmetic, tables(): table = jnp.concatenate([jnp.cos(angle), -jnp.sin(angle)], axis=1)  16.5 us
    concatenate x1, other arithmetic, body(): joined = jnp.concatenate([earlier, voltages], axis=1)  14.1 us
    dot_general x1, matrix products, correlate(): jnp.einsum('cik,cjk->cij', left, right, preferred_element_type=jnp.float32)  12.6 us
  transfers between devices with their start and end apart: 2, of which 1 were waited for; matrix products, arithmetic and copies ran while one was open for 14% of the time, Pallas kernels for 0%

commit v1 on v0

v1 whole, which is shorter than its diff:
```python
import numpy as np

import jax
import jax.numpy as jnp
from jax import lax
from jax.experimental import pallas as pl
from jax.experimental.pallas import tpu as pltpu
from jax.sharding import PartitionSpec as P

FRAME = 2048
TAPS = 4
CH_FIRST = 512
QUARTER = FRAME // 4
CLASSES = 4
F32 = jnp.float32
BF16 = jnp.bfloat16
ROWS = 256
LANES = 256
VMEM = 48 * 1024 * 1024


def halves(x):
    high = x.astype(BF16)
    return high, (x - high.astype(F32)).astype(BF16)


def dft_tables():
    tables = []
    index = np.arange(QUARTER)
    for b in range(CLASSES):
        bins = CH_FIRST + b + CLASSES * np.arange(128)
        phase = (bins[:, None] * index[None, :]) % FRAME
        turn = np.exp(-2j * np.pi / FRAME * phase)
        if b % 2:
            turn = np.concatenate([turn, turn * (-1j if b == 1 else 1j)], axis=1)
        tables.append(np.stack([turn.real, turn.imag], axis=1).reshape(2 * len(bins), -1))
    both = np.concatenate(tables, axis=1)
    high = both.astype(BF16)
    return high, (both - high.astype(np.float64)).astype(BF16)


def spectra_kernel(times, groups, fine, v_hbm, w_ref, *refs):
    n = 2 if fine else 1
    tables_hbm, refs = refs[:n], refs[n:]
    outs, refs = refs[: len(groups)], refs[len(groups) :]
    frames, high, low, v_ref = refs[:4]
    tables = refs[4 : 4 + n]
    v_sem, table_sem = refs[4 + n :]
    classes = [b for group in groups for b in group]
    block = ROWS // TAPS
    sub = 16
    v_copies = [
        pltpu.make_async_copy(v_hbm.at[pl.ds(i * block, block)], v_ref.at[pl.ds(i * block, block)], v_sem.at[i])
        for i in range(ROWS // block)
    ]
    table_copies = [pltpu.make_async_copy(tables_hbm[k], tables[k], table_sem.at[k]) for k in range(n)]
    for copy in v_copies + table_copies:
        copy.start()

    to = lax.broadcasted_iota(jnp.int32, (ROWS, ROWS), 0)
    at = lax.broadcasted_iota(jnp.int32, (ROWS, ROWS), 1)
    sort = jnp.where(at == (to % block) * TAPS + to // block, 1.0, 0.0).astype(BF16)

    def per_block(i):
        v_copies[i].wait()
        x = v_ref[pl.ds(i * block, block)].reshape(ROWS, FRAME)
        frames[...] = jnp.dot(sort, x, preferred_element_type=F32)

        def per_rows(r, carry):
            for col in range(QUARTER // 128):
                spans = [pl.ds(m * QUARTER + col * 128, 128) for m in range(4)]
                taps = [[w_ref[pl.ds(j, 1), span] for span in spans] for j in range(TAPS)]
                parts = [
                    [frames[pl.ds(s * block + r * sub, sub), span] for span in spans]
                    for s in range(TAPS)
                ]
                for slot, t in enumerate(times):
                    u = []
                    for m in range(4):
                        terms = [taps[j][m] * parts[t - j][m] for j in range(TAPS) if 0 <= t - j < TAPS]
                        total = terms[0]
                        for term in terms[1:]:
                            total = total + term
                        u.append(total)
                    even, odd = u[0] + u[2], u[1] + u[3]
                    folded = {}
                    if 0 in classes:
                        folded[0] = even + odd
                    if 2 in classes:
                        folded[1] = even - odd
                    if 1 in classes or 3 in classes:
                        folded[2] = u[0] - u[2]
                        folded[3] = u[1] - u[3]
                    for f, value in folded.items():
                        where = slot, pl.ds(i * block + r * sub, sub), pl.ds(f * QUARTER + col * 128, 128)
                        if fine:
                            high[where], low[where] = halves(value)
                        else:
                            high[where] = value.astype(BF16)
            return carry

        lax.fori_loop(0, block // sub, per_rows, 0)

    for i in range(ROWS // block):
        per_block(i)
    spans = [slice(0, 512), slice(1024, 2048), slice(512, 1024), slice(1024, 2048)]
    columns = [slice(0, 512), slice(512, 1536), slice(1536, 2048), slice(2048, 3072)]
    contract = (((1,), (1,)), ((), ()))
    for copy in table_copies:
        copy.wait()

    def per_time(slot, carry):
        for b in classes:
            h = high[slot, :, spans[b]]
            table = tables[0][:, columns[b]]
            total = lax.dot_general(table, h, contract, preferred_element_type=F32)
            if fine:
                l = low[slot, :, spans[b]]
                total += lax.dot_general(table, l, contract, preferred_element_type=F32)
                total += lax.dot_general(tables[1][:, columns[b]], h, contract, preferred_element_type=F32)
            for group, out in zip(groups, outs):
                if b in group:
                    out[group.index(b) * len(times) + slot] = total.astype(out.dtype)
        return carry

    lax.fori_loop(0, len(times), per_time, 0)


def spectra(v, window, tables, times, groups, fine):
    def kernel(*refs):
        spectra_kernel(times, groups, fine, *refs)

    n = len(times)
    tables = tables if fine else tables[:1]
    anywhere = pl.BlockSpec(memory_space=pltpu.HBM)
    return pl.pallas_call(
        kernel,
        out_shape=[jax.ShapeDtypeStruct((n * len(g), 256, LANES), F32 if fine else BF16) for g in groups],
        in_specs=[anywhere, pl.BlockSpec()] + [anywhere] * len(tables),
        scratch_shapes=[
            pltpu.VMEM((ROWS, FRAME), F32),
            pltpu.VMEM((n, ROWS, FRAME), BF16),
            pltpu.VMEM((n if fine else 1, ROWS, FRAME), BF16),
            pltpu.VMEM((ROWS, TAPS, FRAME), BF16),
            *[pltpu.VMEM(t.shape, BF16) for t in tables],
            pltpu.SemaphoreType.DMA((4,)),
            pltpu.SemaphoreType.DMA((len(tables),)),
        ],
        compiler_params=pltpu.CompilerParams(vmem_limit_bytes=VMEM),
        cost_estimate=pl.CostEstimate(flops=n * sum(map(len, groups)) * 300000000, bytes_accessed=12 << 20, transcendentals=0),
        name="spectra",
    )(v, window, *tables)


def combine_kernel(order, parts, *refs):
    own, halo = refs[: len(order)], refs[len(order)]
    rows = refs[-1]
    outs = refs[len(refs) - 1 - parts : -1]
    size = 32 // parts
    for k, halo_at in enumerate(order):
        for half in range(LANES // 128):
            span = pl.ds(half * 128, 128)
            for t in range(TAPS):
                value = own[k][t, :, span]
                if t < TAPS - 1:
                    value = value + halo[halo_at * (TAPS - 1) + t, :, span].astype(F32)
                rows[half, pl.ds(t, 256, stride=TAPS), :] = value
            for part in range(parts):
                value = rows[half, pl.ds(part * size * 32, size * 32)].astype(BF16)
                outs[part][:, pl.ds(k * 32, 32), span] = value.reshape(size, 32, 128)


def combine(own, halo, order, parts, after=()):
    n = len(order)

    def kernel(*refs):
        combine_kernel(order, parts, *refs)

    return pl.pallas_call(
        kernel,
        out_shape=[jax.ShapeDtypeStruct((32 // parts, 32 * n, LANES), BF16)] * parts,
        in_specs=[pl.BlockSpec()] * (n + 1) + [pl.BlockSpec(memory_space=pltpu.HBM)] * len(after),
        scratch_shapes=[pltpu.VMEM((LANES // 128, 1024, 128), F32)],
        compiler_params=pltpu.CompilerParams(vmem_limit_bytes=VMEM),
        cost_estimate=pl.CostEstimate(flops=n << 20, bytes_accessed=n * (2 << 20), transcendentals=0),
        name="combine",
    )(*own, halo, *after)


def take(parts, after=()):
    def kernel(*refs):
        for k in range(len(parts)):
            refs[len(refs) - len(parts) + k][...] = refs[k][...]

    in_specs = [pl.BlockSpec(shape, lambda g, at=at: at) for _, shape, at in parts]
    out_specs = [pl.BlockSpec(shape, lambda g: (0, 0, 0)) for _, shape, _ in parts]
    return pl.pallas_call(
        kernel,
        out_shape=[jax.ShapeDtypeStruct(shape, BF16) for _, shape, _ in parts],
        grid=(1,),
        in_specs=in_specs + [pl.BlockSpec(memory_space=pltpu.HBM)] * len(after),
        out_specs=out_specs,
        compiler_params=pltpu.CompilerParams(vmem_limit_bytes=VMEM),
        cost_estimate=pl.CostEstimate(flops=0, bytes_accessed=2 << 20, transcendentals=0),
        name="take",
    )(*[array for array, _, _ in parts], *after)


def pack_kernel(own, right, far_a, far_b, left, *refs):
    out = refs[-1]
    out[:, 0:32] = own[...]
    out[:, 32:64] = right[...]
    out[:, 96:128] = left[...]

    @pl.when(pl.program_id(0) < 2)
    def _():
        out[:, 64:96] = far_a[...]

    @pl.when(pl.program_id(0) >= 2)
    def _():
        out[:, 64:96] = far_b[...]


def pack(own, planes, after=()):
    part = (8, 32, LANES)
    whole = pl.BlockSpec(part, lambda g: (g, 0, 0))
    return pl.pallas_call(
        pack_kernel,
        out_shape=jax.ShapeDtypeStruct((32, 128, LANES), BF16),
        grid=(4,),
        in_specs=[
            whole,
            whole,
            pl.BlockSpec(part, lambda g: (jnp.minimum(g, 1), 0, 0)),
            pl.BlockSpec(part, lambda g: (jnp.maximum(g - 2, 0), 0, 0)),
            whole,
        ]
        + [pl.BlockSpec(memory_space=pltpu.HBM)] * len(after),
        out_specs=pl.BlockSpec((8, 128, LANES), lambda g: (g, 0, 0)),
        compiler_params=pltpu.CompilerParams(vmem_limit_bytes=VMEM),
        cost_estimate=pl.CostEstimate(flops=0, bytes_accessed=4 << 20, transcendentals=0),
        name="pack",
    )(own, *planes[1], *planes[2], *planes[3], *after)


def correlate_kernel(steps, n_own, whole, place, *refs):
    out = refs[-1]
    y = place[0]
    scale = 1.0 / 128
    ids = lax.broadcasted_iota(jnp.int32, (8, 1), 0)
    sign = jnp.where(ids < 4, 1.0, -1.0)
    row = lax.broadcasted_iota(jnp.int32, (ROWS, ROWS), 0)
    col = lax.broadcasted_iota(jnp.int32, (ROWS, ROWS), 1)

    def pair(ref):
        return ref[...].astype(F32).reshape(ref.shape[0], 2, 8, LANES)

    def flat(x):
        return x.reshape(x.shape[0] * 8, LANES)

    def times_of(plane, other):
        return jnp.dot(plane, other, preferred_element_type=F32) * scale

    mine = [pair(ref) for ref in refs[:n_own]]
    planes = []
    for i in range(2):
        p = jnp.concatenate([x[:, i] for x in mine], axis=0)
        flipped = pltpu.roll(p, 4, 1) * sign
        if whole:
            planes.append((flat(p).astype(BF16).T, flat(flipped).astype(BF16).T))
        else:
            planes.append((p, flipped))

    def products(step, pieces):
        pieces = [pair(refs[k]) for k in pieces]
        q = lax.rem(y + step, 4)
        for i in range(2):
            real, imag = planes[i]
            if step == 0:
                same = jnp.concatenate([flat(x[:, i]) for x in mine], axis=0).astype(BF16)
                yield i, y, jnp.where(row <= col, times_of(real, same), times_of(imag, same))
            else:
                plane = jnp.where(q < y, imag, real)
                if not whole:
                    plane = flat(plane).astype(BF16).T
                other = jnp.concatenate([flat(x[:, i]) for x in pieces], axis=0).astype(BF16)
                yield i, q, times_of(plane, other)

    if whole:
        for step, pieces in steps:
            for i, q, value in products(step, pieces):
                out[i, 0, :, pl.ds(pl.multiple_of(q * 256, 256), 256)] = value
    else:
        for e, (step, pieces) in enumerate(steps):

            @pl.when(pl.program_id(1) == e)
            def _():
                for i, _, value in products(step, pieces):
                    out[i, 0] = value


def correlate(place, b, own, others, before, whole, base=0, after=()):
    def spec(array, step):
        row = {32: 0, 64: base, 128: step}[array.shape[1]]
        return pl.BlockSpec((array.shape[0], 16, LANES), lambda g, *rest: (0, 2 * row + g, 0))

    if not isinstance(own, (list, tuple)):
        own = [own]
    in_specs = [spec(array, 0) for array in own]
    args = [place, *own]
    steps = []
    for step, arrays in others.items():
        steps.append((step, tuple(range(len(args) - 1, len(args) - 1 + len(arrays)))))
        for array in arrays:
            in_specs.append(spec(array, step))
            args.append(array)
    aliases = {}
    if before is not None:
        in_specs.append(pl.BlockSpec(memory_space=pltpu.HBM))
        aliases = {len(args): 0}
        args.append(before)

    in_specs += [pl.BlockSpec(memory_space=pltpu.HBM)] * len(after)
    args += after

    def kernel(*refs):
        correlate_kernel(steps, len(own), whole, *refs)

    first = steps[0][0]
    if whole:
        grid = (2,)
        out_spec = pl.BlockSpec((2, 1, ROWS, 1024), lambda g, y: (g, b, 0, 0))
    else:
        grid = (2, len(steps))
        out_spec = pl.BlockSpec((2, 1, ROWS, 256), lambda g, e, y: (g, b, 0, lax.rem(y[0] + first + e, 4)))
    return pl.pallas_call(
        kernel,
        out_shape=jax.ShapeDtypeStruct((4, 4, ROWS, 1024), F32),
        grid_spec=pltpu.PrefetchScalarGridSpec(
            num_scalar_prefetch=1, grid=grid, in_specs=in_specs, out_specs=out_spec
        ),
        input_output_aliases=aliases,
        compiler_params=pltpu.CompilerParams(vmem_limit_bytes=60 * 1024 * 1024),
        cost_estimate=pl.CostEstimate(flops=len(steps) * 160000000, bytes_accessed=6 << 20, transcendentals=0),
        name="correlate",
    )(*args)


def body(v, window):
    groups = lax.axis_size("tm")
    ring = lax.axis_size("inp")
    tables = [jnp.asarray(t) for t in dft_tables()]
    place = lax.axis_index("inp").astype(jnp.int32).reshape(1)
    later = [(i, i + 1) for i in range(groups - 1)]

    def up(x):
        return lax.ppermute(x, "inp", [(i, (i + 1) % ring) for i in range(ring)])

    def down(x):
        return lax.ppermute(x, "inp", [(i, (i - 1) % ring) for i in range(ring)])

    def swap(x):
        return lax.all_to_all(x, "tm", split_axis=0, concat_axis=0, tiled=True)

    (passed,) = spectra(v, window, tables, (4, 5, 6), ((1, 3, 2, 0),), False)
    halo = lax.ppermute(passed, "tm", later)
    own = spectra(v, window, tables, (0, 1, 2, 3), ((1,), (3,), (2,), (0,)), True)
    lower, upper, half = (0, 0, 0), (1, 0, 0), (16, 32, LANES)

    (early,) = combine(own[3:], halo, (3,), 1)
    (rows,) = combine(own[:3], halo, (0, 1, 2), 1, (early,))
    late = swap(rows)
    left, right = up(early), down(early)
    first, second = take([(left, half, lower), (right, half, upper)])
    early = pack(early, {1: [right], 2: [up(first), down(second)], 3: [left]})
    odd, even = take([(late, (32, 64, LANES), (0, 0, 0)), (late, (32, 32, LANES), (0, 2, 0))])
    odd_left, odd_right = up(odd), down(odd)
    even_left, even_right = up(even), down(even)
    early = swap(early)

    whole = (32, 32, LANES)
    near = {0: [], 1: [odd_right], 3: [odd_left]}
    out = correlate(place, 0, early, {0: [], 1: [early], 2: [early], 3: [early]}, None, True, 0, [odd_left, odd_right])
    first, second = take([(odd_left, whole, (0, 0, 0)), (odd_right, whole, (0, 1, 0))], (out,))
    odd_far = up(first), down(second)
    out = correlate(place, 1, odd, near, out, True, 0)
    out = correlate(place, 3, odd, near, out, True, 1)
    first, second = take([(even_left, half, lower), (even_right, half, upper)], (out,))
    even_far = [up(first), down(second)]
    out = correlate(place, 2, even, {0: [], 1: [even_right], 3: [even_left]}, out, True, 0, list(odd_far))
    out = correlate(place, 1, odd, {2: [odd_far[0]]}, out, False, 0)
    out = correlate(place, 3, odd, {2: [odd_far[1]]}, out, False, 1)
    out = correlate(place, 2, even, {2: even_far}, out, False, 0)
    return out.reshape(16, ROWS, 1024)


def solution(mesh):
    in_specs = (P("inp", "tm", None), P())
    out_specs = P("tm", "inp", None)
    return jax.shard_map(body, mesh=mesh, in_specs=in_specs, out_specs=out_specs, check_vma=False)
```

time: 328 us -> 145 us (0.44); the launches traced: 322 us -> 144 us
  matrix products: 69.5 us -> 0 us
  local copies, waits for them, and re-layouts: 75 us -> 11.2 us
  Pallas kernels: 0 us -> 44.5 us
  other arithmetic: 43.6 us -> 0 us
  blocking collectives: 35.3 us -> 0 us
  starting transfers between devices: 2.14 us -> 32.7 us
  waiting for transfers between devices: 82.9 us -> 55.9 us
  between operations: 13.8 us -> 0.14 us
    all_gather x1 -> x0, waiting for transfers between devices: 82.9 us -> none  [body(): lax.all_gather(local, 'inp', axis=1, tiled=True)]
    dot_general x6 -> x0, matrix products: 69.5 us -> none  [the longest x4 39.7 us: body(): jnp.dot(frames, filt[tap], preferred_element_type=jnp.float32)]
    ppermute x1 -> x13, waiting for transfers between devices: 0.01 us -> 55.9 us  [the longest x6 32.4 us: down(): return lax.ppermute(x, 'inp', [(i, (i - 1) % ring) for i in range(ring)])]
    pallas_call x0 -> x16, Pallas kernels: none -> 44.5 us  [the longest x7 22 us: correlate(): pl.pallas_call(kernel, out_shape=jax.ShapeDtypeStruct((4, 4, ROWS, 1024),...]
    reshape x5 -> x0, local copies, waits for them, and re-layouts: 40.3 us -> none  [the longest x4 27.7 us: body(): frames = joined[:, hold - tap:hold - tap + frames_dev, :].reshape(-1, frame)]
    all_to_all x1 -> x0, blocking collectives: 35.3 us -> none  [body(): lax.all_to_all(turned, 'tm', split_axis=0, concat_axis=3, tiled=True)]
    concatenate x2 -> x0, other arithmetic: 18.8 us -> none  [the longest x1 14.1 us: body(): joined = jnp.concatenate([earlier, voltages], axis=1)]
    ppermute x1 -> x13, starting transfers between devices: 2.13 us -> 18.9 us  [the longest x6 14.6 us: down(): return lax.ppermute(x, 'inp', [(i, (i - 1) % ring) for i in range(ring)])]
  transfers between devices with their start and end apart: 2 -> 15, of which waited for: 1 -> 8; matrix products, arithmetic and copies ran while one was open for 14% -> 0% of each run, Pallas kernels for 0% -> 23%
where the time goes in v1:
time: 145 us; the launch traced here: 144 us
  waiting for transfers between devices  55.9 us (39%)
  Pallas kernels  44.5 us (31%)
  starting transfers between devices  32.7 us (23%)
  local copies, waits for them, and re-layouts  11.2 us (8%)
    ppermute x6, waiting for transfers between devices, down(): return lax.ppermute(x, 'inp', [(i, (i - 1) % ring) for i in range(ring)])  32.4 us
    pallas_call x7, Pallas kernels, correlate(): pl.pallas_call(kernel, out_shape=jax.ShapeDtypeStruct((4, 4, ROWS, 1024),...  22 us
    pallas_call x2, Pallas kernels, spectra(): pl.pallas_call(kernel, out_shape=[jax.ShapeDtypeStruct((n * len(g), 256,...  18 us
    ppermute x6, starting transfers between devices, down(): return lax.ppermute(x, 'inp', [(i, (i - 1) % ring) for i in range(ring)])  14.6 us
    all_to_all x2, starting transfers between devices, swap(): return lax.all_to_all(x, 'tm', split_axis=0, concat_axis=0, tiled=True)  13.8 us
    ppermute x6, waiting for transfers between devices, up(): return lax.ppermute(x, 'inp', [(i, (i + 1) % ring) for i in range(ring)])  13.4 us
    unnamed x28, local copies, waits for them, and re-layouts  11.2 us
    ppermute x1, waiting for transfers between devices, body(): halo = lax.ppermute(passed, 'tm', later)  10.2 us
  transfers between devices with their start and end apart: 15, of which 8 were waited for; matrix products, arithmetic and copies ran while one was open for 0% of the time, Pallas kernels for 23%

profile of v1, /device:TPU:2, one launch (start us, length us, event | category | flops | bytes accessed | tf_op | source)
XLA Modules:
  0.0 144.5 jit_solution(3210414408890968844)
XLA Ops:
  0.0 0.8 copy-done.8
  0.8 0.0 copy-start.9
  0.8 1.4 copy-done.9
  2.2 6.3 %spectra.3 = bf16[12,256,256]{2,1,0:T(8,128)(2,1)S(1)} custom-call(bf16[256,4,2048]{2,1,0:T(4,128)(2,1)} %refs_0_.3, f32[4,2048]{1,0:T(4,128)S(1)} %copy-done.8, bf16[256,3072]{1,0:T(8,128)(2,1)S(1)} %copy-done.9), custom_call_target="tpu_custom_call" | custom-call | flops 3600000000 | bytes 12582912 | tf_op jit(solution)/shard_map/spectra/pallas_call | solution.py:136
  8.4 1.9 %collective-permute-start = (bf16[12,256,256]{2,1,0:T(8,128)(2,1)S(1)}, bf16[12,256,256]{2,1,0:T(8,128)(2,1)S(1)}, u32[]{:S(2)}, u32[]{:S(2)}) collective-permute-start(bf16[12,256,256]{2,1,0:T(8,128)(2,1)S(1)} %spectra.3), channel_id=1, source_target_pairs={{0,1},{1,2},{2,3},{3,4},{4,5},{5,6},{6,7},{7,8},{8,9},{9,10},{10,1... | collective-permute-start | bytes 4718600 | tf_op jit(solution)/shard_map/ppermute | solution.py:366
  10.4 11.7 %spectra.2 = (f32[4,256,256]{2,1,0:T(8,128)S(1)}, f32[4,256,256]{2,1,0:T(8,128)S(1)}, f32[4,256,256]{2,1,0:T(8,128)S(1)}, f32[4,256,256]{2,1,0:T(8,128)S(1)}) custom-call(bf16[256,4,2048]{2,1,0:T(4,128)(2,1)} %refs_0_.3, f32[4,2048]{1,0:T(4,128)S(1)} %copy-done.8, bf16[256,3072]{1,0:T(8,128)(2,1)S(1)} %copy-done.9, bf16[256,3072]{1,0:T(8,128)(2,1)} %constant.11.clone.refs_3_), custom_call_target="tpu_custom_call" | custom-call | flops 4800000000 | bytes 12582912 | tf_op jit(solution)/shard_map/spectra/pallas_call | solution.py:136
  22.1 10.2 %collective-permute-done.refs_1_.refs_3_ = bf16[12,256,256]{2,1,0:T(8,128)(2,1)S(1)} collective-permute-done((bf16[12,256,256]{2,1,0:T(8,128)(2,1)S(1)}, bf16[12,256,256]{2,1,0:T(8,128)(2,1)S(1)}, u32[]{:S(2)}, u32[]{:S(2)}) %collective-permute-start) | collective-permute-done | bytes 1572896 | tf_op jit(solution)/shard_map/ppermute | solution.py:366
  32.3 0.0 copy-start.7
  32.3 0.2 combine.2.refs_4_.own
  32.5 0.9 copy-done.7
  33.4 2.0 %combine.3 = bf16[32,96,256]{2,1,0:T(8,128)(2,1)S(1)} custom-call(f32[4,256,256]{2,1,0:T(8,128)S(1)} %get-tuple-element.17.refs_0_, f32[4,256,256]{2,1,0:T(8,128)S(1)} %get-tuple-element.18.refs_1_, f32[4,256,256]{2,1,0:T(8,128)S(1)} %get-tuple-element.19.refs_2_, bf16[12,256,256]{2,1,0:T(8,128)(2,1)} %copy-done.7, bf16[32,32,256]{2,1,0:T(8,128)(2,1)S(1)} %combine.2.refs_4_.own), custom_call_target="tpu_custom_call" | custom-call | flops 3145728 | bytes 6291456 | tf_op jit(solution)/shard_map/combine/pallas_call | solution.py:179
  35.5 0.0 copy-start.6
  35.5 1.2 copy-done.6
  36.7 6.4 %all-to-all-start = ((bf16[32,96,256]{2,1,0:T(8,128)(2,1)}), bf16[32,96,256]{2,1,0:T(8,128)(2,1)S(1)}, u32[]{:S(2)}, u32[]{:S(2)}) async-start(bf16[32,96,256]{2,1,0:T(8,128)(2,1)} %copy-done.6), calls=%async_computation | async-start | bytes 3145728 | tf_op jit(solution)/shard_map/all_to_all | solution.py:363
  43.0 3.1 %collective-permute-start.5 = (bf16[32,32,256]{2,1,0:T(8,128)(2,1)S(1)}, bf16[32,32,256]{2,1,0:T(8,128)(2,1)S(1)}, u32[]{:S(2)}, u32[]{:S(2)}) collective-permute-start(bf16[32,32,256]{2,1,0:T(8,128)(2,1)S(1)} %combine.2.refs_4_.own), channel_id=1, source_target_pairs={{0,96},{32,0},{64,32},{96,64},{1,97},{33,1},{65,33},{97,65},{2,98}... | collective-permute-start | bytes 1572872 | tf_op jit(solution)/shard_map/ppermute | solution.py:360
  46.1 0.0 collective-permute-start.6
  46.1 11.5 %collective-permute-done.5.refs_1_.right = bf16[32,32,256]{2,1,0:T(8,128)(2,1)S(1)} collective-permute-done((bf16[32,32,256]{2,1,0:T(8,128)(2,1)S(1)}, bf16[32,32,256]{2,1,0:T(8,128)(2,1)S(1)}, u32[]{:S(2)}, u32[]{:S(2)}) %collective-permute-start.5) | collective-permute-done | bytes 524320 | tf_op jit(solution)/shard_map/ppermute | solution.py:360
  57.6 3.4 %collective-permute-done.6.refs_0_.left = bf16[32,32,256]{2,1,0:T(8,128)(2,1)S(1)} collective-permute-done((bf16[32,32,256]{2,1,0:T(8,128)(2,1)S(1)}, bf16[32,32,256]{2,1,0:T(8,128)(2,1)S(1)}, u32[]{:S(2)}, u32[]{:S(2)}) %collective-permute-start.6) | collective-permute-done | bytes 524320 | tf_op jit(solution)/shard_map/ppermute | solution.py:357
  61.1 0.1 collective-permute-start.7
  61.1 3.2 %collective-permute-start.8 = (bf16[16,32,256]{2,1,0:T(8,128)(2,1)S(1)}, bf16[16,32,256]{2,1,0:T(8,128)(2,1)S(1)}, u32[]{:S(2)}, u32[]{:S(2)}) collective-permute-start(bf16[16,32,256]{2,1,0:T(8,128)(2,1)S(1)} %get-tuple-element.24), channel_id=1, source_target_pairs={{0,96},{32,0},{64,32},{96,64},{1,97},{33,1},{65,33},{97,65},{2,98}... | collective-permute-start | bytes 786440 | tf_op jit(solution)/shard_map/ppermute | solution.py:360
  64.4 5.2 %collective-permute-done.7.far_a = bf16[16,32,256]{2,1,0:T(8,128)(2,1)S(1)} collective-permute-done((bf16[16,32,256]{2,1,0:T(8,128)(2,1)S(1)}, bf16[16,32,256]{2,1,0:T(8,128)(2,1)S(1)}, u32[]{:S(2)}, u32[]{:S(2)}) %collective-permute-start.7) | collective-permute-done | bytes 262176 | tf_op jit(solution)/shard_map/ppermute | solution.py:357
  69.5 0.0 collective-permute-done.8.far_b
  69.5 0.2 pack.1
  69.8 0.0 copy-start.5
  69.8 1.3 copy-done.5
  71.1 0.0 all-to-all-done.refs_0_.refs_1_
  71.1 7.4 %all-to-all-start.1 = ((bf16[32,128,256]{2,1,0:T(8,128)(2,1)}), bf16[32,128,256]{2,1,0:T(8,128)(2,1)}, u32[]{:S(2)}, u32[]{:S(2)}) async-start(bf16[32,128,256]{2,1,0:T(8,128)(2,1)} %copy-done.5), calls=%async_computation.1 | async-start | bytes 4194304 | tf_op jit(solution)/shard_map/all_to_all | solution.py:363
  78.5 0.9 take.4
  79.4 0.0 copy-start
  79.4 3.0 %collective-permute-start.3 = (bf16[32,64,256]{2,1,0:T(8,128)(2,1)S(1)}, bf16[32,64,256]{2,1,0:T(8,128)(2,1)S(1)}, u32[]{:S(2)}, u32[]{:S(2)}) collective-permute-start(bf16[32,64,256]{2,1,0:T(8,128)(2,1)S(1)} %get-tuple-element.22.refs_1_), channel_id=1, source_target_pairs={{0,96},{32,0},{64,32},{96,64},{1,97},{33,1},{65,33},{97,65},{2,98}... | collective-permute-start | bytes 3145736 | tf_op jit(solution)/shard_map/ppermute | solution.py:360
  82.4 0.0 collective-permute-start.4
  82.4 0.0 collective-permute-start.1
  82.4 3.3 %collective-permute-start.2 = (bf16[32,32,256]{2,1,0:T(8,128)(2,1)}, bf16[32,32,256]{2,1,0:T(8,128)(2,1)}, u32[]{:S(2)}, u32[]{:S(2)}) collective-permute-start(bf16[32,32,256]{2,1,0:T(8,128)(2,1)} %get-tuple-element.21.refs_1_), channel_id=1, source_target_pairs={{0,96},{32,0},{64,32},{96,64},{1,97},{33,1},{65,33},{97,65},{2,98}... | collective-permute-start | bytes 1572872 | tf_op jit(solution)/shard_map/ppermute | solution.py:360
  85.6 20.3 %collective-permute-done.3.refs_6_.refs_2_.refs_1_ = bf16[32,64,256]{2,1,0:T(8,128)(2,1)S(1)} collective-permute-done((bf16[32,64,256]{2,1,0:T(8,128)(2,1)S(1)}, bf16[32,64,256]{2,1,0:T(8,128)(2,1)S(1)}, u32[]{:S(2)}, u32[]{:S(2)}) %collective-permute-start.3) | collective-permute-done | bytes 1048608 | tf_op jit(solution)/shard_map/ppermute | solution.py:360
  105.9 3.7 %collective-permute-done.4.refs_5_.refs_3_.refs_0_ = bf16[32,64,256]{2,1,0:T(8,128)(2,1)S(1)} collective-permute-done((bf16[32,64,256]{2,1,0:T(8,128)(2,1)S(1)}, bf16[32,64,256]{2,1,0:T(8,128)(2,1)S(1)}, u32[]{:S(2)}, u32[]{:S(2)}) %collective-permute-start.4) | collective-permute-done | bytes 1048608 | tf_op jit(solution)/shard_map/ppermute | solution.py:357
  109.6 0.0 all-to-all-done.1.refs_1_.refs_2_.refs_3_.refs_4_
  109.6 0.0 copy-done.1
  109.6 1.0 copy-done.3
  110.7 3.8 %correlate.7.refs_4_.refs_2_ = f32[4,4,256,1024]{3,2,1,0:T(8,128)} custom-call(s32[1]{0:T(128)} %bitcast.refs_0_, bf16[32,128,256]{2,1,0:T(8,128)(2,1)} %all-to-all-done.1.refs_1_.refs_2_.refs_3_.refs_4_, bf16[32,128,256]{2,1,0:T(8,128)(2,1)} %all-to-all-done.1.refs_1_.refs_2_.refs_3_.refs_4_, ...), custom_call_target="tpu_custom_call" | custom-call | flops 640000000 | bytes 6291456 | tf_op jit(solution)/shard_map/correlate/pallas_call | solution.py:336
  114.4 0.0 copy-done
  114.4 1.2 copy-done.2
  115.7 1.2 copy-done.4
  116.9 0.1 take.7
  117.0 0.5 collective-permute-start.11
  117.5 1.7 %collective-permute-start.12 = (bf16[32,32,256]{2,1,0:T(8,128)(2,1)S(1)}, bf16[32,32,256]{2,1,0:T(8,128)(2,1)S(1)}, u32[]{:S(2)}, u32[]{:S(2)}) collective-permute-start(bf16[32,32,256]{2,1,0:T(8,128)(2,1)S(1)} %get-tuple-element.28), channel_id=1, source_target_pairs={{0,32},{32,64},{64,96},{96,0},{1,33},{33,65},{65,97},{97,1},{2,34}... | collective-permute-start | bytes 1572872 | tf_op jit(solution)/shard_map/ppermute | solution.py:357
  119.2 3.6 %correlate.8.refs_4_ = f32[4,4,256,1024]{3,2,1,0:T(8,128)} custom-call(s32[1]{0:T(128)} %bitcast.refs_0_, bf16[32,64,256]{2,1,0:T(8,128)(2,1)} %copy-done, bf16[32,64,256]{2,1,0:T(8,128)(2,1)} %copy-done.1, bf16[32,64,256]{2,1,0:T(8,128)(2,1)} %copy-done.3, f32[4,4,256,1024]{3,2,1,0:T(8,128)} %correlate.7.refs_4_.refs_2_), custom_call_target="tpu_custom_call", output_to_operand_aliasing={{}: (4, {})} | custom-call | flops 480000000 | bytes 6291456 | tf_op jit(solution)/shard_map/correlate/pallas_call | solution.py:336
  122.9 3.6 %correlate.9.refs_2_.refs_4_ = f32[4,4,256,1024]{3,2,1,0:T(8,128)} custom-call(s32[1]{0:T(128)} %bitcast.refs_0_, bf16[32,64,256]{2,1,0:T(8,128)(2,1)} %copy-done, bf16[32,64,256]{2,1,0:T(8,128)(2,1)} %copy-done.1, bf16[32,64,256]{2,1,0:T(8,128)(2,1)} %copy-done.3, f32[4,4,256,1024]{3,2,1,0:T(8,128)} %correlate.8.refs_4_), custom_call_target="tpu_custom_call", output_to_operand_aliasing={{}: (4, {})} | custom-call | flops 480000000 | bytes 6291456 | tf_op jit(solution)/shard_map/correlate/pallas_call | solution.py:336
  126.5 0.0 collective-permute-done.1.refs_0_.refs_3_
  126.5 0.0 collective-permute-done.2.refs_1_.refs_2_
  126.5 1.1 take.6
  127.6 1.5 %collective-permute-start.10 = (bf16[16,32,256]{2,1,0:T(8,128)(2,1)S(1)}, bf16[16,32,256]{2,1,0:T(8,128)(2,1)S(1)}, u32[]{:S(2)}, u32[]{:S(2)}) collective-permute-start(bf16[16,32,256]{2,1,0:T(8,128)(2,1)S(1)} %get-tuple-element.26), channel_id=1, source_target_pairs={{0,96},{32,0},{64,32},{96,64},{1,97},{33,1},{65,33},{97,65},{2,98}... | collective-permute-start | bytes 786440 | tf_op jit(solution)/shard_map/ppermute | solution.py:360
  129.1 0.6 collective-permute-start.9
  129.6 0.6 collective-permute-done.11.refs_6_.refs_2_
  130.3 1.0 collective-permute-done.12.refs_5_.refs_2_
  131.3 0.0 copy-done.10
  131.3 0.8 copy-done.11
  132.1 3.6 %correlate.10.refs_3_ = f32[4,4,256,1024]{3,2,1,0:T(8,128)} custom-call(s32[1]{0:T(128)} %bitcast.refs_0_, bf16[32,32,256]{2,1,0:T(8,128)(2,1)} %get-tuple-element.21.refs_1_, bf16[32,32,256]{2,1,0:T(8,128)(2,1)} %collective-permute-done.2.refs_1_.refs_2_, ...), custom_call_target="tpu_custom_call", output_to_operand_aliasing={{}: (4, {})} | custom-call | flops 480000000 | bytes 6291456 | tf_op jit(solution)/shard_map/correlate/pallas_call | solution.py:336
  135.7 2.4 %correlate.11.refs_3_ = f32[4,4,256,1024]{3,2,1,0:T(8,128)} custom-call(s32[1]{0:T(128)} %bitcast.refs_0_, bf16[32,64,256]{2,1,0:T(8,128)(2,1)} %copy-done, bf16[32,32,256]{2,1,0:T(8,128)(2,1)} %copy-done.11, f32[4,4,256,1024]{3,2,1,0:T(8,128)} %correlate.10.refs_3_), custom_call_target="tpu_custom_call", output_to_operand_aliasing={{}: (3, {})} | custom-call | flops 160000000 | bytes 6291456 | tf_op jit(solution)/shard_map/correlate/pallas_call | solution.py:336
  138.2 2.5 %correlate.12.refs_4_ = f32[4,4,256,1024]{3,2,1,0:T(8,128)} custom-call(s32[1]{0:T(128)} %bitcast.refs_0_, bf16[32,64,256]{2,1,0:T(8,128)(2,1)} %copy-done, bf16[32,32,256]{2,1,0:T(8,128)(2,1)} %copy-done.10, f32[4,4,256,1024]{3,2,1,0:T(8,128)} %correlate.11.refs_3_), custom_call_target="tpu_custom_call", output_to_operand_aliasing={{}: (3, {})} | custom-call | flops 160000000 | bytes 6291456 | tf_op jit(solution)/shard_map/correlate/pallas_call | solution.py:336
  140.6 0.0 collective-permute-done.10.refs_3_
  140.6 0.0 collective-permute-done.9.refs_2_
  140.6 0.7 copy-done.12
  141.3 0.7 copy-done.13
  142.0 2.5 %correlate.13 = f32[4,4,256,1024]{3,2,1,0:T(8,128)} custom-call(s32[1]{0:T(128)} %bitcast.refs_0_, bf16[32,32,256]{2,1,0:T(8,128)(2,1)} %get-tuple-element.21.refs_1_, bf16[16,32,256]{2,1,0:T(8,128)(2,1)} %copy-done.13, bf16[16,32,256]{2,1,0:T(8,128)(2,1)} %copy-done.12, f32[4,4,256,1024]{3,2,1,0:T(8,128)} %correlate.12.refs_4_), custom_call_target="tpu_custom_call", output_to_operand_aliasing={{}: (4, {})} | custom-call | flops 160000000 | bytes 6291456 | tf_op jit(solution)/shard_map/correlate/pallas_call | solution.py:336
  (10 shorter events, 0.0 us)
Async XLA Ops:
  0.0 0.8 copy-start.8
  0.8 1.4 copy-start.9
  8.4 23.8 %collective-permute-start = (bf16[12,256,256]{2,1,0:T(8,128)(2,1)S(1)}, bf16[12,256,256]{2,1,0:T(8,128)(2,1)S(1)}, u32[]{:S(2)}, u32[]{:S(2)}) collective-permute-start(bf16[12,256,256]{2,1,0:T(8,128)(2,1)S(1)} %spectra.3), channel_id=1, source_target_pairs={{0,1},{1,2},{2,3},{3,4},{4,5},{5,6},{6,7},{7,8},{8,9},{9,10},{10,1... | collective-permute-start | bytes 4718600 | tf_op jit(solution)/shard_map/ppermute | solution.py:366
  32.3 1.1 copy-start.7
  35.5 1.2 copy-start.6
  36.7 34.4 %all-to-all-start = ((bf16[32,96,256]{2,1,0:T(8,128)(2,1)}), bf16[32,96,256]{2,1,0:T(8,128)(2,1)S(1)}, u32[]{:S(2)}, u32[]{:S(2)}) async-start(bf16[32,96,256]{2,1,0:T(8,128)(2,1)} %copy-done.6), calls=%async_computation | async-start | bytes 3145728 | tf_op jit(solution)/shard_map/all_to_all | solution.py:363
  43.0 14.6 %collective-permute-start.5 = (bf16[32,32,256]{2,1,0:T(8,128)(2,1)S(1)}, bf16[32,32,256]{2,1,0:T(8,128)(2,1)S(1)}, u32[]{:S(2)}, u32[]{:S(2)}) collective-permute-start(bf16[32,32,256]{2,1,0:T(8,128)(2,1)S(1)} %combine.2.refs_4_.own), channel_id=1, source_target_pairs={{0,96},{32,0},{64,32},{96,64},{1,97},{33,1},{65,33},{97,65},{2,98}... | collective-permute-start | bytes 1572872 | tf_op jit(solution)/shard_map/ppermute | solution.py:360
  46.1 14.9 %collective-permute-start.6 = (bf16[32,32,256]{2,1,0:T(8,128)(2,1)S(1)}, bf16[32,32,256]{2,1,0:T(8,128)(2,1)S(1)}, u32[]{:S(2)}, u32[]{:S(2)}) collective-permute-start(bf16[32,32,256]{2,1,0:T(8,128)(2,1)S(1)} %combine.2.refs_4_.own), channel_id=1, source_target_pairs={{0,32},{32,64},{64,96},{96,0},{1,33},{33,65},{65,97},{97,1},{2,34}... | collective-permute-start | bytes 1572872 | tf_op jit(solution)/shard_map/ppermute | solution.py:357
  61.1 8.5 %collective-permute-start.7 = (bf16[16,32,256]{2,1,0:T(8,128)(2,1)S(1)}, bf16[16,32,256]{2,1,0:T(8,128)(2,1)S(1)}, u32[]{:S(2)}, u32[]{:S(2)}) collective-permute-start(bf16[16,32,256]{2,1,0:T(8,128)(2,1)S(1)} %get-tuple-element.23), channel_id=1, source_target_pairs={{0,32},{32,64},{64,96},{96,0},{1,33},{33,65},{65,97},{97,1},{2,34}... | collective-permute-start | bytes 786440 | tf_op jit(solution)/shard_map/ppermute | solution.py:357
  61.1 8.4 %collective-permute-start.8 = (bf16[16,32,256]{2,1,0:T(8,128)(2,1)S(1)}, bf16[16,32,256]{2,1,0:T(8,128)(2,1)S(1)}, u32[]{:S(2)}, u32[]{:S(2)}) collective-permute-start(bf16[16,32,256]{2,1,0:T(8,128)(2,1)S(1)} %get-tuple-element.24), channel_id=1, source_target_pairs={{0,96},{32,0},{64,32},{96,64},{1,97},{33,1},{65,33},{97,65},{2,98}... | collective-permute-start | bytes 786440 | tf_op jit(solution)/shard_map/ppermute | solution.py:360
  69.8 1.3 copy-start.5
  71.1 38.5 %all-to-all-start.1 = ((bf16[32,128,256]{2,1,0:T(8,128)(2,1)}), bf16[32,128,256]{2,1,0:T(8,128)(2,1)}, u32[]{:S(2)}, u32[]{:S(2)}) async-start(bf16[32,128,256]{2,1,0:T(8,128)(2,1)} %copy-done.5), calls=%async_computation.1 | async-start | bytes 4194304 | tf_op jit(solution)/shard_map/all_to_all | solution.py:363
  79.4 35.0 %copy-start = (bf16[32,64,256]{2,1,0:T(8,128)(2,1)}, bf16[32,64,256]{2,1,0:T(8,128)(2,1)S(1)}, u32[]{:S(2)}) copy-start(bf16[32,64,256]{2,1,0:T(8,128)(2,1)S(1)} %get-tuple-element.22.refs_1_) | copy-start | bytes 3145732
  79.4 26.5 %collective-permute-start.3 = (bf16[32,64,256]{2,1,0:T(8,128)(2,1)S(1)}, bf16[32,64,256]{2,1,0:T(8,128)(2,1)S(1)}, u32[]{:S(2)}, u32[]{:S(2)}) collective-permute-start(bf16[32,64,256]{2,1,0:T(8,128)(2,1)S(1)} %get-tuple-element.22.refs_1_), channel_id=1, source_target_pairs={{0,96},{32,0},{64,32},{96,64},{1,97},{33,1},{65,33},{97,65},{2,98}... | collective-permute-start | bytes 3145736 | tf_op jit(solution)/shard_map/ppermute | solution.py:360
  82.4 27.3 %collective-permute-start.4 = (bf16[32,64,256]{2,1,0:T(8,128)(2,1)S(1)}, bf16[32,64,256]{2,1,0:T(8,128)(2,1)S(1)}, u32[]{:S(2)}, u32[]{:S(2)}) collective-permute-start(bf16[32,64,256]{2,1,0:T(8,128)(2,1)S(1)} %get-tuple-element.22.refs_1_), channel_id=1, source_target_pairs={{0,32},{32,64},{64,96},{96,0},{1,33},{33,65},{65,97},{97,1},{2,34}... | collective-permute-start | bytes 3145736 | tf_op jit(solution)/shard_map/ppermute | solution.py:357
  82.4 44.1 %collective-permute-start.1 = (bf16[32,32,256]{2,1,0:T(8,128)(2,1)}, bf16[32,32,256]{2,1,0:T(8,128)(2,1)}, u32[]{:S(2)}, u32[]{:S(2)}) collective-permute-start(bf16[32,32,256]{2,1,0:T(8,128)(2,1)} %get-tuple-element.21.refs_1_), channel_id=1, source_target_pairs={{0,32},{32,64},{64,96},{96,0},{1,33},{33,65},{65,97},{97,1},{2,34}... | collective-permute-start | bytes 1572872 | tf_op jit(solution)/shard_map/ppermute | solution.py:357
  82.4 44.1 %collective-permute-start.2 = (bf16[32,32,256]{2,1,0:T(8,128)(2,1)}, bf16[32,32,256]{2,1,0:T(8,128)(2,1)}, u32[]{:S(2)}, u32[]{:S(2)}) collective-permute-start(bf16[32,32,256]{2,1,0:T(8,128)(2,1)} %get-tuple-element.21.refs_1_), channel_id=1, source_target_pairs={{0,96},{32,0},{64,32},{96,64},{1,97},{33,1},{65,33},{97,65},{2,98}... | collective-permute-start | bytes 1572872 | tf_op jit(solution)/shard_map/ppermute | solution.py:360
  105.9 3.7 %copy-start.1 = (bf16[32,64,256]{2,1,0:T(8,128)(2,1)}, bf16[32,64,256]{2,1,0:T(8,128)(2,1)S(1)}, u32[]{:S(2)}) copy-start(bf16[32,64,256]{2,1,0:T(8,128)(2,1)S(1)} %collective-permute-done.3.refs_6_.refs_2_.refs_1_) | copy-start | bytes 3145732
  109.6 1.0 copy-start.3
  114.4 1.2 copy-start.2
  115.7 1.2 copy-start.4
  117.0 13.3 %collective-permute-start.11 = (bf16[32,32,256]{2,1,0:T(8,128)(2,1)S(1)}, bf16[32,32,256]{2,1,0:T(8,128)(2,1)S(1)}, u32[]{:S(2)}, u32[]{:S(2)}) collective-permute-start(bf16[32,32,256]{2,1,0:T(8,128)(2,1)S(1)} %get-tuple-element.27), channel_id=1, source_target_pairs={{0,96},{32,0},{64,32},{96,64},{1,97},{33,1},{65,33},{97,65},{2,98}... | collective-permute-start | bytes 1572872 | tf_op jit(solution)/shard_map/ppermute | solution.py:360
  117.5 13.8 %collective-permute-start.12 = (bf16[32,32,256]{2,1,0:T(8,128)(2,1)S(1)}, bf16[32,32,256]{2,1,0:T(8,128)(2,1)S(1)}, u32[]{:S(2)}, u32[]{:S(2)}) collective-permute-start(bf16[32,32,256]{2,1,0:T(8,128)(2,1)S(1)} %get-tuple-element.28), channel_id=1, source_target_pairs={{0,32},{32,64},{64,96},{96,0},{1,33},{33,65},{65,97},{97,1},{2,34}... | collective-permute-start | bytes 1572872 | tf_op jit(solution)/shard_map/ppermute | solution.py:357
  127.6 13.1 %collective-permute-start.10 = (bf16[16,32,256]{2,1,0:T(8,128)(2,1)S(1)}, bf16[16,32,256]{2,1,0:T(8,128)(2,1)S(1)}, u32[]{:S(2)}, u32[]{:S(2)}) collective-permute-start(bf16[16,32,256]{2,1,0:T(8,128)(2,1)S(1)} %get-tuple-element.26), channel_id=1, source_target_pairs={{0,96},{32,0},{64,32},{96,64},{1,97},{33,1},{65,33},{97,65},{2,98}... | collective-permute-start | bytes 786440 | tf_op jit(solution)/shard_map/ppermute | solution.py:360
  129.1 11.5 %collective-permute-start.9 = (bf16[16,32,256]{2,1,0:T(8,128)(2,1)S(1)}, bf16[16,32,256]{2,1,0:T(8,128)(2,1)S(1)}, u32[]{:S(2)}, u32[]{:S(2)}) collective-permute-start(bf16[16,32,256]{2,1,0:T(8,128)(2,1)S(1)} %get-tuple-element.25), channel_id=1, source_target_pairs={{0,32},{32,64},{64,96},{96,0},{1,33},{33,65},{65,97},{97,1},{2,34}... | collective-permute-start | bytes 786440 | tf_op jit(solution)/shard_map/ppermute | solution.py:357
  130.3 1.1 copy-start.10
  131.3 0.8 copy-start.11
  140.6 0.7 copy-start.12
  141.3 0.7 copy-start.13

commit v2 on v1

--- a/solution.py
+++ b/solution.py
@@ -39,7 +39,7 @@
     return high, (both - high.astype(np.float64)).astype(BF16)
 
 
-def spectra_kernel(times, groups, fine, v_hbm, w_ref, *refs):
+def spectra_kernel(times, groups, fine, inputs, v_hbm, w_ref, *refs):
     n = 2 if fine else 1
     tables_hbm, refs = refs[:n], refs[n:]
     outs, refs = refs[: len(groups)], refs[len(groups) :]
@@ -50,8 +50,10 @@
     block = ROWS // TAPS
     sub = 16
     v_copies = [
-        pltpu.make_async_copy(v_hbm.at[pl.ds(i * block, block)], v_ref.at[pl.ds(i * block, block)], v_sem.at[i])
-        for i in range(ROWS // block)
+        pltpu.make_async_copy(
+            v_hbm.at[pl.ds(inputs.start + i * block, block)], v_ref.at[pl.ds(i * block, block)], v_sem.at[i]
+        )
+        for i in range(len(inputs) // block)
     ]
     table_copies = [pltpu.make_async_copy(tables_hbm[k], tables[k], table_sem.at[k]) for k in range(n)]
     for copy in v_copies + table_copies:
@@ -101,7 +103,7 @@
 
         lax.fori_loop(0, block // sub, per_rows, 0)
 
-    for i in range(ROWS // block):
+    for i in range(len(inputs) // block):
         per_block(i)
     spans = [slice(0, 512), slice(1024, 2048), slice(512, 1024), slice(1024, 2048)]
     columns = [slice(0, 512), slice(512, 1536), slice(1536, 2048), slice(2048, 3072)]
@@ -126,24 +128,24 @@
     lax.fori_loop(0, len(times), per_time, 0)
 
 
-def spectra(v, window, tables, times, groups, fine):
+def spectra(v, window, tables, times, groups, fine, inputs=range(ROWS)):
     def kernel(*refs):
-        spectra_kernel(times, groups, fine, *refs)
-
-    n = len(times)
+        spectra_kernel(times, groups, fine, inputs, *refs)
+
+    n, size = len(times), len(inputs)
     tables = tables if fine else tables[:1]
     anywhere = pl.BlockSpec(memory_space=pltpu.HBM)
     return pl.pallas_call(
         kernel,
-        out_shape=[jax.ShapeDtypeStruct((n * len(g), 256, LANES), F32 if fine else BF16) for g in groups],
+        out_shape=[jax.ShapeDtypeStruct((n * len(g), 256, size), F32 if fine else BF16) for g in groups],
         in_specs=[anywhere, pl.BlockSpec()] + [anywhere] * len(tables),
         scratch_shapes=[
             pltpu.VMEM((ROWS, FRAME), F32),
-            pltpu.VMEM((n, ROWS, FRAME), BF16),
-            pltpu.VMEM((n if fine else 1, ROWS, FRAME), BF16),
-            pltpu.VMEM((ROWS, TAPS, FRAME), BF16),
+            pltpu.VMEM((n, size, FRAME), BF16),
+            pltpu.VMEM((n if fine else 1, size, FRAME), BF16),
+            pltpu.VMEM((size, TAPS, FRAME), BF16),
             *[pltpu.VMEM(t.shape, BF16) for t in tables],
-            pltpu.SemaphoreType.DMA((4,)),
+            pltpu.SemaphoreType.DMA((size // (ROWS // TAPS),)),
             pltpu.SemaphoreType.DMA((len(tables),)),
         ],
         compiler_params=pltpu.CompilerParams(vmem_limit_bytes=VMEM),
@@ -153,7 +155,7 @@
 
 
 def combine_kernel(order, parts, *refs):
-    own, halo = refs[: len(order)], refs[len(order)]
+    own, halo = refs[: len(order)], refs[len(order) : len(order) + 2]
     rows = refs[-1]
     outs = refs[len(refs) - 1 - parts : -1]
     size = 32 // parts
@@ -163,7 +165,7 @@
             for t in range(TAPS):
                 value = own[k][t, :, span]
                 if t < TAPS - 1:
-                    value = value + halo[halo_at * (TAPS - 1) + t, :, span].astype(F32)
+                    value = value + halo[half][halo_at * (TAPS - 1) + t].astype(F32)
                 rows[half, pl.ds(t, 256, stride=TAPS), :] = value
             for part in range(parts):
                 value = rows[half, pl.ds(part * size * 32, size * 32)].astype(BF16)
@@ -179,12 +181,12 @@
     return pl.pallas_call(
         kernel,
         out_shape=[jax.ShapeDtypeStruct((32 // parts, 32 * n, LANES), BF16)] * parts,
-        in_specs=[pl.BlockSpec()] * (n + 1) + [pl.BlockSpec(memory_space=pltpu.HBM)] * len(after),
+        in_specs=[pl.BlockSpec()] * (n + 2) + [pl.BlockSpec(memory_space=pltpu.HBM)] * len(after),
         scratch_shapes=[pltpu.VMEM((LANES // 128, 1024, 128), F32)],
         compiler_params=pltpu.CompilerParams(vmem_limit_bytes=VMEM),
         cost_estimate=pl.CostEstimate(flops=n << 20, bytes_accessed=n * (2 << 20), transcendentals=0),
         name="combine",
-    )(*own, halo, *after)
+    )(*own, *halo, *after)
 
 
 def take(parts, after=()):
@@ -362,8 +364,10 @@
     def swap(x):
         return lax.all_to_all(x, "tm", split_axis=0, concat_axis=0, tiled=True)
 
-    (passed,) = spectra(v, window, tables, (4, 5, 6), ((1, 3, 2, 0),), False)
-    halo = lax.ppermute(passed, "tm", later)
+    halo = []
+    for inputs in (range(0, 128), range(128, 256)):
+        (passed,) = spectra(v, window, tables, (4, 5, 6), ((1, 3, 2, 0),), False, inputs)
+        halo.append(lax.ppermute(passed, "tm", later))
     own = spectra(v, window, tables, (0, 1, 2, 3), ((1,), (3,), (2,), (0,)), True)
     lower, upper, half = (0, 0, 0), (1, 0, 0), (16, 32, LANES)
 
@@ -379,18 +383,16 @@
     early = swap(early)
 
     whole = (32, 32, LANES)
-    near = {0: [], 1: [odd_right], 3: [odd_left]}
-    out = correlate(place, 0, early, {0: [], 1: [early], 2: [early], 3: [early]}, None, True, 0, [odd_left, odd_right])
-    first, second = take([(odd_left, whole, (0, 0, 0)), (odd_right, whole, (0, 1, 0))], (out,))
+    first, second = take([(odd_left, whole, (0, 0, 0)), (odd_right, whole, (0, 1, 0))])
     odd_far = up(first), down(second)
-    out = correlate(place, 1, odd, near, out, True, 0)
-    out = correlate(place, 3, odd, near, out, True, 1)
+    out = correlate(place, 0, early, {0: [], 1: [early], 2: [early], 3: [early]}, None, True)
     first, second = take([(even_left, half, lower), (even_right, half, upper)], (out,))
     even_far = [up(first), down(second)]
-    out = correlate(place, 2, even, {0: [], 1: [even_right], 3: [even_left]}, out, True, 0, list(odd_far))
-    out = correlate(place, 1, odd, {2: [odd_far[0]]}, out, False, 0)
-    out = correlate(place, 3, odd, {2: [odd_far[1]]}, out, False, 1)
-    out = correlate(place, 2, even, {2: even_far}, out, False, 0)
+    out = correlate(place, 2, even, {0: [], 1: [even_right], 3: [even_left]}, out, True)
+    for k in range(2):
+        planes = {0: [], 1: [odd_right], 2: [odd_far[k]], 3: [odd_left]}
+        out = correlate(place, 2 * k + 1, odd, planes, out, True, k)
+    out = correlate(place, 2, even, {2: even_far}, out, False)
     return out.reshape(16, ROWS, 1024)
 
 

time: 145 us -> 140 us (0.966)
  local copies, waits for them, and re-layouts: 11.2 us -> 4.9 us
  starting transfers between devices: 32.7 us -> 38.8 us
  waiting for transfers between devices: 55.9 us -> 52.1 us
    ppermute x1 -> x2, waiting for transfers between devices: 10.2 us -> 1.7 us  [body(): halo.append(lax.ppermute(passed, 'tm', later))]
    unnamed x28 -> x18, local copies, waits for them, and re-layouts: 11.2 us -> 4.9 us
    ppermute x6, waiting for transfers between devices: 13.4 us -> 18.7 us  [up(): return lax.ppermute(x, 'inp', [(i, (i + 1) % ring) for i in range(ring)])]
    pallas_call x7 -> x5, Pallas kernels: 22 us -> 17.4 us  [correlate(): pl.pallas_call(kernel, out_shape=jax.ShapeDtypeStruct((4, 4, ROWS, 1024),...]
    ppermute x6, starting transfers between devices: 14.6 us -> 19 us  [down(): return lax.ppermute(x, 'inp', [(i, (i - 1) % ring) for i in range(ring)])]
    ppermute x1 -> x2, starting transfers between devices: 1.92 us -> 5.85 us  [body(): halo.append(lax.ppermute(passed, 'tm', later))]
    pallas_call x2 -> x3, Pallas kernels: 18 us -> 20.8 us  [spectra(): pl.pallas_call(kernel, out_shape=[jax.ShapeDtypeStruct((n * len(g), 256,...]
    ppermute x6, starting transfers between devices: 2.38 us -> 0.16 us  [up(): return lax.ppermute(x, 'inp', [(i, (i + 1) % ring) for i in range(ring)])]
  transfers between devices with their start and end apart: 15 -> 16, of which waited for: 8 -> 8; matrix products, arithmetic and copies ran while one was open for 0% -> 0% of each run, Pallas kernels for 23% -> 25%
where the time goes in v2:
time: 140 us
  waiting for transfers between devices  52.1 us (37%)
  Pallas kernels  43.6 us (31%)
  starting transfers between devices  38.8 us (28%)
  local copies, waits for them, and re-layouts  4.9 us (4%)
    ppermute x6, waiting for transfers between devices, down(): return lax.ppermute(x, 'inp', [(i, (i - 1) % ring) for i in range(ring)])  31.8 us
    pallas_call x3, Pallas kernels, spectra(): pl.pallas_call(kernel, out_shape=[jax.ShapeDtypeStruct((n * len(g), 256,...  20.8 us
    ppermute x6, starting transfers between devices, down(): return lax.ppermute(x, 'inp', [(i, (i - 1) % ring) for i in range(ring)])  19 us
    ppermute x6, waiting for transfers between devices, up(): return lax.ppermute(x, 'inp', [(i, (i + 1) % ring) for i in range(ring)])  18.7 us
    pallas_call x5, Pallas kernels, correlate(): pl.pallas_call(kernel, out_shape=jax.ShapeDtypeStruct((4, 4, ROWS, 1024),...  17.4 us
    all_to_all x2, starting transfers between devices, swap(): return lax.all_to_all(x, 'tm', split_axis=0, concat_axis=0, tiled=True)  13.8 us
    ppermute x2, starting transfers between devices, body(): halo.append(lax.ppermute(passed, 'tm', later))  5.85 us
    unnamed x18, local copies, waits for them, and re-layouts  4.9 us
  transfers between devices with their start and end apart: 16, of which 8 were waited for; matrix products, arithmetic and copies ran while one was open for 0% of the time, Pallas kernels for 25%

profile of v2, /device:TPU:2, one launch (start us, length us, event | category | flops | bytes accessed | tf_op | source)
XLA Modules:
  0.0 139.6 jit_solution(10705285313771584387)
XLA Ops:
  0.0 0.0 copy-start.4
  0.0 0.8 copy-done.4
  0.8 0.0 copy-start.6
  0.8 1.4 %copy-done.6 = bf16[256,3072]{1,0:T(8,128)(2,1)S(1)} copy-done((bf16[256,3072]{1,0:T(8,128)(2,1)S(1)}, bf16[256,3072]{1,0:T(8,128)(2,1)}, u32[]{:S(2)}) %copy-start.6) | copy-done | bytes 1572888
  2.2 4.5 %spectra.4 = bf16[12,256,128]{2,1,0:T(8,128)(2,1)S(1)} custom-call(bf16[256,4,2048]{2,1,0:T(4,128)(2,1)} %refs_0_.5, f32[4,2048]{1,0:T(4,128)S(1)} %copy-done.4, bf16[256,3072]{1,0:T(8,128)(2,1)S(1)} %copy-done.6), custom_call_target="tpu_custom_call" | custom-call | flops 3600000000 | bytes 12582912 | tf_op jit(solution)/shard_map/spectra/pallas_call | solution.py:138
  6.7 0.0 copy-start.5
  6.7 1.9 %collective-permute-start = (bf16[12,256,128]{2,1,0:T(8,128)(2,1)S(1)}, bf16[12,256,128]{2,1,0:T(8,128)(2,1)S(1)}, u32[]{:S(2)}, u32[]{:S(2)}) collective-permute-start(bf16[12,256,128]{2,1,0:T(8,128)(2,1)S(1)} %spectra.4), channel_id=1, source_target_pairs={{0,1},{1,2},{2,3},{3,4},{4,5},{5,6},{6,7},{7,8},{8,9},{9,10},{10,1... | collective-permute-start | bytes 2359304 | tf_op jit(solution)/shard_map/ppermute | solution.py:370
  8.7 4.5 %spectra.5 = bf16[12,256,128]{2,1,0:T(8,128)(2,1)S(1)} custom-call(bf16[256,4,2048]{2,1,0:T(4,128)(2,1)} %refs_0_.5, f32[4,2048]{1,0:T(4,128)S(1)} %copy-done.4, bf16[256,3072]{1,0:T(8,128)(2,1)S(1)} %copy-done.6), custom_call_target="tpu_custom_call" | custom-call | flops 3600000000 | bytes 12582912 | tf_op jit(solution)/shard_map/spectra/pallas_call | solution.py:138
  13.2 3.9 %collective-permute-start.1 = (bf16[12,256,128]{2,1,0:T(8,128)(2,1)S(1)}, bf16[12,256,128]{2,1,0:T(8,128)(2,1)S(1)}, u32[]{:S(2)}, u32[]{:S(2)}) collective-permute-start(bf16[12,256,128]{2,1,0:T(8,128)(2,1)S(1)} %spectra.5), channel_id=1, source_target_pairs={{0,1},{1,2},{2,3},{3,4},{4,5},{5,6},{6,7},{7,8},{8,9},{9,10},{10,1... | collective-permute-start | bytes 2359304 | tf_op jit(solution)/shard_map/ppermute | solution.py:370
  17.1 0.0 copy-done.5
  17.2 11.7 %spectra.3 = (f32[4,256,256]{2,1,0:T(8,128)S(1)}, f32[4,256,256]{2,1,0:T(8,128)S(1)}, f32[4,256,256]{2,1,0:T(8,128)S(1)}, f32[4,256,256]{2,1,0:T(8,128)S(1)}) custom-call(bf16[256,4,2048]{2,1,0:T(4,128)(2,1)} %refs_0_.5, f32[4,2048]{1,0:T(4,128)S(1)} %copy-done.5, bf16[256,3072]{1,0:T(8,128)(2,1)S(1)} %copy-done.6, bf16[256,3072]{1,0:T(8,128)(2,1)} %constant.11.clone.refs_3_), custom_call_target="tpu_custom_call" | custom-call | flops 4800000000 | bytes 12582912 | tf_op jit(solution)/shard_map/spectra/pallas_call | solution.py:138
  28.9 0.0 collective-permute-done.refs_1_.refs_3_
  28.9 1.7 %collective-permute-done.1.refs_2_.refs_4_ = bf16[12,256,128]{2,1,0:T(8,128)(2,1)S(1)} collective-permute-done((bf16[12,256,128]{2,1,0:T(8,128)(2,1)S(1)}, bf16[12,256,128]{2,1,0:T(8,128)(2,1)S(1)}, u32[]{:S(2)}, u32[]{:S(2)}) %collective-permute-start.1) | collective-permute-done | bytes 786464 | tf_op jit(solution)/shard_map/ppermute | solution.py:370
  30.6 0.2 combine.2.refs_5_.own
  30.8 1.8 %combine.3 = bf16[32,96,256]{2,1,0:T(8,128)(2,1)} custom-call(f32[4,256,256]{2,1,0:T(8,128)S(1)} %get-tuple-element.17.refs_0_, f32[4,256,256]{2,1,0:T(8,128)S(1)} %get-tuple-element.18.refs_1_, f32[4,256,256]{2,1,0:T(8,128)S(1)} %get-tuple-element.19.refs_2_, bf16[12,256,128]{2,1,0:T(8,128)(2,1)S(1)} %collective-permute-done.refs_1_.refs_3_, ...), custom_call_target="tpu_custom_call" | custom-call | flops 3145728 | bytes 6291456 | tf_op jit(solution)/shard_map/combine/pallas_call | solution.py:181
  32.6 6.4 %all-to-all-start = ((bf16[32,96,256]{2,1,0:T(8,128)(2,1)}), bf16[32,96,256]{2,1,0:T(8,128)(2,1)S(1)}, u32[]{:S(2)}, u32[]{:S(2)}) async-start(bf16[32,96,256]{2,1,0:T(8,128)(2,1)} %combine.3), calls=%async_computation | async-start | bytes 3145728 | tf_op jit(solution)/shard_map/all_to_all | solution.py:365
  39.0 3.1 %collective-permute-start.4 = (bf16[32,32,256]{2,1,0:T(8,128)(2,1)S(1)}, bf16[32,32,256]{2,1,0:T(8,128)(2,1)S(1)}, u32[]{:S(2)}, u32[]{:S(2)}) collective-permute-start(bf16[32,32,256]{2,1,0:T(8,128)(2,1)S(1)} %combine.2.refs_5_.own), channel_id=1, source_target_pairs={{0,96},{32,0},{64,32},{96,64},{1,97},{33,1},{65,33},{97,65},{2,98}... | collective-permute-start | bytes 1572872 | tf_op jit(solution)/shard_map/ppermute | solution.py:362
  42.0 0.0 collective-permute-start.5
  42.0 11.5 %collective-permute-done.4.refs_1_.right = bf16[32,32,256]{2,1,0:T(8,128)(2,1)S(1)} collective-permute-done((bf16[32,32,256]{2,1,0:T(8,128)(2,1)S(1)}, bf16[32,32,256]{2,1,0:T(8,128)(2,1)S(1)}, u32[]{:S(2)}, u32[]{:S(2)}) %collective-permute-start.4) | collective-permute-done | bytes 524320 | tf_op jit(solution)/shard_map/ppermute | solution.py:362
  53.5 3.4 %collective-permute-done.5.refs_0_.left = bf16[32,32,256]{2,1,0:T(8,128)(2,1)S(1)} collective-permute-done((bf16[32,32,256]{2,1,0:T(8,128)(2,1)S(1)}, bf16[32,32,256]{2,1,0:T(8,128)(2,1)S(1)}, u32[]{:S(2)}, u32[]{:S(2)}) %collective-permute-start.5) | collective-permute-done | bytes 524320 | tf_op jit(solution)/shard_map/ppermute | solution.py:359
  57.0 0.1 collective-permute-start.6
  57.1 3.2 %collective-permute-start.7 = (bf16[16,32,256]{2,1,0:T(8,128)(2,1)S(1)}, bf16[16,32,256]{2,1,0:T(8,128)(2,1)S(1)}, u32[]{:S(2)}, u32[]{:S(2)}) collective-permute-start(bf16[16,32,256]{2,1,0:T(8,128)(2,1)S(1)} %get-tuple-element.23), channel_id=1, source_target_pairs={{0,96},{32,0},{64,32},{96,64},{1,97},{33,1},{65,33},{97,65},{2,98}... | collective-permute-start | bytes 786440 | tf_op jit(solution)/shard_map/ppermute | solution.py:362
  60.3 5.2 %collective-permute-done.6.far_a = bf16[16,32,256]{2,1,0:T(8,128)(2,1)S(1)} collective-permute-done((bf16[16,32,256]{2,1,0:T(8,128)(2,1)S(1)}, bf16[16,32,256]{2,1,0:T(8,128)(2,1)S(1)}, u32[]{:S(2)}, u32[]{:S(2)}) %collective-permute-start.6) | collective-permute-done | bytes 262176 | tf_op jit(solution)/shard_map/ppermute | solution.py:359
  65.5 0.0 collective-permute-done.7.far_b
  65.5 0.2 pack.1
  65.7 0.0 copy-start.2
  65.7 1.3 copy-done.2
  67.0 0.0 all-to-all-done.refs_0_.refs_1_
  67.0 7.4 %all-to-all-start.1 = ((bf16[32,128,256]{2,1,0:T(8,128)(2,1)}), bf16[32,128,256]{2,1,0:T(8,128)(2,1)}, u32[]{:S(2)}, u32[]{:S(2)}) async-start(bf16[32,128,256]{2,1,0:T(8,128)(2,1)} %copy-done.2), calls=%async_computation.1 | async-start | bytes 4194304 | tf_op jit(solution)/shard_map/all_to_all | solution.py:365
  74.5 0.9 take.4
  75.4 0.0 copy-start.3
  75.4 3.0 %collective-permute-start.10 = (bf16[32,64,256]{2,1,0:T(8,128)(2,1)S(1)}, bf16[32,64,256]{2,1,0:T(8,128)(2,1)S(1)}, u32[]{:S(2)}, u32[]{:S(2)}) collective-permute-start(bf16[32,64,256]{2,1,0:T(8,128)(2,1)S(1)} %get-tuple-element.26.refs_1_), channel_id=1, source_target_pairs={{0,96},{32,0},{64,32},{96,64},{1,97},{33,1},{65,33},{97,65},{2,98}... | collective-permute-start | bytes 3145736 | tf_op jit(solution)/shard_map/ppermute | solution.py:362
  78.3 0.0 collective-permute-start.11
  78.3 0.0 collective-permute-start.2
  78.3 3.3 %collective-permute-start.3 = (bf16[32,32,256]{2,1,0:T(8,128)(2,1)}, bf16[32,32,256]{2,1,0:T(8,128)(2,1)}, u32[]{:S(2)}, u32[]{:S(2)}) collective-permute-start(bf16[32,32,256]{2,1,0:T(8,128)(2,1)} %get-tuple-element.21.refs_1_), channel_id=1, source_target_pairs={{0,96},{32,0},{64,32},{96,64},{1,97},{33,1},{65,33},{97,65},{2,98}... | collective-permute-start | bytes 1572872 | tf_op jit(solution)/shard_map/ppermute | solution.py:362
  81.6 20.3 %collective-permute-done.10.refs_1_.refs_2_ = bf16[32,64,256]{2,1,0:T(8,128)(2,1)S(1)} collective-permute-done((bf16[32,64,256]{2,1,0:T(8,128)(2,1)S(1)}, bf16[32,64,256]{2,1,0:T(8,128)(2,1)S(1)}, u32[]{:S(2)}, u32[]{:S(2)}) %collective-permute-start.10) | collective-permute-done | bytes 1048608 | tf_op jit(solution)/shard_map/ppermute | solution.py:362
  101.9 0.0 copy-start
  101.9 3.7 %collective-permute-done.11.refs_0_.refs_4_ = bf16[32,64,256]{2,1,0:T(8,128)(2,1)S(1)} collective-permute-done((bf16[32,64,256]{2,1,0:T(8,128)(2,1)S(1)}, bf16[32,64,256]{2,1,0:T(8,128)(2,1)S(1)}, u32[]{:S(2)}, u32[]{:S(2)}) %collective-permute-start.11) | collective-permute-done | bytes 1048608 | tf_op jit(solution)/shard_map/ppermute | solution.py:359
  105.6 0.0 copy-start.1
  105.6 1.2 take.7
  106.8 0.0 collective-permute-start.13
  106.8 3.2 %collective-permute-start.12 = (bf16[32,32,256]{2,1,0:T(8,128)(2,1)}, bf16[32,32,256]{2,1,0:T(8,128)(2,1)}, u32[]{:S(2)}, u32[]{:S(2)}) collective-permute-start(bf16[32,32,256]{2,1,0:T(8,128)(2,1)} %get-tuple-element.27), channel_id=1, source_target_pairs={{0,96},{32,0},{64,32},{96,64},{1,97},{33,1},{65,33},{97,65},{2,98}... | collective-permute-start | bytes 1572872 | tf_op jit(solution)/shard_map/ppermute | solution.py:362
  110.0 0.0 all-to-all-done.1.refs_1_.refs_2_.refs_3_.refs_4_
  110.0 3.8 %correlate.5.refs_2_.refs_4_ = f32[4,4,256,1024]{3,2,1,0:T(8,128)} custom-call(s32[1]{0:T(128)} %bitcast.refs_0_, bf16[32,128,256]{2,1,0:T(8,128)(2,1)} %all-to-all-done.1.refs_1_.refs_2_.refs_3_.refs_4_, bf16[32,128,256]{2,1,0:T(8,128)(2,1)} %all-to-all-done.1.refs_1_.refs_2_.refs_3_.refs_4_, ...), custom_call_target="tpu_custom_call" | custom-call | flops 640000000 | bytes 6291456 | tf_op jit(solution)/shard_map/correlate/pallas_call | solution.py:338
  113.8 0.0 copy-done.3
  113.8 0.0 copy-done
  113.8 0.0 copy-done.1
  113.8 3.1 %collective-permute-done.2.refs_0_.refs_3_ = bf16[32,32,256]{2,1,0:T(8,128)(2,1)} collective-permute-done((bf16[32,32,256]{2,1,0:T(8,128)(2,1)}, bf16[32,32,256]{2,1,0:T(8,128)(2,1)}, u32[]{:S(2)}, u32[]{:S(2)}) %collective-permute-start.2) | collective-permute-done | bytes 524320 | tf_op jit(solution)/shard_map/ppermute | solution.py:359
  116.9 0.0 collective-permute-done.3.refs_1_.refs_2_
  116.9 1.1 take.6
  118.0 0.1 collective-permute-start.8
  118.1 3.2 %collective-permute-start.9 = (bf16[16,32,256]{2,1,0:T(8,128)(2,1)S(1)}, bf16[16,32,256]{2,1,0:T(8,128)(2,1)S(1)}, u32[]{:S(2)}, u32[]{:S(2)}) collective-permute-start(bf16[16,32,256]{2,1,0:T(8,128)(2,1)S(1)} %get-tuple-element.25), channel_id=1, source_target_pairs={{0,96},{32,0},{64,32},{96,64},{1,97},{33,1},{65,33},{97,65},{2,98}... | collective-permute-start | bytes 786440 | tf_op jit(solution)/shard_map/ppermute | solution.py:362
  121.3 3.6 %correlate.6.refs_5_ = f32[4,4,256,1024]{3,2,1,0:T(8,128)} custom-call(s32[1]{0:T(128)} %bitcast.refs_0_, bf16[32,32,256]{2,1,0:T(8,128)(2,1)} %get-tuple-element.21.refs_1_, bf16[32,32,256]{2,1,0:T(8,128)(2,1)} %collective-permute-done.3.refs_1_.refs_2_, ...), custom_call_target="tpu_custom_call", output_to_operand_aliasing={{}: (4, {})} | custom-call | flops 480000000 | bytes 6291456 | tf_op jit(solution)/shard_map/correlate/pallas_call | solution.py:338
  124.9 3.2 %collective-permute-done.13.refs_3_ = bf16[32,32,256]{2,1,0:T(8,128)(2,1)} collective-permute-done((bf16[32,32,256]{2,1,0:T(8,128)(2,1)}, bf16[32,32,256]{2,1,0:T(8,128)(2,1)}, u32[]{:S(2)}, u32[]{:S(2)}) %collective-permute-start.13) | collective-permute-done | bytes 524320 | tf_op jit(solution)/shard_map/ppermute | solution.py:359
  128.2 3.8 %correlate.7.refs_5_ = f32[4,4,256,1024]{3,2,1,0:T(8,128)} custom-call(s32[1]{0:T(128)} %bitcast.refs_0_, bf16[32,64,256]{2,1,0:T(8,128)(2,1)} %copy-done.3, bf16[32,64,256]{2,1,0:T(8,128)(2,1)} %copy-done, bf16[32,32,256]{2,1,0:T(8,128)(2,1)} %collective-permute-done.13.refs_3_, bf16[32,64,256]{2,1,0:T(8,128)(2,1)} %copy-done.1, ...), custom_call_target="tpu_custom_call", output_to_operand_aliasing={{}: (5, {})} | custom-call | flops 640000000 | bytes 6291456 | tf_op jit(solution)/shard_map/correlate/pallas_call | solution.py:338
  131.9 0.0 collective-permute-done.12.refs_3_
  131.9 3.8 %correlate.8.refs_4_ = f32[4,4,256,1024]{3,2,1,0:T(8,128)} custom-call(s32[1]{0:T(128)} %bitcast.refs_0_, bf16[32,64,256]{2,1,0:T(8,128)(2,1)} %copy-done.3, bf16[32,64,256]{2,1,0:T(8,128)(2,1)} %copy-done, bf16[32,32,256]{2,1,0:T(8,128)(2,1)} %collective-permute-done.12.refs_3_, bf16[32,64,256]{2,1,0:T(8,128)(2,1)} %copy-done.1, ...), custom_call_target="tpu_custom_call", output_to_operand_aliasing={{}: (5, {})} | custom-call | flops 640000000 | bytes 6291456 | tf_op jit(solution)/shard_map/correlate/pallas_call | solution.py:338
  135.7 0.0 collective-permute-done.8.refs_2_
  135.7 0.0 copy-start.7
  135.8 0.0 collective-permute-done.9.refs_3_
  135.8 0.7 copy-done.7
  136.4 0.0 copy-start.8
  136.5 0.7 copy-done.8
  137.2 2.5 %correlate.9 = f32[4,4,256,1024]{3,2,1,0:T(8,128)} custom-call(s32[1]{0:T(128)} %bitcast.refs_0_, bf16[32,32,256]{2,1,0:T(8,128)(2,1)} %get-tuple-element.21.refs_1_, bf16[16,32,256]{2,1,0:T(8,128)(2,1)} %copy-done.7, bf16[16,32,256]{2,1,0:T(8,128)(2,1)} %copy-done.8, f32[4,4,256,1024]{3,2,1,0:T(8,128)} %correlate.8.refs_4_), custom_call_target="tpu_custom_call", output_to_operand_aliasing={{}: (4, {})} | custom-call | flops 160000000 | bytes 6291456 | tf_op jit(solution)/shard_map/correlate/pallas_call | solution.py:338
  (1 shorter events, 0.0 us)
Async XLA Ops:
  0.0 0.8 copy-start.4
  0.8 1.4 %copy-start.6 = (bf16[256,3072]{1,0:T(8,128)(2,1)S(1)}, bf16[256,3072]{1,0:T(8,128)(2,1)}, u32[]{:S(2)}) copy-start(bf16[256,3072]{1,0:T(8,128)(2,1)} %constant.10.clone.refs_2_) | copy-start | bytes 4718596
  6.7 10.4 %copy-start.5 = (f32[4,2048]{1,0:T(4,128)S(1)}, f32[4,2048]{1,0:T(4,128)}, u32[]{:S(2)}) copy-start(f32[4,2048]{1,0:T(4,128)} %refs_1_.5) | copy-start | bytes 98308
  6.7 22.1 %collective-permute-start = (bf16[12,256,128]{2,1,0:T(8,128)(2,1)S(1)}, bf16[12,256,128]{2,1,0:T(8,128)(2,1)S(1)}, u32[]{:S(2)}, u32[]{:S(2)}) collective-permute-start(bf16[12,256,128]{2,1,0:T(8,128)(2,1)S(1)} %spectra.4), channel_id=1, source_target_pairs={{0,1},{1,2},{2,3},{3,4},{4,5},{5,6},{6,7},{7,8},{8,9},{9,10},{10,1... | collective-permute-start | bytes 2359304 | tf_op jit(solution)/shard_map/ppermute | solution.py:370
  13.2 17.4 %collective-permute-start.1 = (bf16[12,256,128]{2,1,0:T(8,128)(2,1)S(1)}, bf16[12,256,128]{2,1,0:T(8,128)(2,1)S(1)}, u32[]{:S(2)}, u32[]{:S(2)}) collective-permute-start(bf16[12,256,128]{2,1,0:T(8,128)(2,1)S(1)} %spectra.5), channel_id=1, source_target_pairs={{0,1},{1,2},{2,3},{3,4},{4,5},{5,6},{6,7},{7,8},{8,9},{9,10},{10,1... | collective-permute-start | bytes 2359304 | tf_op jit(solution)/shard_map/ppermute | solution.py:370
  32.6 34.4 %all-to-all-start = ((bf16[32,96,256]{2,1,0:T(8,128)(2,1)}), bf16[32,96,256]{2,1,0:T(8,128)(2,1)S(1)}, u32[]{:S(2)}, u32[]{:S(2)}) async-start(bf16[32,96,256]{2,1,0:T(8,128)(2,1)} %combine.3), calls=%async_computation | async-start | bytes 3145728 | tf_op jit(solution)/shard_map/all_to_all | solution.py:365
  39.0 14.6 %collective-permute-start.4 = (bf16[32,32,256]{2,1,0:T(8,128)(2,1)S(1)}, bf16[32,32,256]{2,1,0:T(8,128)(2,1)S(1)}, u32[]{:S(2)}, u32[]{:S(2)}) collective-permute-start(bf16[32,32,256]{2,1,0:T(8,128)(2,1)S(1)} %combine.2.refs_5_.own), channel_id=1, source_target_pairs={{0,96},{32,0},{64,32},{96,64},{1,97},{33,1},{65,33},{97,65},{2,98}... | collective-permute-start | bytes 1572872 | tf_op jit(solution)/shard_map/ppermute | solution.py:362
  42.0 14.9 %collective-permute-start.5 = (bf16[32,32,256]{2,1,0:T(8,128)(2,1)S(1)}, bf16[32,32,256]{2,1,0:T(8,128)(2,1)S(1)}, u32[]{:S(2)}, u32[]{:S(2)}) collective-permute-start(bf16[32,32,256]{2,1,0:T(8,128)(2,1)S(1)} %combine.2.refs_5_.own), channel_id=1, source_target_pairs={{0,32},{32,64},{64,96},{96,0},{1,33},{33,65},{65,97},{97,1},{2,34}... | collective-permute-start | bytes 1572872 | tf_op jit(solution)/shard_map/ppermute | solution.py:359
  57.0 8.5 %collective-permute-start.6 = (bf16[16,32,256]{2,1,0:T(8,128)(2,1)S(1)}, bf16[16,32,256]{2,1,0:T(8,128)(2,1)S(1)}, u32[]{:S(2)}, u32[]{:S(2)}) collective-permute-start(bf16[16,32,256]{2,1,0:T(8,128)(2,1)S(1)} %get-tuple-element.22), channel_id=1, source_target_pairs={{0,32},{32,64},{64,96},{96,0},{1,33},{33,65},{65,97},{97,1},{2,34}... | collective-permute-start | bytes 786440 | tf_op jit(solution)/shard_map/ppermute | solution.py:359
  57.1 8.4 %collective-permute-start.7 = (bf16[16,32,256]{2,1,0:T(8,128)(2,1)S(1)}, bf16[16,32,256]{2,1,0:T(8,128)(2,1)S(1)}, u32[]{:S(2)}, u32[]{:S(2)}) collective-permute-start(bf16[16,32,256]{2,1,0:T(8,128)(2,1)S(1)} %get-tuple-element.23), channel_id=1, source_target_pairs={{0,96},{32,0},{64,32},{96,64},{1,97},{33,1},{65,33},{97,65},{2,98}... | collective-permute-start | bytes 786440 | tf_op jit(solution)/shard_map/ppermute | solution.py:362
  65.7 1.3 copy-start.2
  67.0 43.0 %all-to-all-start.1 = ((bf16[32,128,256]{2,1,0:T(8,128)(2,1)}), bf16[32,128,256]{2,1,0:T(8,128)(2,1)}, u32[]{:S(2)}, u32[]{:S(2)}) async-start(bf16[32,128,256]{2,1,0:T(8,128)(2,1)} %copy-done.2), calls=%async_computation.1 | async-start | bytes 4194304 | tf_op jit(solution)/shard_map/all_to_all | solution.py:365
  75.4 38.4 %copy-start.3 = (bf16[32,64,256]{2,1,0:T(8,128)(2,1)}, bf16[32,64,256]{2,1,0:T(8,128)(2,1)S(1)}, u32[]{:S(2)}) copy-start(bf16[32,64,256]{2,1,0:T(8,128)(2,1)S(1)} %get-tuple-element.26.refs_1_) | copy-start | bytes 3145732
  75.4 26.5 %collective-permute-start.10 = (bf16[32,64,256]{2,1,0:T(8,128)(2,1)S(1)}, bf16[32,64,256]{2,1,0:T(8,128)(2,1)S(1)}, u32[]{:S(2)}, u32[]{:S(2)}) collective-permute-start(bf16[32,64,256]{2,1,0:T(8,128)(2,1)S(1)} %get-tuple-element.26.refs_1_), channel_id=1, source_target_pairs={{0,96},{32,0},{64,32},{96,64},{1,97},{33,1},{65,33},{97,65},{2,98}... | collective-permute-start | bytes 3145736 | tf_op jit(solution)/shard_map/ppermute | solution.py:362
  78.3 27.3 %collective-permute-start.11 = (bf16[32,64,256]{2,1,0:T(8,128)(2,1)S(1)}, bf16[32,64,256]{2,1,0:T(8,128)(2,1)S(1)}, u32[]{:S(2)}, u32[]{:S(2)}) collective-permute-start(bf16[32,64,256]{2,1,0:T(8,128)(2,1)S(1)} %get-tuple-element.26.refs_1_), channel_id=1, source_target_pairs={{0,32},{32,64},{64,96},{96,0},{1,33},{33,65},{65,97},{97,1},{2,34}... | collective-permute-start | bytes 3145736 | tf_op jit(solution)/shard_map/ppermute | solution.py:359
  78.3 38.6 %collective-permute-start.2 = (bf16[32,32,256]{2,1,0:T(8,128)(2,1)}, bf16[32,32,256]{2,1,0:T(8,128)(2,1)}, u32[]{:S(2)}, u32[]{:S(2)}) collective-permute-start(bf16[32,32,256]{2,1,0:T(8,128)(2,1)} %get-tuple-element.21.refs_1_), channel_id=1, source_target_pairs={{0,32},{32,64},{64,96},{96,0},{1,33},{33,65},{65,97},{97,1},{2,34}... | collective-permute-start | bytes 1572872 | tf_op jit(solution)/shard_map/ppermute | solution.py:359
  78.3 38.6 %collective-permute-start.3 = (bf16[32,32,256]{2,1,0:T(8,128)(2,1)}, bf16[32,32,256]{2,1,0:T(8,128)(2,1)}, u32[]{:S(2)}, u32[]{:S(2)}) collective-permute-start(bf16[32,32,256]{2,1,0:T(8,128)(2,1)} %get-tuple-element.21.refs_1_), channel_id=1, source_target_pairs={{0,96},{32,0},{64,32},{96,64},{1,97},{33,1},{65,33},{97,65},{2,98}... | collective-permute-start | bytes 1572872 | tf_op jit(solution)/shard_map/ppermute | solution.py:362
  101.9 12.0 %copy-start = (bf16[32,64,256]{2,1,0:T(8,128)(2,1)}, bf16[32,64,256]{2,1,0:T(8,128)(2,1)S(1)}, u32[]{:S(2)}) copy-start(bf16[32,64,256]{2,1,0:T(8,128)(2,1)S(1)} %collective-permute-done.10.refs_1_.refs_2_) | copy-start | bytes 3145732
  105.6 8.2 %copy-start.1 = (bf16[32,64,256]{2,1,0:T(8,128)(2,1)}, bf16[32,64,256]{2,1,0:T(8,128)(2,1)S(1)}, u32[]{:S(2)}) copy-start(bf16[32,64,256]{2,1,0:T(8,128)(2,1)S(1)} %collective-permute-done.11.refs_0_.refs_4_) | copy-start | bytes 3145732
  106.8 21.4 %collective-permute-start.13 = (bf16[32,32,256]{2,1,0:T(8,128)(2,1)}, bf16[32,32,256]{2,1,0:T(8,128)(2,1)}, u32[]{:S(2)}, u32[]{:S(2)}) collective-permute-start(bf16[32,32,256]{2,1,0:T(8,128)(2,1)} %get-tuple-element.28), channel_id=1, source_target_pairs={{0,32},{32,64},{64,96},{96,0},{1,33},{33,65},{65,97},{97,1},{2,34}... | collective-permute-start | bytes 1572872 | tf_op jit(solution)/shard_map/ppermute | solution.py:359
  106.8 25.1 %collective-permute-start.12 = (bf16[32,32,256]{2,1,0:T(8,128)(2,1)}, bf16[32,32,256]{2,1,0:T(8,128)(2,1)}, u32[]{:S(2)}, u32[]{:S(2)}) collective-permute-start(bf16[32,32,256]{2,1,0:T(8,128)(2,1)} %get-tuple-element.27), channel_id=1, source_target_pairs={{0,96},{32,0},{64,32},{96,64},{1,97},{33,1},{65,33},{97,65},{2,98}... | collective-permute-start | bytes 1572872 | tf_op jit(solution)/shard_map/ppermute | solution.py:362
  118.0 17.7 %collective-permute-start.8 = (bf16[16,32,256]{2,1,0:T(8,128)(2,1)S(1)}, bf16[16,32,256]{2,1,0:T(8,128)(2,1)S(1)}, u32[]{:S(2)}, u32[]{:S(2)}) collective-permute-start(bf16[16,32,256]{2,1,0:T(8,128)(2,1)S(1)} %get-tuple-element.24), channel_id=1, source_target_pairs={{0,32},{32,64},{64,96},{96,0},{1,33},{33,65},{65,97},{97,1},{2,34}... | collective-permute-start | bytes 786440 | tf_op jit(solution)/shard_map/ppermute | solution.py:359
  118.1 17.7 %collective-permute-start.9 = (bf16[16,32,256]{2,1,0:T(8,128)(2,1)S(1)}, bf16[16,32,256]{2,1,0:T(8,128)(2,1)S(1)}, u32[]{:S(2)}, u32[]{:S(2)}) collective-permute-start(bf16[16,32,256]{2,1,0:T(8,128)(2,1)S(1)} %get-tuple-element.25), channel_id=1, source_target_pairs={{0,96},{32,0},{64,32},{96,64},{1,97},{33,1},{65,33},{97,65},{2,98}... | collective-permute-start | bytes 786440 | tf_op jit(solution)/shard_map/ppermute | solution.py:362
  135.7 0.7 copy-start.7
  136.4 0.7 copy-start.8

commit v3 on v2

--- a/solution.py
+++ b/solution.py
@@ -385,13 +385,15 @@
     whole = (32, 32, LANES)
     first, second = take([(odd_left, whole, (0, 0, 0)), (odd_right, whole, (0, 1, 0))])
     odd_far = up(first), down(second)
+    near = {0: [], 1: [odd_right], 3: [odd_left]}
     out = correlate(place, 0, early, {0: [], 1: [early], 2: [early], 3: [early]}, None, True)
+    out = correlate(place, 1, odd, near, out, True, 0)
     first, second = take([(even_left, half, lower), (even_right, half, upper)], (out,))
     even_far = [up(first), down(second)]
+    out = correlate(place, 3, odd, near, out, True, 1)
     out = correlate(place, 2, even, {0: [], 1: [even_right], 3: [even_left]}, out, True)
     for k in range(2):
-        planes = {0: [], 1: [odd_right], 2: [odd_far[k]], 3: [odd_left]}
-        out = correlate(place, 2 * k + 1, odd, planes, out, True, k)
+        out = correlate(place, 2 * k + 1, odd, {2: [odd_far[k]]}, out, False, k)
     out = correlate(place, 2, even, {2: even_far}, out, False)
     return out.reshape(16, ROWS, 1024)
 

time: 140 us -> 138 us (0.986)
  waiting for transfers between devices: 52.1 us -> 45.8 us
  Pallas kernels: 43.6 us -> 48.2 us
    ppermute x6, waiting for transfers between devices: 18.7 us -> 12.3 us  [up(): return lax.ppermute(x, 'inp', [(i, (i + 1) % ring) for i in range(ring)])]
    pallas_call x5 -> x7, Pallas kernels: 17.4 us -> 22 us  [correlate(): pl.pallas_call(kernel, out_shape=jax.ShapeDtypeStruct((4, 4, ROWS, 1024),...]
  transfers between devices with their start and end apart: 16 -> 16, of which waited for: 8 -> 6; matrix products, arithmetic and copies ran while one was open for 0% -> 0% of each run, Pallas kernels for 25% -> 28%
where the time goes in v3:
time: 138 us
  Pallas kernels  48.2 us (35%)
  waiting for transfers between devices  45.8 us (33%)
  starting transfers between devices  38.8 us (28%)
  local copies, waits for them, and re-layouts  4.9 us (4%)
    ppermute x6, waiting for transfers between devices, down(): return lax.ppermute(x, 'inp', [(i, (i - 1) % ring) for i in range(ring)])  31.8 us
    pallas_call x7, Pallas kernels, correlate(): pl.pallas_call(kernel, out_shape=jax.ShapeDtypeStruct((4, 4, ROWS, 1024),...  22 us
    pallas_call x3, Pallas kernels, spectra(): pl.pallas_call(kernel, out_shape=[jax.ShapeDtypeStruct((n * len(g), 256,...  20.8 us
    ppermute x6, starting transfers between devices, down(): return lax.ppermute(x, 'inp', [(i, (i - 1) % ring) for i in range(ring)])  19 us
    all_to_all x2, starting transfers between devices, swap(): return lax.all_to_all(x, 'tm', split_axis=0, concat_axis=0, tiled=True)  13.8 us
    ppermute x6, waiting for transfers between devices, up(): return lax.ppermute(x, 'inp', [(i, (i + 1) % ring) for i in range(ring)])  12.3 us
    ppermute x2, starting transfers between devices, body(): halo.append(lax.ppermute(passed, 'tm', later))  5.85 us
    unnamed x18, local copies, waits for them, and re-layouts  4.9 us
  transfers between devices with their start and end apart: 16, of which 6 were waited for; matrix products, arithmetic and copies ran while one was open for 0% of the time, Pallas kernels for 28%

profile of v3, /device:TPU:2, one launch (start us, length us, event | category | flops | bytes accessed | tf_op | source)
XLA Modules:
  0.0 137.9 jit_solution(8344201661220450043)
XLA Ops:
  0.0 0.0 copy-start.4
  0.0 0.8 copy-done.4
  0.8 0.0 copy-start.6
  0.8 1.4 %copy-done.6 = bf16[256,3072]{1,0:T(8,128)(2,1)S(1)} copy-done((bf16[256,3072]{1,0:T(8,128)(2,1)S(1)}, bf16[256,3072]{1,0:T(8,128)(2,1)}, u32[]{:S(2)}) %copy-start.6) | copy-done | bytes 1572888
  2.2 0.0 copy-start.5
  2.2 4.5 %spectra.4 = bf16[12,256,128]{2,1,0:T(8,128)(2,1)S(1)} custom-call(bf16[256,4,2048]{2,1,0:T(4,128)(2,1)} %refs_0_.5, f32[4,2048]{1,0:T(4,128)S(1)} %copy-done.4, bf16[256,3072]{1,0:T(8,128)(2,1)S(1)} %copy-done.6), custom_call_target="tpu_custom_call" | custom-call | flops 3600000000 | bytes 12582912 | tf_op jit(solution)/shard_map/spectra/pallas_call | solution.py:138
  6.7 1.9 %collective-permute-start = (bf16[12,256,128]{2,1,0:T(8,128)(2,1)S(1)}, bf16[12,256,128]{2,1,0:T(8,128)(2,1)S(1)}, u32[]{:S(2)}, u32[]{:S(2)}) collective-permute-start(bf16[12,256,128]{2,1,0:T(8,128)(2,1)S(1)} %spectra.4), channel_id=1, source_target_pairs={{0,1},{1,2},{2,3},{3,4},{4,5},{5,6},{6,7},{7,8},{8,9},{9,10},{10,1... | collective-permute-start | bytes 2359304 | tf_op jit(solution)/shard_map/ppermute | solution.py:370
  8.7 4.5 %spectra.5 = bf16[12,256,128]{2,1,0:T(8,128)(2,1)S(1)} custom-call(bf16[256,4,2048]{2,1,0:T(4,128)(2,1)} %refs_0_.5, f32[4,2048]{1,0:T(4,128)S(1)} %copy-done.4, bf16[256,3072]{1,0:T(8,128)(2,1)S(1)} %copy-done.6), custom_call_target="tpu_custom_call" | custom-call | flops 3600000000 | bytes 12582912 | tf_op jit(solution)/shard_map/spectra/pallas_call | solution.py:138
  13.2 3.9 %collective-permute-start.1 = (bf16[12,256,128]{2,1,0:T(8,128)(2,1)S(1)}, bf16[12,256,128]{2,1,0:T(8,128)(2,1)S(1)}, u32[]{:S(2)}, u32[]{:S(2)}) collective-permute-start(bf16[12,256,128]{2,1,0:T(8,128)(2,1)S(1)} %spectra.5), channel_id=1, source_target_pairs={{0,1},{1,2},{2,3},{3,4},{4,5},{5,6},{6,7},{7,8},{8,9},{9,10},{10,1... | collective-permute-start | bytes 2359304 | tf_op jit(solution)/shard_map/ppermute | solution.py:370
  17.2 0.0 copy-done.5
  17.2 11.7 %spectra.3 = (f32[4,256,256]{2,1,0:T(8,128)S(1)}, f32[4,256,256]{2,1,0:T(8,128)S(1)}, f32[4,256,256]{2,1,0:T(8,128)S(1)}, f32[4,256,256]{2,1,0:T(8,128)S(1)}) custom-call(bf16[256,4,2048]{2,1,0:T(4,128)(2,1)} %refs_0_.5, f32[4,2048]{1,0:T(4,128)S(1)} %copy-done.5, bf16[256,3072]{1,0:T(8,128)(2,1)S(1)} %copy-done.6, bf16[256,3072]{1,0:T(8,128)(2,1)} %constant.11.clone.refs_3_), custom_call_target="tpu_custom_call" | custom-call | flops 4800000000 | bytes 12582912 | tf_op jit(solution)/shard_map/spectra/pallas_call | solution.py:138
  28.9 0.0 collective-permute-done.refs_1_.refs_3_
  28.9 1.7 %collective-permute-done.1.refs_2_.refs_4_ = bf16[12,256,128]{2,1,0:T(8,128)(2,1)S(1)} collective-permute-done((bf16[12,256,128]{2,1,0:T(8,128)(2,1)S(1)}, bf16[12,256,128]{2,1,0:T(8,128)(2,1)S(1)}, u32[]{:S(2)}, u32[]{:S(2)}) %collective-permute-start.1) | collective-permute-done | bytes 786464 | tf_op jit(solution)/shard_map/ppermute | solution.py:370
  30.6 0.2 combine.2.refs_5_.own
  30.8 1.8 %combine.3 = bf16[32,96,256]{2,1,0:T(8,128)(2,1)} custom-call(f32[4,256,256]{2,1,0:T(8,128)S(1)} %get-tuple-element.17.refs_0_, f32[4,256,256]{2,1,0:T(8,128)S(1)} %get-tuple-element.18.refs_1_, f32[4,256,256]{2,1,0:T(8,128)S(1)} %get-tuple-element.19.refs_2_, bf16[12,256,128]{2,1,0:T(8,128)(2,1)S(1)} %collective-permute-done.refs_1_.refs_3_, ...), custom_call_target="tpu_custom_call" | custom-call | flops 3145728 | bytes 6291456 | tf_op jit(solution)/shard_map/combine/pallas_call | solution.py:181
  32.6 6.4 %all-to-all-start = ((bf16[32,96,256]{2,1,0:T(8,128)(2,1)}), bf16[32,96,256]{2,1,0:T(8,128)(2,1)S(1)}, u32[]{:S(2)}, u32[]{:S(2)}) async-start(bf16[32,96,256]{2,1,0:T(8,128)(2,1)} %combine.3), calls=%async_computation | async-start | bytes 3145728 | tf_op jit(solution)/shard_map/all_to_all | solution.py:365
  39.0 3.1 %collective-permute-start.6 = (bf16[32,32,256]{2,1,0:T(8,128)(2,1)S(1)}, bf16[32,32,256]{2,1,0:T(8,128)(2,1)S(1)}, u32[]{:S(2)}, u32[]{:S(2)}) collective-permute-start(bf16[32,32,256]{2,1,0:T(8,128)(2,1)S(1)} %combine.2.refs_5_.own), channel_id=1, source_target_pairs={{0,96},{32,0},{64,32},{96,64},{1,97},{33,1},{65,33},{97,65},{2,98}... | collective-permute-start | bytes 1572872 | tf_op jit(solution)/shard_map/ppermute | solution.py:362
  42.1 0.0 collective-permute-start.7
  42.1 11.5 %collective-permute-done.6.refs_1_.right = bf16[32,32,256]{2,1,0:T(8,128)(2,1)S(1)} collective-permute-done((bf16[32,32,256]{2,1,0:T(8,128)(2,1)S(1)}, bf16[32,32,256]{2,1,0:T(8,128)(2,1)S(1)}, u32[]{:S(2)}, u32[]{:S(2)}) %collective-permute-start.6) | collective-permute-done | bytes 524320 | tf_op jit(solution)/shard_map/ppermute | solution.py:362
  53.5 3.4 %collective-permute-done.7.refs_0_.left = bf16[32,32,256]{2,1,0:T(8,128)(2,1)S(1)} collective-permute-done((bf16[32,32,256]{2,1,0:T(8,128)(2,1)S(1)}, bf16[32,32,256]{2,1,0:T(8,128)(2,1)S(1)}, u32[]{:S(2)}, u32[]{:S(2)}) %collective-permute-start.7) | collective-permute-done | bytes 524320 | tf_op jit(solution)/shard_map/ppermute | solution.py:359
  57.0 0.1 collective-permute-start.8
  57.1 3.2 %collective-permute-start.9 = (bf16[16,32,256]{2,1,0:T(8,128)(2,1)S(1)}, bf16[16,32,256]{2,1,0:T(8,128)(2,1)S(1)}, u32[]{:S(2)}, u32[]{:S(2)}) collective-permute-start(bf16[16,32,256]{2,1,0:T(8,128)(2,1)S(1)} %get-tuple-element.24), channel_id=1, source_target_pairs={{0,96},{32,0},{64,32},{96,64},{1,97},{33,1},{65,33},{97,65},{2,98}... | collective-permute-start | bytes 786440 | tf_op jit(solution)/shard_map/ppermute | solution.py:362
  60.3 5.2 %collective-permute-done.8.far_a = bf16[16,32,256]{2,1,0:T(8,128)(2,1)S(1)} collective-permute-done((bf16[16,32,256]{2,1,0:T(8,128)(2,1)S(1)}, bf16[16,32,256]{2,1,0:T(8,128)(2,1)S(1)}, u32[]{:S(2)}, u32[]{:S(2)}) %collective-permute-start.8) | collective-permute-done | bytes 262176 | tf_op jit(solution)/shard_map/ppermute | solution.py:359
  65.5 0.0 collective-permute-done.9.far_b
  65.5 0.2 pack.1
  65.7 0.0 copy-start.3
  65.7 1.3 copy-done.3
  67.0 0.0 all-to-all-done.refs_0_.refs_1_
  67.0 7.4 %all-to-all-start.1 = ((bf16[32,128,256]{2,1,0:T(8,128)(2,1)}), bf16[32,128,256]{2,1,0:T(8,128)(2,1)}, u32[]{:S(2)}, u32[]{:S(2)}) async-start(bf16[32,128,256]{2,1,0:T(8,128)(2,1)} %copy-done.3), calls=%async_computation.1 | async-start | bytes 4194304 | tf_op jit(solution)/shard_map/all_to_all | solution.py:365
  74.5 0.9 take.4
  75.4 0.0 copy-start
  75.4 3.0 %collective-permute-start.4 = (bf16[32,64,256]{2,1,0:T(8,128)(2,1)S(1)}, bf16[32,64,256]{2,1,0:T(8,128)(2,1)S(1)}, u32[]{:S(2)}, u32[]{:S(2)}) collective-permute-start(bf16[32,64,256]{2,1,0:T(8,128)(2,1)S(1)} %get-tuple-element.22.refs_1_), channel_id=1, source_target_pairs={{0,96},{32,0},{64,32},{96,64},{1,97},{33,1},{65,33},{97,65},{2,98}... | collective-permute-start | bytes 3145736 | tf_op jit(solution)/shard_map/ppermute | solution.py:362
  78.3 0.0 collective-permute-start.5
  78.4 0.0 collective-permute-start.2
  78.4 3.3 %collective-permute-start.3 = (bf16[32,32,256]{2,1,0:T(8,128)(2,1)}, bf16[32,32,256]{2,1,0:T(8,128)(2,1)}, u32[]{:S(2)}, u32[]{:S(2)}) collective-permute-start(bf16[32,32,256]{2,1,0:T(8,128)(2,1)} %get-tuple-element.21.refs_1_), channel_id=1, source_target_pairs={{0,96},{32,0},{64,32},{96,64},{1,97},{33,1},{65,33},{97,65},{2,98}... | collective-permute-start | bytes 1572872 | tf_op jit(solution)/shard_map/ppermute | solution.py:362
  81.6 20.3 %collective-permute-done.4.refs_2_.refs_1_ = bf16[32,64,256]{2,1,0:T(8,128)(2,1)S(1)} collective-permute-done((bf16[32,64,256]{2,1,0:T(8,128)(2,1)S(1)}, bf16[32,64,256]{2,1,0:T(8,128)(2,1)S(1)}, u32[]{:S(2)}, u32[]{:S(2)}) %collective-permute-start.4) | collective-permute-done | bytes 1048608 | tf_op jit(solution)/shard_map/ppermute | solution.py:362
  101.9 0.0 copy-start.1
  101.9 3.7 %collective-permute-done.5.refs_3_.refs_0_ = bf16[32,64,256]{2,1,0:T(8,128)(2,1)S(1)} collective-permute-done((bf16[32,64,256]{2,1,0:T(8,128)(2,1)S(1)}, bf16[32,64,256]{2,1,0:T(8,128)(2,1)S(1)}, u32[]{:S(2)}, u32[]{:S(2)}) %collective-permute-start.5) | collective-permute-done | bytes 1048608 | tf_op jit(solution)/shard_map/ppermute | solution.py:359
  105.6 0.0 copy-start.2
  105.6 1.1 take.7
  106.7 0.0 collective-permute-start.13
  106.7 3.2 %collective-permute-start.12 = (bf16[32,32,256]{2,1,0:T(8,128)(2,1)}, bf16[32,32,256]{2,1,0:T(8,128)(2,1)}, u32[]{:S(2)}, u32[]{:S(2)}) collective-permute-start(bf16[32,32,256]{2,1,0:T(8,128)(2,1)} %get-tuple-element.27), channel_id=1, source_target_pairs={{0,96},{32,0},{64,32},{96,64},{1,97},{33,1},{65,33},{97,65},{2,98}... | collective-permute-start | bytes 1572872 | tf_op jit(solution)/shard_map/ppermute | solution.py:362
  110.0 0.0 all-to-all-done.1.refs_1_.refs_2_.refs_3_.refs_4_
  110.0 3.8 %correlate.7.refs_4_ = f32[4,4,256,1024]{3,2,1,0:T(8,128)} custom-call(s32[1]{0:T(128)} %bitcast.refs_0_, bf16[32,128,256]{2,1,0:T(8,128)(2,1)} %all-to-all-done.1.refs_1_.refs_2_.refs_3_.refs_4_, bf16[32,128,256]{2,1,0:T(8,128)(2,1)} %all-to-all-done.1.refs_1_.refs_2_.refs_3_.refs_4_, bf16[32,128,256]{2,1,0:T(8,128)(2,1)} %all-to-all-done.1.refs_1_.refs_2_.refs_3_.refs_4_, ...), custom_call_target="tpu_custom_call" | custom-call | flops 640000000 | bytes 6291456 | tf_op jit(solution)/shard_map/correlate/pallas_call | solution.py:338
  113.8 0.0 copy-done
  113.8 0.0 copy-done.1
  113.8 0.0 copy-done.2
  113.8 3.6 %correlate.8.refs_2_.refs_4_ = f32[4,4,256,1024]{3,2,1,0:T(8,128)} custom-call(s32[1]{0:T(128)} %bitcast.refs_0_, bf16[32,64,256]{2,1,0:T(8,128)(2,1)} %copy-done, bf16[32,64,256]{2,1,0:T(8,128)(2,1)} %copy-done.1, bf16[32,64,256]{2,1,0:T(8,128)(2,1)} %copy-done.2, f32[4,4,256,1024]{3,2,1,0:T(8,128)} %correlate.7.refs_4_), custom_call_target="tpu_custom_call", output_to_operand_aliasing={{}: (4, {})} | custom-call | flops 480000000 | bytes 6291456 | tf_op jit(solution)/shard_map/correlate/pallas_call | solution.py:338
  117.4 0.0 collective-permute-done.2.refs_0_.refs_3_
  117.4 0.0 collective-permute-done.3.refs_1_.refs_2_
  117.4 1.1 take.6
  118.5 0.1 collective-permute-start.10
  118.6 3.2 %collective-permute-start.11 = (bf16[16,32,256]{2,1,0:T(8,128)(2,1)S(1)}, bf16[16,32,256]{2,1,0:T(8,128)(2,1)S(1)}, u32[]{:S(2)}, u32[]{:S(2)}) collective-permute-start(bf16[16,32,256]{2,1,0:T(8,128)(2,1)S(1)} %get-tuple-element.26), channel_id=1, source_target_pairs={{0,96},{32,0},{64,32},{96,64},{1,97},{33,1},{65,33},{97,65},{2,98}... | collective-permute-start | bytes 786440 | tf_op jit(solution)/shard_map/ppermute | solution.py:362
  121.8 3.6 %correlate.9.refs_4_ = f32[4,4,256,1024]{3,2,1,0:T(8,128)} custom-call(s32[1]{0:T(128)} %bitcast.refs_0_, bf16[32,64,256]{2,1,0:T(8,128)(2,1)} %copy-done, bf16[32,64,256]{2,1,0:T(8,128)(2,1)} %copy-done.1, bf16[32,64,256]{2,1,0:T(8,128)(2,1)} %copy-done.2, f32[4,4,256,1024]{3,2,1,0:T(8,128)} %correlate.8.refs_2_.refs_4_), custom_call_target="tpu_custom_call", output_to_operand_aliasing={{}: (4, {})} | custom-call | flops 480000000 | bytes 6291456 | tf_op jit(solution)/shard_map/correlate/pallas_call | solution.py:338
  125.4 3.6 %correlate.10.refs_3_ = f32[4,4,256,1024]{3,2,1,0:T(8,128)} custom-call(s32[1]{0:T(128)} %bitcast.refs_0_, bf16[32,32,256]{2,1,0:T(8,128)(2,1)} %get-tuple-element.21.refs_1_, bf16[32,32,256]{2,1,0:T(8,128)(2,1)} %collective-permute-done.3.refs_1_.refs_2_, ...), custom_call_target="tpu_custom_call", output_to_operand_aliasing={{}: (4, {})} | custom-call | flops 480000000 | bytes 6291456 | tf_op jit(solution)/shard_map/correlate/pallas_call | solution.py:338
  129.0 0.0 collective-permute-done.13.refs_2_
  129.0 2.5 %correlate.11.refs_3_ = f32[4,4,256,1024]{3,2,1,0:T(8,128)} custom-call(s32[1]{0:T(128)} %bitcast.refs_0_, bf16[32,64,256]{2,1,0:T(8,128)(2,1)} %copy-done, bf16[32,32,256]{2,1,0:T(8,128)(2,1)} %collective-permute-done.13.refs_2_, f32[4,4,256,1024]{3,2,1,0:T(8,128)} %correlate.10.refs_3_), custom_call_target="tpu_custom_call", output_to_operand_aliasing={{}: (3, {})} | custom-call | flops 160000000 | bytes 6291456 | tf_op jit(solution)/shard_map/correlate/pallas_call | solution.py:338
  131.5 0.0 collective-permute-done.12.refs_2_
  131.5 2.5 %correlate.12.refs_4_ = f32[4,4,256,1024]{3,2,1,0:T(8,128)} custom-call(s32[1]{0:T(128)} %bitcast.refs_0_, bf16[32,64,256]{2,1,0:T(8,128)(2,1)} %copy-done, bf16[32,32,256]{2,1,0:T(8,128)(2,1)} %collective-permute-done.12.refs_2_, f32[4,4,256,1024]{3,2,1,0:T(8,128)} %correlate.11.refs_3_), custom_call_target="tpu_custom_call", output_to_operand_aliasing={{}: (3, {})} | custom-call | flops 160000000 | bytes 6291456 | tf_op jit(solution)/shard_map/correlate/pallas_call | solution.py:338
  134.0 0.0 collective-permute-done.10.refs_2_
  134.0 0.0 collective-permute-done.11.refs_3_
  134.0 0.7 copy-done.7
  134.7 0.7 copy-done.8
  135.4 2.5 %correlate.13 = f32[4,4,256,1024]{3,2,1,0:T(8,128)} custom-call(s32[1]{0:T(128)} %bitcast.refs_0_, bf16[32,32,256]{2,1,0:T(8,128)(2,1)} %get-tuple-element.21.refs_1_, bf16[16,32,256]{2,1,0:T(8,128)(2,1)} %copy-done.7, bf16[16,32,256]{2,1,0:T(8,128)(2,1)} %copy-done.8, f32[4,4,256,1024]{3,2,1,0:T(8,128)} %correlate.12.refs_4_), custom_call_target="tpu_custom_call", output_to_operand_aliasing={{}: (4, {})} | custom-call | flops 160000000 | bytes 6291456 | tf_op jit(solution)/shard_map/correlate/pallas_call | solution.py:338
  (3 shorter events, 0.0 us)
Async XLA Ops:
  0.0 0.8 copy-start.4
  0.8 1.4 %copy-start.6 = (bf16[256,3072]{1,0:T(8,128)(2,1)S(1)}, bf16[256,3072]{1,0:T(8,128)(2,1)}, u32[]{:S(2)}) copy-start(bf16[256,3072]{1,0:T(8,128)(2,1)} %constant.10.clone.refs_2_) | copy-start | bytes 4718596
  2.2 15.0 %copy-start.5 = (f32[4,2048]{1,0:T(4,128)S(1)}, f32[4,2048]{1,0:T(4,128)}, u32[]{:S(2)}) copy-start(f32[4,2048]{1,0:T(4,128)} %refs_1_.5) | copy-start | bytes 98308
  6.7 22.1 %collective-permute-start = (bf16[12,256,128]{2,1,0:T(8,128)(2,1)S(1)}, bf16[12,256,128]{2,1,0:T(8,128)(2,1)S(1)}, u32[]{:S(2)}, u32[]{:S(2)}) collective-permute-start(bf16[12,256,128]{2,1,0:T(8,128)(2,1)S(1)} %spectra.4), channel_id=1, source_target_pairs={{0,1},{1,2},{2,3},{3,4},{4,5},{5,6},{6,7},{7,8},{8,9},{9,10},{10,1... | collective-permute-start | bytes 2359304 | tf_op jit(solution)/shard_map/ppermute | solution.py:370
  13.2 17.4 %collective-permute-start.1 = (bf16[12,256,128]{2,1,0:T(8,128)(2,1)S(1)}, bf16[12,256,128]{2,1,0:T(8,128)(2,1)S(1)}, u32[]{:S(2)}, u32[]{:S(2)}) collective-permute-start(bf16[12,256,128]{2,1,0:T(8,128)(2,1)S(1)} %spectra.5), channel_id=1, source_target_pairs={{0,1},{1,2},{2,3},{3,4},{4,5},{5,6},{6,7},{7,8},{8,9},{9,10},{10,1... | collective-permute-start | bytes 2359304 | tf_op jit(solution)/shard_map/ppermute | solution.py:370
  32.6 34.4 %all-to-all-start = ((bf16[32,96,256]{2,1,0:T(8,128)(2,1)}), bf16[32,96,256]{2,1,0:T(8,128)(2,1)S(1)}, u32[]{:S(2)}, u32[]{:S(2)}) async-start(bf16[32,96,256]{2,1,0:T(8,128)(2,1)} %combine.3), calls=%async_computation | async-start | bytes 3145728 | tf_op jit(solution)/shard_map/all_to_all | solution.py:365
  39.0 14.6 %collective-permute-start.6 = (bf16[32,32,256]{2,1,0:T(8,128)(2,1)S(1)}, bf16[32,32,256]{2,1,0:T(8,128)(2,1)S(1)}, u32[]{:S(2)}, u32[]{:S(2)}) collective-permute-start(bf16[32,32,256]{2,1,0:T(8,128)(2,1)S(1)} %combine.2.refs_5_.own), channel_id=1, source_target_pairs={{0,96},{32,0},{64,32},{96,64},{1,97},{33,1},{65,33},{97,65},{2,98}... | collective-permute-start | bytes 1572872 | tf_op jit(solution)/shard_map/ppermute | solution.py:362
  42.1 14.9 %collective-permute-start.7 = (bf16[32,32,256]{2,1,0:T(8,128)(2,1)S(1)}, bf16[32,32,256]{2,1,0:T(8,128)(2,1)S(1)}, u32[]{:S(2)}, u32[]{:S(2)}) collective-permute-start(bf16[32,32,256]{2,1,0:T(8,128)(2,1)S(1)} %combine.2.refs_5_.own), channel_id=1, source_target_pairs={{0,32},{32,64},{64,96},{96,0},{1,33},{33,65},{65,97},{97,1},{2,34}... | collective-permute-start | bytes 1572872 | tf_op jit(solution)/shard_map/ppermute | solution.py:359
  57.0 8.5 %collective-permute-start.8 = (bf16[16,32,256]{2,1,0:T(8,128)(2,1)S(1)}, bf16[16,32,256]{2,1,0:T(8,128)(2,1)S(1)}, u32[]{:S(2)}, u32[]{:S(2)}) collective-permute-start(bf16[16,32,256]{2,1,0:T(8,128)(2,1)S(1)} %get-tuple-element.23), channel_id=1, source_target_pairs={{0,32},{32,64},{64,96},{96,0},{1,33},{33,65},{65,97},{97,1},{2,34}... | collective-permute-start | bytes 786440 | tf_op jit(solution)/shard_map/ppermute | solution.py:359
  57.1 8.4 %collective-permute-start.9 = (bf16[16,32,256]{2,1,0:T(8,128)(2,1)S(1)}, bf16[16,32,256]{2,1,0:T(8,128)(2,1)S(1)}, u32[]{:S(2)}, u32[]{:S(2)}) collective-permute-start(bf16[16,32,256]{2,1,0:T(8,128)(2,1)S(1)} %get-tuple-element.24), channel_id=1, source_target_pairs={{0,96},{32,0},{64,32},{96,64},{1,97},{33,1},{65,33},{97,65},{2,98}... | collective-permute-start | bytes 786440 | tf_op jit(solution)/shard_map/ppermute | solution.py:362
  65.7 1.3 copy-start.3
  67.0 43.0 %all-to-all-start.1 = ((bf16[32,128,256]{2,1,0:T(8,128)(2,1)}), bf16[32,128,256]{2,1,0:T(8,128)(2,1)}, u32[]{:S(2)}, u32[]{:S(2)}) async-start(bf16[32,128,256]{2,1,0:T(8,128)(2,1)} %copy-done.3), calls=%async_computation.1 | async-start | bytes 4194304 | tf_op jit(solution)/shard_map/all_to_all | solution.py:365
  75.4 38.4 %copy-start = (bf16[32,64,256]{2,1,0:T(8,128)(2,1)}, bf16[32,64,256]{2,1,0:T(8,128)(2,1)S(1)}, u32[]{:S(2)}) copy-start(bf16[32,64,256]{2,1,0:T(8,128)(2,1)S(1)} %get-tuple-element.22.refs_1_) | copy-start | bytes 3145732
  75.4 26.5 %collective-permute-start.4 = (bf16[32,64,256]{2,1,0:T(8,128)(2,1)S(1)}, bf16[32,64,256]{2,1,0:T(8,128)(2,1)S(1)}, u32[]{:S(2)}, u32[]{:S(2)}) collective-permute-start(bf16[32,64,256]{2,1,0:T(8,128)(2,1)S(1)} %get-tuple-element.22.refs_1_), channel_id=1, source_target_pairs={{0,96},{32,0},{64,32},{96,64},{1,97},{33,1},{65,33},{97,65},{2,98}... | collective-permute-start | bytes 3145736 | tf_op jit(solution)/shard_map/ppermute | solution.py:362
  78.3 27.3 %collective-permute-start.5 = (bf16[32,64,256]{2,1,0:T(8,128)(2,1)S(1)}, bf16[32,64,256]{2,1,0:T(8,128)(2,1)S(1)}, u32[]{:S(2)}, u32[]{:S(2)}) collective-permute-start(bf16[32,64,256]{2,1,0:T(8,128)(2,1)S(1)} %get-tuple-element.22.refs_1_), channel_id=1, source_target_pairs={{0,32},{32,64},{64,96},{96,0},{1,33},{33,65},{65,97},{97,1},{2,34}... | collective-permute-start | bytes 3145736 | tf_op jit(solution)/shard_map/ppermute | solution.py:359
  78.4 39.1 %collective-permute-start.2 = (bf16[32,32,256]{2,1,0:T(8,128)(2,1)}, bf16[32,32,256]{2,1,0:T(8,128)(2,1)}, u32[]{:S(2)}, u32[]{:S(2)}) collective-permute-start(bf16[32,32,256]{2,1,0:T(8,128)(2,1)} %get-tuple-element.21.refs_1_), channel_id=1, source_target_pairs={{0,32},{32,64},{64,96},{96,0},{1,33},{33,65},{65,97},{97,1},{2,34}... | collective-permute-start | bytes 1572872 | tf_op jit(solution)/shard_map/ppermute | solution.py:359
  78.4 39.1 %collective-permute-start.3 = (bf16[32,32,256]{2,1,0:T(8,128)(2,1)}, bf16[32,32,256]{2,1,0:T(8,128)(2,1)}, u32[]{:S(2)}, u32[]{:S(2)}) collective-permute-start(bf16[32,32,256]{2,1,0:T(8,128)(2,1)} %get-tuple-element.21.refs_1_), channel_id=1, source_target_pairs={{0,96},{32,0},{64,32},{96,64},{1,97},{33,1},{65,33},{97,65},{2,98}... | collective-permute-start | bytes 1572872 | tf_op jit(solution)/shard_map/ppermute | solution.py:362
  101.9 11.9 %copy-start.1 = (bf16[32,64,256]{2,1,0:T(8,128)(2,1)}, bf16[32,64,256]{2,1,0:T(8,128)(2,1)S(1)}, u32[]{:S(2)}) copy-start(bf16[32,64,256]{2,1,0:T(8,128)(2,1)S(1)} %collective-permute-done.4.refs_2_.refs_1_) | copy-start | bytes 3145732
  105.6 8.2 %copy-start.2 = (bf16[32,64,256]{2,1,0:T(8,128)(2,1)}, bf16[32,64,256]{2,1,0:T(8,128)(2,1)S(1)}, u32[]{:S(2)}) copy-start(bf16[32,64,256]{2,1,0:T(8,128)(2,1)S(1)} %collective-permute-done.5.refs_3_.refs_0_) | copy-start | bytes 3145732
  106.7 22.3 %collective-permute-start.13 = (bf16[32,32,256]{2,1,0:T(8,128)(2,1)}, bf16[32,32,256]{2,1,0:T(8,128)(2,1)}, u32[]{:S(2)}, u32[]{:S(2)}) collective-permute-start(bf16[32,32,256]{2,1,0:T(8,128)(2,1)} %get-tuple-element.28), channel_id=1, source_target_pairs={{0,32},{32,64},{64,96},{96,0},{1,33},{33,65},{65,97},{97,1},{2,34}... | collective-permute-start | bytes 1572872 | tf_op jit(solution)/shard_map/ppermute | solution.py:359
  106.7 24.8 %collective-permute-start.12 = (bf16[32,32,256]{2,1,0:T(8,128)(2,1)}, bf16[32,32,256]{2,1,0:T(8,128)(2,1)}, u32[]{:S(2)}, u32[]{:S(2)}) collective-permute-start(bf16[32,32,256]{2,1,0:T(8,128)(2,1)} %get-tuple-element.27), channel_id=1, source_target_pairs={{0,96},{32,0},{64,32},{96,64},{1,97},{33,1},{65,33},{97,65},{2,98}... | collective-permute-start | bytes 1572872 | tf_op jit(solution)/shard_map/ppermute | solution.py:362
  118.5 15.5 %collective-permute-start.10 = (bf16[16,32,256]{2,1,0:T(8,128)(2,1)S(1)}, bf16[16,32,256]{2,1,0:T(8,128)(2,1)S(1)}, u32[]{:S(2)}, u32[]{:S(2)}) collective-permute-start(bf16[16,32,256]{2,1,0:T(8,128)(2,1)S(1)} %get-tuple-element.25), channel_id=1, source_target_pairs={{0,32},{32,64},{64,96},{96,0},{1,33},{33,65},{65,97},{97,1},{2,34}... | collective-permute-start | bytes 786440 | tf_op jit(solution)/shard_map/ppermute | solution.py:359
  118.6 15.4 %collective-permute-start.11 = (bf16[16,32,256]{2,1,0:T(8,128)(2,1)S(1)}, bf16[16,32,256]{2,1,0:T(8,128)(2,1)S(1)}, u32[]{:S(2)}, u32[]{:S(2)}) collective-permute-start(bf16[16,32,256]{2,1,0:T(8,128)(2,1)S(1)} %get-tuple-element.26), channel_id=1, source_target_pairs={{0,96},{32,0},{64,32},{96,64},{1,97},{33,1},{65,33},{97,65},{2,98}... | collective-permute-start | bytes 786440 | tf_op jit(solution)/shard_map/ppermute | solution.py:362
  134.0 0.7 copy-start.7
  134.7 0.7 copy-start.8

commit v4 on v3

--- a/solution.py
+++ b/solution.py
@@ -17,6 +17,7 @@
 ROWS = 256
 LANES = 256
 VMEM = 48 * 1024 * 1024
+LARGE = 60 * 1024 * 1024
 
 
 def halves(x):
@@ -301,7 +302,7 @@
                     out[i, 0] = value
 
 
-def correlate(place, b, own, others, before, whole, base=0, after=()):
+def correlate(place, b, own, others, before, whole, base=0, after=(), room=VMEM):
     def spec(array, step):
         row = {32: 0, 64: base, 128: step}[array.shape[1]]
         return pl.BlockSpec((array.shape[0], 16, LANES), lambda g, *rest: (0, 2 * row + g, 0))
@@ -342,10 +343,51 @@
             num_scalar_prefetch=1, grid=grid, in_specs=in_specs, out_specs=out_spec
         ),
         input_output_aliases=aliases,
-        compiler_params=pltpu.CompilerParams(vmem_limit_bytes=60 * 1024 * 1024),
+        compiler_params=pltpu.CompilerParams(vmem_limit_bytes=room),
         cost_estimate=pl.CostEstimate(flops=len(steps) * 160000000, bytes_accessed=6 << 20, transcendentals=0),
         name="correlate",
     )(*args)
+
+
+def far_kernel(place, own, first, second, _, out):
+    y = place[0]
+    ids = lax.broadcasted_iota(jnp.int32, (8, 1), 0)
+    sign = jnp.where(ids < 4, 1.0, -1.0)
+
+    def pair(x):
+        return x.astype(F32).reshape(x.shape[0], 2, 8, LANES)
+
+    def flat(x):
+        return x.reshape(x.shape[0] * 8, LANES).astype(BF16)
+
+    mine = pair(own[...])
+    other = pair(jnp.where(pl.program_id(0) == 0, first[...], second[...]))
+    for i in range(2):
+        p = mine[:, i]
+        plane = jnp.where(lax.rem(y + 2, 4) < y, pltpu.roll(p, 4, 1) * sign, p)
+        out[i, 0] = jnp.dot(flat(plane).T, flat(other[:, i]), preferred_element_type=F32) * (1.0 / 128)
+
+
+def correlate_far(place, own, first, second, before):
+    part = (32, 16, LANES)
+    in_specs = [
+        pl.BlockSpec(part, lambda k, g, y: (0, 2 * k + g, 0)),
+        pl.BlockSpec(part, lambda k, g, y: (0, g, 0)),
+        pl.BlockSpec(part, lambda k, g, y: (0, g, 0)),
+        pl.BlockSpec(memory_space=pltpu.HBM),
+    ]
+    out_spec = pl.BlockSpec((2, 1, ROWS, 256), lambda k, g, y: (g, 1 + 2 * k, 0, lax.rem(y[0] + 2, 4)))
+    return pl.pallas_call(
+        far_kernel,
+        out_shape=jax.ShapeDtypeStruct((4, 4, ROWS, 1024), F32),
+        grid_spec=pltpu.PrefetchScalarGridSpec(
+            num_scalar_prefetch=1, grid=(2, 2), in_specs=in_specs, out_specs=out_spec
+        ),
+        input_output_aliases={4: 0},
+        compiler_params=pltpu.CompilerParams(vmem_limit_bytes=VMEM),
+        cost_estimate=pl.CostEstimate(flops=320000000, bytes_accessed=6 << 20, transcendentals=0),
+        name="correlate_far",
+    )(place, own, first, second, before)
 
 
 def body(v, window):
@@ -386,14 +428,13 @@
     first, second = take([(odd_left, whole, (0, 0, 0)), (odd_right, whole, (0, 1, 0))])
     odd_far = up(first), down(second)
     near = {0: [], 1: [odd_right], 3: [odd_left]}
-    out = correlate(place, 0, early, {0: [], 1: [early], 2: [early], 3: [early]}, None, True)
-    out = correlate(place, 1, odd, near, out, True, 0)
+    out = correlate(place, 0, early, {0: [], 1: [early], 2: [early], 3: [early]}, None, True, room=LARGE)
+    out = correlate(place, 1, odd, near, out, True, 0, room=LARGE)
     first, second = take([(even_left, half, lower), (even_right, half, upper)], (out,))
     even_far = [up(first), down(second)]
     out = correlate(place, 3, odd, near, out, True, 1)
     out = correlate(place, 2, even, {0: [], 1: [even_right], 3: [even_left]}, out, True)
-    for k in range(2):
-        out = correlate(place, 2 * k + 1, odd, {2: [odd_far[k]]}, out, False, k)
+    out = correlate_far(place, odd, *odd_far, out)
     out = correlate(place, 2, even, {2: even_far}, out, False)
     return out.reshape(16, ROWS, 1024)
 

time: 138 us -> 135 us (0.978)
  Pallas kernels: 48.2 us -> 44.8 us
    pallas_call x7 -> x5, Pallas kernels: 22 us -> 15.1 us  [correlate(): pl.pallas_call(kernel, out_shape=jax.ShapeDtypeStruct((4, 4, ROWS, 1024),...]
    pallas_call x0 -> x1, Pallas kernels: none -> 4.38 us  [correlate_far(): pl.pallas_call(far_kernel, out_shape=jax.ShapeDtypeStruct((4, 4, ROWS, 10...]
    unnamed x18 -> x20, local copies, waits for them, and re-layouts: 4.9 us -> 4.52 us
  transfers between devices with their start and end apart: 16 -> 16, of which waited for: 6 -> 6; matrix products, arithmetic and copies ran while one was open for 0% -> 0% of each run, Pallas kernels for 28% -> 27%
where the time goes in v4:
time: 135 us; the launch traced here: 134 us
  waiting for transfers between devices  45.8 us (34%)
  Pallas kernels  44.8 us (33%)
  starting transfers between devices  38.8 us (29%)
  local copies, waits for them, and re-layouts  4.52 us (3%)
    ppermute x6, waiting for transfers between devices, down(): return lax.ppermute(x, 'inp', [(i, (i - 1) % ring) for i in range(ring)])  31.8 us
    pallas_call x3, Pallas kernels, spectra(): pl.pallas_call(kernel, out_shape=[jax.ShapeDtypeStruct((n * len(g), 256,...  20.8 us
    ppermute x6, starting transfers between devices, down(): return lax.ppermute(x, 'inp', [(i, (i - 1) % ring) for i in range(ring)])  19 us
    pallas_call x5, Pallas kernels, correlate(): pl.pallas_call(kernel, out_shape=jax.ShapeDtypeStruct((4, 4, ROWS, 1024),...  15.1 us
    all_to_all x2, starting transfers between devices, swap(): return lax.all_to_all(x, 'tm', split_axis=0, concat_axis=0, tiled=True)  13.8 us
    ppermute x6, waiting for transfers between devices, up(): return lax.ppermute(x, 'inp', [(i, (i + 1) % ring) for i in range(ring)])  12.3 us
    ppermute x2, starting transfers between devices, body(): halo.append(lax.ppermute(passed, 'tm', later))  5.85 us
    unnamed x20, local copies, waits for them, and re-layouts  4.52 us
  transfers between devices with their start and end apart: 16, of which 6 were waited for; matrix products, arithmetic and copies ran while one was open for 0% of the time, Pallas kernels for 27%

profile of v4, /device:TPU:2, one launch (start us, length us, event | category | flops | bytes accessed | tf_op | source)
XLA Modules:
  0.0 134.1 jit_solution(13813802983233877953)
XLA Ops:
  0.0 0.0 copy-start.7
  0.0 0.8 copy-done.7
  0.8 0.0 copy-start.9
  0.8 1.4 %copy-done.9 = bf16[256,3072]{1,0:T(8,128)(2,1)S(1)} copy-done((bf16[256,3072]{1,0:T(8,128)(2,1)S(1)}, bf16[256,3072]{1,0:T(8,128)(2,1)}, u32[]{:S(2)}) %copy-start.9) | copy-done | bytes 1572888
  2.2 4.5 %spectra.4 = bf16[12,256,128]{2,1,0:T(8,128)(2,1)S(1)} custom-call(bf16[256,4,2048]{2,1,0:T(4,128)(2,1)} %refs_0_.5, f32[4,2048]{1,0:T(4,128)S(1)} %copy-done.7, bf16[256,3072]{1,0:T(8,128)(2,1)S(1)} %copy-done.9), custom_call_target="tpu_custom_call" | custom-call | flops 3600000000 | bytes 12582912 | tf_op jit(solution)/shard_map/spectra/pallas_call | solution.py:139
  6.7 0.0 copy-start.8
  6.7 1.9 %collective-permute-start = (bf16[12,256,128]{2,1,0:T(8,128)(2,1)S(1)}, bf16[12,256,128]{2,1,0:T(8,128)(2,1)S(1)}, u32[]{:S(2)}, u32[]{:S(2)}) collective-permute-start(bf16[12,256,128]{2,1,0:T(8,128)(2,1)S(1)} %spectra.4), channel_id=1, source_target_pairs={{0,1},{1,2},{2,3},{3,4},{4,5},{5,6},{6,7},{7,8},{8,9},{9,10},{10,1... | collective-permute-start | bytes 2359304 | tf_op jit(solution)/shard_map/ppermute | solution.py:412
  8.7 4.5 %spectra.5 = bf16[12,256,128]{2,1,0:T(8,128)(2,1)S(1)} custom-call(bf16[256,4,2048]{2,1,0:T(4,128)(2,1)} %refs_0_.5, f32[4,2048]{1,0:T(4,128)S(1)} %copy-done.7, bf16[256,3072]{1,0:T(8,128)(2,1)S(1)} %copy-done.9), custom_call_target="tpu_custom_call" | custom-call | flops 3600000000 | bytes 12582912 | tf_op jit(solution)/shard_map/spectra/pallas_call | solution.py:139
  13.2 3.9 %collective-permute-start.1 = (bf16[12,256,128]{2,1,0:T(8,128)(2,1)S(1)}, bf16[12,256,128]{2,1,0:T(8,128)(2,1)S(1)}, u32[]{:S(2)}, u32[]{:S(2)}) collective-permute-start(bf16[12,256,128]{2,1,0:T(8,128)(2,1)S(1)} %spectra.5), channel_id=1, source_target_pairs={{0,1},{1,2},{2,3},{3,4},{4,5},{5,6},{6,7},{7,8},{8,9},{9,10},{10,1... | collective-permute-start | bytes 2359304 | tf_op jit(solution)/shard_map/ppermute | solution.py:412
  17.1 0.0 copy-done.8
  17.2 11.7 %spectra.3 = (f32[4,256,256]{2,1,0:T(8,128)S(1)}, f32[4,256,256]{2,1,0:T(8,128)S(1)}, f32[4,256,256]{2,1,0:T(8,128)S(1)}, f32[4,256,256]{2,1,0:T(8,128)S(1)}) custom-call(bf16[256,4,2048]{2,1,0:T(4,128)(2,1)} %refs_0_.5, f32[4,2048]{1,0:T(4,128)S(1)} %copy-done.8, bf16[256,3072]{1,0:T(8,128)(2,1)S(1)} %copy-done.9, bf16[256,3072]{1,0:T(8,128)(2,1)} %constant.11.clone.refs_3_), custom_call_target="tpu_custom_call" | custom-call | flops 4800000000 | bytes 12582912 | tf_op jit(solution)/shard_map/spectra/pallas_call | solution.py:139
  28.9 0.0 collective-permute-done.refs_1_.refs_3_
  28.9 1.7 %collective-permute-done.1.refs_2_.refs_4_ = bf16[12,256,128]{2,1,0:T(8,128)(2,1)S(1)} collective-permute-done((bf16[12,256,128]{2,1,0:T(8,128)(2,1)S(1)}, bf16[12,256,128]{2,1,0:T(8,128)(2,1)S(1)}, u32[]{:S(2)}, u32[]{:S(2)}) %collective-permute-start.1) | collective-permute-done | bytes 786464 | tf_op jit(solution)/shard_map/ppermute | solution.py:412
  30.6 0.2 combine.2.refs_5_.own
  30.8 1.8 %combine.3 = bf16[32,96,256]{2,1,0:T(8,128)(2,1)} custom-call(f32[4,256,256]{2,1,0:T(8,128)S(1)} %get-tuple-element.17.refs_0_, f32[4,256,256]{2,1,0:T(8,128)S(1)} %get-tuple-element.18.refs_1_, f32[4,256,256]{2,1,0:T(8,128)S(1)} %get-tuple-element.19.refs_2_, bf16[12,256,128]{2,1,0:T(8,128)(2,1)S(1)} %collective-permute-done.refs_1_.refs_3_, ...), custom_call_target="tpu_custom_call" | custom-call | flops 3145728 | bytes 6291456 | tf_op jit(solution)/shard_map/combine/pallas_call | solution.py:182
  32.6 6.4 %all-to-all-start = ((bf16[32,96,256]{2,1,0:T(8,128)(2,1)}), bf16[32,96,256]{2,1,0:T(8,128)(2,1)S(1)}, u32[]{:S(2)}, u32[]{:S(2)}) async-start(bf16[32,96,256]{2,1,0:T(8,128)(2,1)} %combine.3), calls=%async_computation | async-start | bytes 3145728 | tf_op jit(solution)/shard_map/all_to_all | solution.py:407
  39.0 3.1 %collective-permute-start.6 = (bf16[32,32,256]{2,1,0:T(8,128)(2,1)S(1)}, bf16[32,32,256]{2,1,0:T(8,128)(2,1)S(1)}, u32[]{:S(2)}, u32[]{:S(2)}) collective-permute-start(bf16[32,32,256]{2,1,0:T(8,128)(2,1)S(1)} %combine.2.refs_5_.own), channel_id=1, source_target_pairs={{0,96},{32,0},{64,32},{96,64},{1,97},{33,1},{65,33},{97,65},{2,98}... | collective-permute-start | bytes 1572872 | tf_op jit(solution)/shard_map/ppermute | solution.py:404
  42.0 0.0 collective-permute-start.7
  42.0 11.5 %collective-permute-done.6.refs_1_.right = bf16[32,32,256]{2,1,0:T(8,128)(2,1)S(1)} collective-permute-done((bf16[32,32,256]{2,1,0:T(8,128)(2,1)S(1)}, bf16[32,32,256]{2,1,0:T(8,128)(2,1)S(1)}, u32[]{:S(2)}, u32[]{:S(2)}) %collective-permute-start.6) | collective-permute-done | bytes 524320 | tf_op jit(solution)/shard_map/ppermute | solution.py:404
  53.5 3.4 %collective-permute-done.7.refs_0_.left = bf16[32,32,256]{2,1,0:T(8,128)(2,1)S(1)} collective-permute-done((bf16[32,32,256]{2,1,0:T(8,128)(2,1)S(1)}, bf16[32,32,256]{2,1,0:T(8,128)(2,1)S(1)}, u32[]{:S(2)}, u32[]{:S(2)}) %collective-permute-start.7) | collective-permute-done | bytes 524320 | tf_op jit(solution)/shard_map/ppermute | solution.py:401
  57.0 0.1 collective-permute-start.8
  57.1 3.2 %collective-permute-start.9 = (bf16[16,32,256]{2,1,0:T(8,128)(2,1)S(1)}, bf16[16,32,256]{2,1,0:T(8,128)(2,1)S(1)}, u32[]{:S(2)}, u32[]{:S(2)}) collective-permute-start(bf16[16,32,256]{2,1,0:T(8,128)(2,1)S(1)} %get-tuple-element.24), channel_id=1, source_target_pairs={{0,96},{32,0},{64,32},{96,64},{1,97},{33,1},{65,33},{97,65},{2,98}... | collective-permute-start | bytes 786440 | tf_op jit(solution)/shard_map/ppermute | solution.py:404
  60.3 5.2 %collective-permute-done.8.far_a = bf16[16,32,256]{2,1,0:T(8,128)(2,1)S(1)} collective-permute-done((bf16[16,32,256]{2,1,0:T(8,128)(2,1)S(1)}, bf16[16,32,256]{2,1,0:T(8,128)(2,1)S(1)}, u32[]{:S(2)}, u32[]{:S(2)}) %collective-permute-start.8) | collective-permute-done | bytes 262176 | tf_op jit(solution)/shard_map/ppermute | solution.py:401
  65.5 0.0 collective-permute-done.9.far_b
  65.5 0.2 pack.1
  65.7 0.0 copy-start.6
  65.7 1.3 copy-done.6
  67.0 0.0 all-to-all-done.refs_0_.refs_1_
  67.0 7.4 %all-to-all-start.1 = ((bf16[32,128,256]{2,1,0:T(8,128)(2,1)}), bf16[32,128,256]{2,1,0:T(8,128)(2,1)}, u32[]{:S(2)}, u32[]{:S(2)}) async-start(bf16[32,128,256]{2,1,0:T(8,128)(2,1)} %copy-done.6), calls=%async_computation.1 | async-start | bytes 4194304 | tf_op jit(solution)/shard_map/all_to_all | solution.py:407
  74.5 0.1 take.4
  74.6 0.0 copy-start
  74.6 3.0 %collective-permute-start.4 = (bf16[32,64,256]{2,1,0:T(8,128)(2,1)S(1)}, bf16[32,64,256]{2,1,0:T(8,128)(2,1)S(1)}, u32[]{:S(2)}, u32[]{:S(2)}) collective-permute-start(bf16[32,64,256]{2,1,0:T(8,128)(2,1)S(1)} %get-tuple-element.22.refs_1_.own), channel_id=1, source_target_pairs={{0,96},{32,0},{64,32},{96,64},{1,97},{33,1},{65,33},{97,65},{2,98}... | collective-permute-start | bytes 3145736 | tf_op jit(solution)/shard_map/ppermute | solution.py:404
  77.6 0.0 collective-permute-start.5
  77.6 0.0 collective-permute-start.2
  77.6 3.3 %collective-permute-start.3 = (bf16[32,32,256]{2,1,0:T(8,128)(2,1)S(1)}, bf16[32,32,256]{2,1,0:T(8,128)(2,1)}, u32[]{:S(2)}, u32[]{:S(2)}) collective-permute-start(bf16[32,32,256]{2,1,0:T(8,128)(2,1)S(1)} %get-tuple-element.21.refs_1_), channel_id=1, source_target_pairs={{0,96},{32,0},{64,32},{96,64},{1,97},{33,1},{65,33},{97,65},{2,98}... | collective-permute-start | bytes 1572872 | tf_op jit(solution)/shard_map/ppermute | solution.py:404
  80.9 20.3 %collective-permute-done.4.refs_2_.refs_1_ = bf16[32,64,256]{2,1,0:T(8,128)(2,1)S(1)} collective-permute-done((bf16[32,64,256]{2,1,0:T(8,128)(2,1)S(1)}, bf16[32,64,256]{2,1,0:T(8,128)(2,1)S(1)}, u32[]{:S(2)}, u32[]{:S(2)}) %collective-permute-start.4) | collective-permute-done | bytes 1048608 | tf_op jit(solution)/shard_map/ppermute | solution.py:404
  101.1 0.0 copy-start.2
  101.1 3.7 %collective-permute-done.5.refs_3_.refs_0_ = bf16[32,64,256]{2,1,0:T(8,128)(2,1)S(1)} collective-permute-done((bf16[32,64,256]{2,1,0:T(8,128)(2,1)S(1)}, bf16[32,64,256]{2,1,0:T(8,128)(2,1)S(1)}, u32[]{:S(2)}, u32[]{:S(2)}) %collective-permute-start.5) | collective-permute-done | bytes 1048608 | tf_op jit(solution)/shard_map/ppermute | solution.py:401
  104.9 1.1 take.7
  105.9 0.0 copy-start.4
  105.9 1.0 copy-done.4
  106.9 0.0 collective-permute-start.12
  106.9 3.2 %collective-permute-start.13 = (bf16[32,32,256]{2,1,0:T(8,128)(2,1)}, bf16[32,32,256]{2,1,0:T(8,128)(2,1)}, u32[]{:S(2)}, u32[]{:S(2)}) collective-permute-start(bf16[32,32,256]{2,1,0:T(8,128)(2,1)} %get-tuple-element.28), channel_id=1, source_target_pairs={{0,96},{32,0},{64,32},{96,64},{1,97},{33,1},{65,33},{97,65},{2,98}... | collective-permute-start | bytes 1572872 | tf_op jit(solution)/shard_map/ppermute | solution.py:404
  110.2 0.0 all-to-all-done.1.refs_1_.refs_2_.refs_3_.refs_4_
  110.2 3.8 %correlate.5.refs_4_ = f32[4,4,256,1024]{3,2,1,0:T(8,128)} custom-call(s32[1]{0:T(128)} %bitcast.refs_0_.place, bf16[32,128,256]{2,1,0:T(8,128)(2,1)} %all-to-all-done.1.refs_1_.refs_2_.refs_3_.refs_4_, bf16[32,128,256]{2,1,0:T(8,128)(2,1)} %all-to-all-done.1.refs_1_.refs_2_.refs_3_.refs_4_, ...), custom_call_target="tpu_custom_call" | custom-call | flops 640000000 | bytes 6291456 | tf_op jit(solution)/shard_map/correlate/pallas_call | solution.py:339
  114.0 0.0 copy-done
  114.0 0.0 copy-done.2
  114.0 3.6 %correlate.6.refs_2_.refs_4_ = f32[4,4,256,1024]{3,2,1,0:T(8,128)} custom-call(s32[1]{0:T(128)} %bitcast.refs_0_.place, bf16[32,64,256]{2,1,0:T(8,128)(2,1)} %copy-done, bf16[32,64,256]{2,1,0:T(8,128)(2,1)} %copy-done.2, bf16[32,64,256]{2,1,0:T(8,128)(2,1)} %copy-done.4, f32[4,4,256,1024]{3,2,1,0:T(8,128)} %correlate.5.refs_4_), custom_call_target="tpu_custom_call", output_to_operand_aliasing={{}: (4, {})} | custom-call | flops 480000000 | bytes 6291456 | tf_op jit(solution)/shard_map/correlate/pallas_call | solution.py:339
  117.6 0.0 collective-permute-done.2.refs_0_.refs_3_
  117.6 0.0 collective-permute-done.3.refs_1_.refs_2_
  117.6 1.1 take.6
  118.8 0.1 collective-permute-start.10
  118.9 3.2 %collective-permute-start.11 = (bf16[16,32,256]{2,1,0:T(8,128)(2,1)S(1)}, bf16[16,32,256]{2,1,0:T(8,128)(2,1)S(1)}, u32[]{:S(2)}, u32[]{:S(2)}) collective-permute-start(bf16[16,32,256]{2,1,0:T(8,128)(2,1)S(1)} %get-tuple-element.26), channel_id=1, source_target_pairs={{0,96},{32,0},{64,32},{96,64},{1,97},{33,1},{65,33},{97,65},{2,98}... | collective-permute-start | bytes 786440 | tf_op jit(solution)/shard_map/ppermute | solution.py:404
  122.1 0.0 copy-done.1
  122.1 0.0 copy-done.3
  122.1 0.0 copy-done.5
  122.1 2.7 %correlate.7.refs_4_ = f32[4,4,256,1024]{3,2,1,0:T(8,128)} custom-call(s32[1]{0:T(128)} %bitcast.refs_0_.place, bf16[32,64,256]{2,1,0:T(8,128)(2,1)S(1)} %copy-done.1, bf16[32,64,256]{2,1,0:T(8,128)(2,1)S(1)} %copy-done.3, bf16[32,64,256]{2,1,0:T(8,128)(2,1)S(1)} %copy-done.5, ...), custom_call_target="tpu_custom_call", output_to_operand_aliasing={{}: (4, {})} | custom-call | flops 480000000 | bytes 6291456 | tf_op jit(solution)/shard_map/correlate/pallas_call | solution.py:339
  124.7 3.5 %correlate.8._ = f32[4,4,256,1024]{3,2,1,0:T(8,128)} custom-call(s32[1]{0:T(128)} %bitcast.refs_0_.place, bf16[32,32,256]{2,1,0:T(8,128)(2,1)S(1)} %get-tuple-element.21.refs_1_, bf16[32,32,256]{2,1,0:T(8,128)(2,1)} %collective-permute-done.3.refs_1_.refs_2_, ...), custom_call_target="tpu_custom_call", output_to_operand_aliasing={{}: (4, {})} | custom-call | flops 480000000 | bytes 6291456 | tf_op jit(solution)/shard_map/correlate/pallas_call | solution.py:339
  128.2 0.0 collective-permute-done.12.first
  128.2 0.0 collective-permute-done.13.second
  128.2 4.4 %correlate_far.1.refs_4_ = f32[4,4,256,1024]{3,2,1,0:T(8,128)} custom-call(s32[1]{0:T(128)} %bitcast.refs_0_.place, bf16[32,64,256]{2,1,0:T(8,128)(2,1)S(1)} %copy-done.1, bf16[32,32,256]{2,1,0:T(8,128)(2,1)} %collective-permute-done.12.first, bf16[32,32,256]{2,1,0:T(8,128)(2,1)} %collective-permute-done.13.second, ...), custom_call_target="tpu_custom_call", output_to_operand_aliasing={{}: (4, {})} | custom-call | flops 320000000 | bytes 6291456 | tf_op jit(solution)/shard_map/correlate_far/pallas_call | solution.py:380
  132.6 0.0 collective-permute-done.10.refs_2_
  132.6 0.0 collective-permute-done.11.refs_3_
  132.6 1.5 %correlate.9 = f32[4,4,256,1024]{3,2,1,0:T(8,128)} custom-call(s32[1]{0:T(128)} %bitcast.refs_0_.place, bf16[32,32,256]{2,1,0:T(8,128)(2,1)S(1)} %get-tuple-element.21.refs_1_, bf16[16,32,256]{2,1,0:T(8,128)(2,1)S(1)} %collective-permute-done.10.refs_2_, bf16[16,32,256]{2,1,0:T(8,128)(2,1)S(1)} %collective-permute-done.11.refs_3_, ...), custom_call_target="tpu_custom_call", output_to_operand_aliasing={{}: (4, {})} | custom-call | flops 160000000 | bytes 6291456 | tf_op jit(solution)/shard_map/correlate/pallas_call | solution.py:339
  (4 shorter events, 0.0 us)
Async XLA Ops:
  0.0 0.8 copy-start.7
  0.8 1.4 %copy-start.9 = (bf16[256,3072]{1,0:T(8,128)(2,1)S(1)}, bf16[256,3072]{1,0:T(8,128)(2,1)}, u32[]{:S(2)}) copy-start(bf16[256,3072]{1,0:T(8,128)(2,1)} %constant.10.clone.refs_2_) | copy-start | bytes 4718596
  6.7 10.4 %copy-start.8 = (f32[4,2048]{1,0:T(4,128)S(1)}, f32[4,2048]{1,0:T(4,128)}, u32[]{:S(2)}) copy-start(f32[4,2048]{1,0:T(4,128)} %refs_1_.5) | copy-start | bytes 98308
  6.7 22.1 %collective-permute-start = (bf16[12,256,128]{2,1,0:T(8,128)(2,1)S(1)}, bf16[12,256,128]{2,1,0:T(8,128)(2,1)S(1)}, u32[]{:S(2)}, u32[]{:S(2)}) collective-permute-start(bf16[12,256,128]{2,1,0:T(8,128)(2,1)S(1)} %spectra.4), channel_id=1, source_target_pairs={{0,1},{1,2},{2,3},{3,4},{4,5},{5,6},{6,7},{7,8},{8,9},{9,10},{10,1... | collective-permute-start | bytes 2359304 | tf_op jit(solution)/shard_map/ppermute | solution.py:412
  13.2 17.4 %collective-permute-start.1 = (bf16[12,256,128]{2,1,0:T(8,128)(2,1)S(1)}, bf16[12,256,128]{2,1,0:T(8,128)(2,1)S(1)}, u32[]{:S(2)}, u32[]{:S(2)}) collective-permute-start(bf16[12,256,128]{2,1,0:T(8,128)(2,1)S(1)} %spectra.5), channel_id=1, source_target_pairs={{0,1},{1,2},{2,3},{3,4},{4,5},{5,6},{6,7},{7,8},{8,9},{9,10},{10,1... | collective-permute-start | bytes 2359304 | tf_op jit(solution)/shard_map/ppermute | solution.py:412
  32.6 34.4 %all-to-all-start = ((bf16[32,96,256]{2,1,0:T(8,128)(2,1)}), bf16[32,96,256]{2,1,0:T(8,128)(2,1)S(1)}, u32[]{:S(2)}, u32[]{:S(2)}) async-start(bf16[32,96,256]{2,1,0:T(8,128)(2,1)} %combine.3), calls=%async_computation | async-start | bytes 3145728 | tf_op jit(solution)/shard_map/all_to_all | solution.py:407
  39.0 14.6 %collective-permute-start.6 = (bf16[32,32,256]{2,1,0:T(8,128)(2,1)S(1)}, bf16[32,32,256]{2,1,0:T(8,128)(2,1)S(1)}, u32[]{:S(2)}, u32[]{:S(2)}) collective-permute-start(bf16[32,32,256]{2,1,0:T(8,128)(2,1)S(1)} %combine.2.refs_5_.own), channel_id=1, source_target_pairs={{0,96},{32,0},{64,32},{96,64},{1,97},{33,1},{65,33},{97,65},{2,98}... | collective-permute-start | bytes 1572872 | tf_op jit(solution)/shard_map/ppermute | solution.py:404
  42.0 14.9 %collective-permute-start.7 = (bf16[32,32,256]{2,1,0:T(8,128)(2,1)S(1)}, bf16[32,32,256]{2,1,0:T(8,128)(2,1)S(1)}, u32[]{:S(2)}, u32[]{:S(2)}) collective-permute-start(bf16[32,32,256]{2,1,0:T(8,128)(2,1)S(1)} %combine.2.refs_5_.own), channel_id=1, source_target_pairs={{0,32},{32,64},{64,96},{96,0},{1,33},{33,65},{65,97},{97,1},{2,34}... | collective-permute-start | bytes 1572872 | tf_op jit(solution)/shard_map/ppermute | solution.py:401
  57.0 8.5 %collective-permute-start.8 = (bf16[16,32,256]{2,1,0:T(8,128)(2,1)S(1)}, bf16[16,32,256]{2,1,0:T(8,128)(2,1)S(1)}, u32[]{:S(2)}, u32[]{:S(2)}) collective-permute-start(bf16[16,32,256]{2,1,0:T(8,128)(2,1)S(1)} %get-tuple-element.23), channel_id=1, source_target_pairs={{0,32},{32,64},{64,96},{96,0},{1,33},{33,65},{65,97},{97,1},{2,34}... | collective-permute-start | bytes 786440 | tf_op jit(solution)/shard_map/ppermute | solution.py:401
  57.1 8.4 %collective-permute-start.9 = (bf16[16,32,256]{2,1,0:T(8,128)(2,1)S(1)}, bf16[16,32,256]{2,1,0:T(8,128)(2,1)S(1)}, u32[]{:S(2)}, u32[]{:S(2)}) collective-permute-start(bf16[16,32,256]{2,1,0:T(8,128)(2,1)S(1)} %get-tuple-element.24), channel_id=1, source_target_pairs={{0,96},{32,0},{64,32},{96,64},{1,97},{33,1},{65,33},{97,65},{2,98}... | collective-permute-start | bytes 786440 | tf_op jit(solution)/shard_map/ppermute | solution.py:404
  65.7 1.3 copy-start.6
  67.0 43.2 %all-to-all-start.1 = ((bf16[32,128,256]{2,1,0:T(8,128)(2,1)}), bf16[32,128,256]{2,1,0:T(8,128)(2,1)}, u32[]{:S(2)}, u32[]{:S(2)}) async-start(bf16[32,128,256]{2,1,0:T(8,128)(2,1)} %copy-done.6), calls=%async_computation.1 | async-start | bytes 4194304 | tf_op jit(solution)/shard_map/all_to_all | solution.py:407
  74.6 39.4 %copy-start = (bf16[32,64,256]{2,1,0:T(8,128)(2,1)}, bf16[32,64,256]{2,1,0:T(8,128)(2,1)S(1)}, u32[]{:S(2)}) copy-start(bf16[32,64,256]{2,1,0:T(8,128)(2,1)S(1)} %get-tuple-element.22.refs_1_.own) | copy-start | bytes 3145732
  74.6 26.5 %collective-permute-start.4 = (bf16[32,64,256]{2,1,0:T(8,128)(2,1)S(1)}, bf16[32,64,256]{2,1,0:T(8,128)(2,1)S(1)}, u32[]{:S(2)}, u32[]{:S(2)}) collective-permute-start(bf16[32,64,256]{2,1,0:T(8,128)(2,1)S(1)} %get-tuple-element.22.refs_1_.own), channel_id=1, source_target_pairs={{0,96},{32,0},{64,32},{96,64},{1,97},{33,1},{65,33},{97,65},{2,98}... | collective-permute-start | bytes 3145736 | tf_op jit(solution)/shard_map/ppermute | solution.py:404
  77.6 27.3 %collective-permute-start.5 = (bf16[32,64,256]{2,1,0:T(8,128)(2,1)S(1)}, bf16[32,64,256]{2,1,0:T(8,128)(2,1)S(1)}, u32[]{:S(2)}, u32[]{:S(2)}) collective-permute-start(bf16[32,64,256]{2,1,0:T(8,128)(2,1)S(1)} %get-tuple-element.22.refs_1_.own), channel_id=1, source_target_pairs={{0,32},{32,64},{64,96},{96,0},{1,33},{33,65},{65,97},{97,1},{2,34}... | collective-permute-start | bytes 3145736 | tf_op jit(solution)/shard_map/ppermute | solution.py:401
  77.6 40.0 %collective-permute-start.2 = (bf16[32,32,256]{2,1,0:T(8,128)(2,1)S(1)}, bf16[32,32,256]{2,1,0:T(8,128)(2,1)S(1)}, u32[]{:S(2)}, u32[]{:S(2)}) collective-permute-start(bf16[32,32,256]{2,1,0:T(8,128)(2,1)S(1)} %get-tuple-element.21.refs_1_), channel_id=1, source_target_pairs={{0,32},{32,64},{64,96},{96,0},{1,33},{33,65},{65,97},{97,1},{2,34}... | collective-permute-start | bytes 1572872 | tf_op jit(solution)/shard_map/ppermute | solution.py:401
  77.6 40.0 %collective-permute-start.3 = (bf16[32,32,256]{2,1,0:T(8,128)(2,1)S(1)}, bf16[32,32,256]{2,1,0:T(8,128)(2,1)}, u32[]{:S(2)}, u32[]{:S(2)}) collective-permute-start(bf16[32,32,256]{2,1,0:T(8,128)(2,1)S(1)} %get-tuple-element.21.refs_1_), channel_id=1, source_target_pairs={{0,96},{32,0},{64,32},{96,64},{1,97},{33,1},{65,33},{97,65},{2,98}... | collective-permute-start | bytes 1572872 | tf_op jit(solution)/shard_map/ppermute | solution.py:404
  101.1 12.8 %copy-start.2 = (bf16[32,64,256]{2,1,0:T(8,128)(2,1)}, bf16[32,64,256]{2,1,0:T(8,128)(2,1)S(1)}, u32[]{:S(2)}) copy-start(bf16[32,64,256]{2,1,0:T(8,128)(2,1)S(1)} %collective-permute-done.4.refs_2_.refs_1_) | copy-start | bytes 3145732
  105.9 1.0 copy-start.4
  106.9 21.3 %collective-permute-start.12 = (bf16[32,32,256]{2,1,0:T(8,128)(2,1)}, bf16[32,32,256]{2,1,0:T(8,128)(2,1)}, u32[]{:S(2)}, u32[]{:S(2)}) collective-permute-start(bf16[32,32,256]{2,1,0:T(8,128)(2,1)} %get-tuple-element.27), channel_id=1, source_target_pairs={{0,32},{32,64},{64,96},{96,0},{1,33},{33,65},{65,97},{97,1},{2,34}... | collective-permute-start | bytes 1572872 | tf_op jit(solution)/shard_map/ppermute | solution.py:401
  106.9 21.3 %collective-permute-start.13 = (bf16[32,32,256]{2,1,0:T(8,128)(2,1)}, bf16[32,32,256]{2,1,0:T(8,128)(2,1)}, u32[]{:S(2)}, u32[]{:S(2)}) collective-permute-start(bf16[32,32,256]{2,1,0:T(8,128)(2,1)} %get-tuple-element.28), channel_id=1, source_target_pairs={{0,96},{32,0},{64,32},{96,64},{1,97},{33,1},{65,33},{97,65},{2,98}... | collective-permute-start | bytes 1572872 | tf_op jit(solution)/shard_map/ppermute | solution.py:404
  117.6 4.5 %copy-start.1 = (bf16[32,64,256]{2,1,0:T(8,128)(2,1)S(1)}, bf16[32,64,256]{2,1,0:T(8,128)(2,1)}, u32[]{:S(2)}) copy-start(bf16[32,64,256]{2,1,0:T(8,128)(2,1)} %copy-done) | copy-start | bytes 3145732
  117.6 4.5 %copy-start.3 = (bf16[32,64,256]{2,1,0:T(8,128)(2,1)S(1)}, bf16[32,64,256]{2,1,0:T(8,128)(2,1)}, u32[]{:S(2)}) copy-start(bf16[32,64,256]{2,1,0:T(8,128)(2,1)} %copy-done.2) | copy-start | bytes 3145732
  117.6 4.5 %copy-start.5 = (bf16[32,64,256]{2,1,0:T(8,128)(2,1)S(1)}, bf16[32,64,256]{2,1,0:T(8,128)(2,1)}, u32[]{:S(2)}) copy-start(bf16[32,64,256]{2,1,0:T(8,128)(2,1)} %copy-done.4) | copy-start | bytes 3145732
  118.8 13.8 %collective-permute-start.10 = (bf16[16,32,256]{2,1,0:T(8,128)(2,1)S(1)}, bf16[16,32,256]{2,1,0:T(8,128)(2,1)S(1)}, u32[]{:S(2)}, u32[]{:S(2)}) collective-permute-start(bf16[16,32,256]{2,1,0:T(8,128)(2,1)S(1)} %get-tuple-element.25), channel_id=1, source_target_pairs={{0,32},{32,64},{64,96},{96,0},{1,33},{33,65},{65,97},{97,1},{2,34}... | collective-permute-start | bytes 786440 | tf_op jit(solution)/shard_map/ppermute | solution.py:401
  118.9 13.8 %collective-permute-start.11 = (bf16[16,32,256]{2,1,0:T(8,128)(2,1)S(1)}, bf16[16,32,256]{2,1,0:T(8,128)(2,1)S(1)}, u32[]{:S(2)}, u32[]{:S(2)}) collective-permute-start(bf16[16,32,256]{2,1,0:T(8,128)(2,1)S(1)} %get-tuple-element.26), channel_id=1, source_target_pairs={{0,96},{32,0},{64,32},{96,64},{1,97},{33,1},{65,33},{97,65},{2,98}... | collective-permute-start | bytes 786440 | tf_op jit(solution)/shard_map/ppermute | solution.py:404

commit v5 on v4

--- a/solution.py
+++ b/solution.py
@@ -17,7 +17,7 @@
 ROWS = 256
 LANES = 256
 VMEM = 48 * 1024 * 1024
-LARGE = 60 * 1024 * 1024
+LARGE = 62 * 1024 * 1024
 
 
 def halves(x):

time: 135 us -> 135 us (level)
    unnamed x20 -> x18, local copies, waits for them, and re-layouts: 4.52 us -> 4.72 us
where the time goes in v5:
time: 135 us
  waiting for transfers between devices  45.8 us (34%)
  Pallas kernels  45 us (33%)
  starting transfers between devices  38.8 us (29%)
  local copies, waits for them, and re-layouts  4.72 us (3%)
    ppermute x6, waiting for transfers between devices, down(): return lax.ppermute(x, 'inp', [(i, (i - 1) % ring) for i in range(ring)])  31.8 us
    pallas_call x3, Pallas kernels, spectra(): pl.pallas_call(kernel, out_shape=[jax.ShapeDtypeStruct((n * len(g), 256,...  20.8 us
    ppermute x6, starting transfers between devices, down(): return lax.ppermute(x, 'inp', [(i, (i - 1) % ring) for i in range(ring)])  19 us
    pallas_call x5, Pallas kernels, correlate(): pl.pallas_call(kernel, out_shape=jax.ShapeDtypeStruct((4, 4, ROWS, 1024),...  15.1 us
    all_to_all x2, starting transfers between devices, swap(): return lax.all_to_all(x, 'tm', split_axis=0, concat_axis=0, tiled=True)  13.8 us
    ppermute x6, waiting for transfers between devices, up(): return lax.ppermute(x, 'inp', [(i, (i + 1) % ring) for i in range(ring)])  12.3 us
    ppermute x2, starting transfers between devices, body(): halo.append(lax.ppermute(passed, 'tm', later))  5.85 us
    unnamed x18, local copies, waits for them, and re-layouts  4.72 us
  transfers between devices with their start and end apart: 16, of which 6 were waited for; matrix products, arithmetic and copies ran while one was open for 0% of the time, Pallas kernels for 27%

profile of v5, /device:TPU:2, one launch (start us, length us, event | category | flops | bytes accessed | tf_op | source)
XLA Modules:
  0.0 134.6 jit_solution(16190920123576180263)
XLA Ops:
  0.0 0.0 copy-start.7
  0.0 0.8 copy-done.7
  0.8 0.0 copy-start.8
  0.8 1.4 %copy-done.8 = bf16[256,3072]{1,0:T(8,128)(2,1)S(1)} copy-done((bf16[256,3072]{1,0:T(8,128)(2,1)S(1)}, bf16[256,3072]{1,0:T(8,128)(2,1)}, u32[]{:S(2)}) %copy-start.8) | copy-done | bytes 1572888
  2.2 4.5 %spectra.4 = bf16[12,256,128]{2,1,0:T(8,128)(2,1)S(1)} custom-call(bf16[256,4,2048]{2,1,0:T(4,128)(2,1)} %refs_0_.5, f32[4,2048]{1,0:T(4,128)S(1)} %copy-done.7, bf16[256,3072]{1,0:T(8,128)(2,1)S(1)} %copy-done.8), custom_call_target="tpu_custom_call" | custom-call | flops 3600000000 | bytes 12582912 | tf_op jit(solution)/shard_map/spectra/pallas_call | solution.py:139
  6.7 1.9 %collective-permute-start = (bf16[12,256,128]{2,1,0:T(8,128)(2,1)S(1)}, bf16[12,256,128]{2,1,0:T(8,128)(2,1)S(1)}, u32[]{:S(2)}, u32[]{:S(2)}) collective-permute-start(bf16[12,256,128]{2,1,0:T(8,128)(2,1)S(1)} %spectra.4), channel_id=1, source_target_pairs={{0,1},{1,2},{2,3},{3,4},{4,5},{5,6},{6,7},{7,8},{8,9},{9,10},{10,1... | collective-permute-start | bytes 2359304 | tf_op jit(solution)/shard_map/ppermute | solution.py:412
  8.6 4.5 %spectra.5 = bf16[12,256,128]{2,1,0:T(8,128)(2,1)S(1)} custom-call(bf16[256,4,2048]{2,1,0:T(4,128)(2,1)} %refs_0_.5, f32[4,2048]{1,0:T(4,128)S(1)} %copy-done.7, bf16[256,3072]{1,0:T(8,128)(2,1)S(1)} %copy-done.8), custom_call_target="tpu_custom_call" | custom-call | flops 3600000000 | bytes 12582912 | tf_op jit(solution)/shard_map/spectra/pallas_call | solution.py:139
  13.2 3.9 %collective-permute-start.1 = (bf16[12,256,128]{2,1,0:T(8,128)(2,1)S(1)}, bf16[12,256,128]{2,1,0:T(8,128)(2,1)S(1)}, u32[]{:S(2)}, u32[]{:S(2)}) collective-permute-start(bf16[12,256,128]{2,1,0:T(8,128)(2,1)S(1)} %spectra.5), channel_id=1, source_target_pairs={{0,1},{1,2},{2,3},{3,4},{4,5},{5,6},{6,7},{7,8},{8,9},{9,10},{10,1... | collective-permute-start | bytes 2359304 | tf_op jit(solution)/shard_map/ppermute | solution.py:412
  17.1 11.7 %spectra.3 = (f32[4,256,256]{2,1,0:T(8,128)S(1)}, f32[4,256,256]{2,1,0:T(8,128)S(1)}, f32[4,256,256]{2,1,0:T(8,128)S(1)}, f32[4,256,256]{2,1,0:T(8,128)S(1)}) custom-call(bf16[256,4,2048]{2,1,0:T(4,128)(2,1)} %refs_0_.5, f32[4,2048]{1,0:T(4,128)S(1)} %copy-done.7, bf16[256,3072]{1,0:T(8,128)(2,1)S(1)} %copy-done.8, bf16[256,3072]{1,0:T(8,128)(2,1)} %constant.11.clone.refs_3_), custom_call_target="tpu_custom_call" | custom-call | flops 4800000000 | bytes 12582912 | tf_op jit(solution)/shard_map/spectra/pallas_call | solution.py:139
  28.8 0.0 collective-permute-done.refs_1_.refs_3_
  28.9 1.7 %collective-permute-done.1.refs_2_.refs_4_ = bf16[12,256,128]{2,1,0:T(8,128)(2,1)S(1)} collective-permute-done((bf16[12,256,128]{2,1,0:T(8,128)(2,1)S(1)}, bf16[12,256,128]{2,1,0:T(8,128)(2,1)S(1)}, u32[]{:S(2)}, u32[]{:S(2)}) %collective-permute-start.1) | collective-permute-done | bytes 786464 | tf_op jit(solution)/shard_map/ppermute | solution.py:412
  30.6 0.2 combine.2.refs_5_.own
  30.8 1.8 %combine.3 = bf16[32,96,256]{2,1,0:T(8,128)(2,1)} custom-call(f32[4,256,256]{2,1,0:T(8,128)S(1)} %get-tuple-element.17.refs_0_, f32[4,256,256]{2,1,0:T(8,128)S(1)} %get-tuple-element.18.refs_1_, f32[4,256,256]{2,1,0:T(8,128)S(1)} %get-tuple-element.19.refs_2_, bf16[12,256,128]{2,1,0:T(8,128)(2,1)S(1)} %collective-permute-done.refs_1_.refs_3_, ...), custom_call_target="tpu_custom_call" | custom-call | flops 3145728 | bytes 6291456 | tf_op jit(solution)/shard_map/combine/pallas_call | solution.py:182
  32.6 6.4 %all-to-all-start = ((bf16[32,96,256]{2,1,0:T(8,128)(2,1)}), bf16[32,96,256]{2,1,0:T(8,128)(2,1)S(1)}, u32[]{:S(2)}, u32[]{:S(2)}) async-start(bf16[32,96,256]{2,1,0:T(8,128)(2,1)} %combine.3), calls=%async_computation | async-start | bytes 3145728 | tf_op jit(solution)/shard_map/all_to_all | solution.py:407
  39.0 3.1 %collective-permute-start.6 = (bf16[32,32,256]{2,1,0:T(8,128)(2,1)S(1)}, bf16[32,32,256]{2,1,0:T(8,128)(2,1)S(1)}, u32[]{:S(2)}, u32[]{:S(2)}) collective-permute-start(bf16[32,32,256]{2,1,0:T(8,128)(2,1)S(1)} %combine.2.refs_5_.own), channel_id=1, source_target_pairs={{0,96},{32,0},{64,32},{96,64},{1,97},{33,1},{65,33},{97,65},{2,98}... | collective-permute-start | bytes 1572872 | tf_op jit(solution)/shard_map/ppermute | solution.py:404
  42.0 0.0 collective-permute-start.7
  42.0 11.5 %collective-permute-done.6.refs_1_.right = bf16[32,32,256]{2,1,0:T(8,128)(2,1)S(1)} collective-permute-done((bf16[32,32,256]{2,1,0:T(8,128)(2,1)S(1)}, bf16[32,32,256]{2,1,0:T(8,128)(2,1)S(1)}, u32[]{:S(2)}, u32[]{:S(2)}) %collective-permute-start.6) | collective-permute-done | bytes 524320 | tf_op jit(solution)/shard_map/ppermute | solution.py:404
  53.5 3.4 %collective-permute-done.7.refs_0_.left = bf16[32,32,256]{2,1,0:T(8,128)(2,1)S(1)} collective-permute-done((bf16[32,32,256]{2,1,0:T(8,128)(2,1)S(1)}, bf16[32,32,256]{2,1,0:T(8,128)(2,1)S(1)}, u32[]{:S(2)}, u32[]{:S(2)}) %collective-permute-start.7) | collective-permute-done | bytes 524320 | tf_op jit(solution)/shard_map/ppermute | solution.py:401
  57.0 0.1 collective-permute-start.8
  57.1 3.2 %collective-permute-start.9 = (bf16[16,32,256]{2,1,0:T(8,128)(2,1)S(1)}, bf16[16,32,256]{2,1,0:T(8,128)(2,1)S(1)}, u32[]{:S(2)}, u32[]{:S(2)}) collective-permute-start(bf16[16,32,256]{2,1,0:T(8,128)(2,1)S(1)} %get-tuple-element.24), channel_id=1, source_target_pairs={{0,96},{32,0},{64,32},{96,64},{1,97},{33,1},{65,33},{97,65},{2,98}... | collective-permute-start | bytes 786440 | tf_op jit(solution)/shard_map/ppermute | solution.py:404
  60.3 5.2 %collective-permute-done.8.far_a = bf16[16,32,256]{2,1,0:T(8,128)(2,1)S(1)} collective-permute-done((bf16[16,32,256]{2,1,0:T(8,128)(2,1)S(1)}, bf16[16,32,256]{2,1,0:T(8,128)(2,1)S(1)}, u32[]{:S(2)}, u32[]{:S(2)}) %collective-permute-start.8) | collective-permute-done | bytes 262176 | tf_op jit(solution)/shard_map/ppermute | solution.py:401
  65.5 0.0 collective-permute-done.9.far_b
  65.5 0.2 pack.1
  65.7 0.0 copy-start.6
  65.7 1.3 copy-done.6
  67.0 0.0 all-to-all-done.refs_0_.refs_1_
  67.0 7.4 %all-to-all-start.1 = ((bf16[32,128,256]{2,1,0:T(8,128)(2,1)}), bf16[32,128,256]{2,1,0:T(8,128)(2,1)}, u32[]{:S(2)}, u32[]{:S(2)}) async-start(bf16[32,128,256]{2,1,0:T(8,128)(2,1)} %copy-done.6), calls=%async_computation.1 | async-start | bytes 4194304 | tf_op jit(solution)/shard_map/all_to_all | solution.py:407
  74.5 0.1 take.4
  74.6 0.0 copy-start
  74.6 3.0 %collective-permute-start.4 = (bf16[32,64,256]{2,1,0:T(8,128)(2,1)S(1)}, bf16[32,64,256]{2,1,0:T(8,128)(2,1)S(1)}, u32[]{:S(2)}, u32[]{:S(2)}) collective-permute-start(bf16[32,64,256]{2,1,0:T(8,128)(2,1)S(1)} %get-tuple-element.22.refs_1_.own), channel_id=1, source_target_pairs={{0,96},{32,0},{64,32},{96,64},{1,97},{33,1},{65,33},{97,65},{2,98}... | collective-permute-start | bytes 3145736 | tf_op jit(solution)/shard_map/ppermute | solution.py:404
  77.6 0.0 collective-permute-start.5
  77.6 0.0 collective-permute-start.2
  77.6 3.3 %collective-permute-start.3 = (bf16[32,32,256]{2,1,0:T(8,128)(2,1)S(1)}, bf16[32,32,256]{2,1,0:T(8,128)(2,1)}, u32[]{:S(2)}, u32[]{:S(2)}) collective-permute-start(bf16[32,32,256]{2,1,0:T(8,128)(2,1)S(1)} %get-tuple-element.21.refs_1_), channel_id=1, source_target_pairs={{0,96},{32,0},{64,32},{96,64},{1,97},{33,1},{65,33},{97,65},{2,98}... | collective-permute-start | bytes 1572872 | tf_op jit(solution)/shard_map/ppermute | solution.py:404
  80.9 20.3 %collective-permute-done.4.refs_2_.refs_1_ = bf16[32,64,256]{2,1,0:T(8,128)(2,1)S(1)} collective-permute-done((bf16[32,64,256]{2,1,0:T(8,128)(2,1)S(1)}, bf16[32,64,256]{2,1,0:T(8,128)(2,1)S(1)}, u32[]{:S(2)}, u32[]{:S(2)}) %collective-permute-start.4) | collective-permute-done | bytes 1048608 | tf_op jit(solution)/shard_map/ppermute | solution.py:404
  101.1 3.7 %collective-permute-done.5.refs_3_.refs_0_ = bf16[32,64,256]{2,1,0:T(8,128)(2,1)S(1)} collective-permute-done((bf16[32,64,256]{2,1,0:T(8,128)(2,1)S(1)}, bf16[32,64,256]{2,1,0:T(8,128)(2,1)S(1)}, u32[]{:S(2)}, u32[]{:S(2)}) %collective-permute-start.5) | collective-permute-done | bytes 1048608 | tf_op jit(solution)/shard_map/ppermute | solution.py:401
  104.9 0.0 copy-start.4
  104.9 1.1 take.7
  106.0 0.2 copy-done.4
  106.2 0.0 copy-start.2
  106.2 1.0 copy-done.2
  107.2 0.0 collective-permute-start.12
  107.2 3.2 %collective-permute-start.13 = (bf16[32,32,256]{2,1,0:T(8,128)(2,1)}, bf16[32,32,256]{2,1,0:T(8,128)(2,1)}, u32[]{:S(2)}, u32[]{:S(2)}) collective-permute-start(bf16[32,32,256]{2,1,0:T(8,128)(2,1)} %get-tuple-element.28), channel_id=1, source_target_pairs={{0,96},{32,0},{64,32},{96,64},{1,97},{33,1},{65,33},{97,65},{2,98}... | collective-permute-start | bytes 1572872 | tf_op jit(solution)/shard_map/ppermute | solution.py:404
  110.4 0.0 all-to-all-done.1.refs_1_.refs_2_.refs_3_.refs_4_
  110.4 3.8 %correlate.5.refs_4_ = f32[4,4,256,1024]{3,2,1,0:T(8,128)} custom-call(s32[1]{0:T(128)} %bitcast.refs_0_.place, bf16[32,128,256]{2,1,0:T(8,128)(2,1)} %all-to-all-done.1.refs_1_.refs_2_.refs_3_.refs_4_, bf16[32,128,256]{2,1,0:T(8,128)(2,1)} %all-to-all-done.1.refs_1_.refs_2_.refs_3_.refs_4_, ...), custom_call_target="tpu_custom_call" | custom-call | flops 640000000 | bytes 6291456 | tf_op jit(solution)/shard_map/correlate/pallas_call | solution.py:339
  114.2 0.0 copy-done
  114.2 3.6 %correlate.6.refs_2_.refs_4_ = f32[4,4,256,1024]{3,2,1,0:T(8,128)} custom-call(s32[1]{0:T(128)} %bitcast.refs_0_.place, bf16[32,64,256]{2,1,0:T(8,128)(2,1)} %copy-done, bf16[32,64,256]{2,1,0:T(8,128)(2,1)} %copy-done.2, bf16[32,64,256]{2,1,0:T(8,128)(2,1)} %copy-done.4, f32[4,4,256,1024]{3,2,1,0:T(8,128)} %correlate.5.refs_4_), custom_call_target="tpu_custom_call", output_to_operand_aliasing={{}: (4, {})} | custom-call | flops 480000000 | bytes 6291456 | tf_op jit(solution)/shard_map/correlate/pallas_call | solution.py:339
  117.9 0.0 copy-start.1
  117.9 0.0 copy-start.3
  117.9 0.0 collective-permute-done.2.refs_0_.refs_3_
  117.9 0.0 collective-permute-done.3.refs_1_.refs_2_
  117.9 1.2 take.6
  119.1 0.1 collective-permute-start.10
  119.2 3.2 %collective-permute-start.11 = (bf16[16,32,256]{2,1,0:T(8,128)(2,1)S(1)}, bf16[16,32,256]{2,1,0:T(8,128)(2,1)S(1)}, u32[]{:S(2)}, u32[]{:S(2)}) collective-permute-start(bf16[16,32,256]{2,1,0:T(8,128)(2,1)S(1)} %get-tuple-element.26), channel_id=1, source_target_pairs={{0,96},{32,0},{64,32},{96,64},{1,97},{33,1},{65,33},{97,65},{2,98}... | collective-permute-start | bytes 786440 | tf_op jit(solution)/shard_map/ppermute | solution.py:404
  122.4 0.0 copy-done.1
  122.4 0.0 copy-done.3
  122.4 0.0 copy-done.5
  122.4 2.7 %correlate.7.refs_4_ = f32[4,4,256,1024]{3,2,1,0:T(8,128)} custom-call(s32[1]{0:T(128)} %bitcast.refs_0_.place, bf16[32,64,256]{2,1,0:T(8,128)(2,1)S(1)} %copy-done.1, bf16[32,64,256]{2,1,0:T(8,128)(2,1)S(1)} %copy-done.3, bf16[32,64,256]{2,1,0:T(8,128)(2,1)S(1)} %copy-done.5, ...), custom_call_target="tpu_custom_call", output_to_operand_aliasing={{}: (4, {})} | custom-call | flops 480000000 | bytes 6291456 | tf_op jit(solution)/shard_map/correlate/pallas_call | solution.py:339
  125.1 3.6 %correlate.8._ = f32[4,4,256,1024]{3,2,1,0:T(8,128)} custom-call(s32[1]{0:T(128)} %bitcast.refs_0_.place, bf16[32,32,256]{2,1,0:T(8,128)(2,1)S(1)} %get-tuple-element.21.refs_1_, bf16[32,32,256]{2,1,0:T(8,128)(2,1)} %collective-permute-done.3.refs_1_.refs_2_, ...), custom_call_target="tpu_custom_call", output_to_operand_aliasing={{}: (4, {})} | custom-call | flops 480000000 | bytes 6291456 | tf_op jit(solution)/shard_map/correlate/pallas_call | solution.py:339
  128.6 0.0 collective-permute-done.12.first
  128.6 0.0 collective-permute-done.13.second
  128.6 4.4 %correlate_far.1.refs_4_ = f32[4,4,256,1024]{3,2,1,0:T(8,128)} custom-call(s32[1]{0:T(128)} %bitcast.refs_0_.place, bf16[32,64,256]{2,1,0:T(8,128)(2,1)S(1)} %copy-done.1, bf16[32,32,256]{2,1,0:T(8,128)(2,1)} %collective-permute-done.12.first, bf16[32,32,256]{2,1,0:T(8,128)(2,1)} %collective-permute-done.13.second, ...), custom_call_target="tpu_custom_call", output_to_operand_aliasing={{}: (4, {})} | custom-call | flops 320000000 | bytes 6291456 | tf_op jit(solution)/shard_map/correlate_far/pallas_call | solution.py:380
  133.0 0.0 collective-permute-done.10.refs_2_
  133.0 0.0 collective-permute-done.11.refs_3_
  133.0 1.5 %correlate.9 = f32[4,4,256,1024]{3,2,1,0:T(8,128)} custom-call(s32[1]{0:T(128)} %bitcast.refs_0_.place, bf16[32,32,256]{2,1,0:T(8,128)(2,1)S(1)} %get-tuple-element.21.refs_1_, bf16[16,32,256]{2,1,0:T(8,128)(2,1)S(1)} %collective-permute-done.10.refs_2_, bf16[16,32,256]{2,1,0:T(8,128)(2,1)S(1)} %collective-permute-done.11.refs_3_, ...), custom_call_target="tpu_custom_call", output_to_operand_aliasing={{}: (4, {})} | custom-call | flops 160000000 | bytes 6291456 | tf_op jit(solution)/shard_map/correlate/pallas_call | solution.py:339
  (2 shorter events, 0.0 us)
Async XLA Ops:
  0.0 0.8 copy-start.7
  0.8 1.4 %copy-start.8 = (bf16[256,3072]{1,0:T(8,128)(2,1)S(1)}, bf16[256,3072]{1,0:T(8,128)(2,1)}, u32[]{:S(2)}) copy-start(bf16[256,3072]{1,0:T(8,128)(2,1)} %constant.10.clone.refs_2_) | copy-start | bytes 4718596
  6.7 22.1 %collective-permute-start = (bf16[12,256,128]{2,1,0:T(8,128)(2,1)S(1)}, bf16[12,256,128]{2,1,0:T(8,128)(2,1)S(1)}, u32[]{:S(2)}, u32[]{:S(2)}) collective-permute-start(bf16[12,256,128]{2,1,0:T(8,128)(2,1)S(1)} %spectra.4), channel_id=1, source_target_pairs={{0,1},{1,2},{2,3},{3,4},{4,5},{5,6},{6,7},{7,8},{8,9},{9,10},{10,1... | collective-permute-start | bytes 2359304 | tf_op jit(solution)/shard_map/ppermute | solution.py:412
  13.2 17.4 %collective-permute-start.1 = (bf16[12,256,128]{2,1,0:T(8,128)(2,1)S(1)}, bf16[12,256,128]{2,1,0:T(8,128)(2,1)S(1)}, u32[]{:S(2)}, u32[]{:S(2)}) collective-permute-start(bf16[12,256,128]{2,1,0:T(8,128)(2,1)S(1)} %spectra.5), channel_id=1, source_target_pairs={{0,1},{1,2},{2,3},{3,4},{4,5},{5,6},{6,7},{7,8},{8,9},{9,10},{10,1... | collective-permute-start | bytes 2359304 | tf_op jit(solution)/shard_map/ppermute | solution.py:412
  32.6 34.4 %all-to-all-start = ((bf16[32,96,256]{2,1,0:T(8,128)(2,1)}), bf16[32,96,256]{2,1,0:T(8,128)(2,1)S(1)}, u32[]{:S(2)}, u32[]{:S(2)}) async-start(bf16[32,96,256]{2,1,0:T(8,128)(2,1)} %combine.3), calls=%async_computation | async-start | bytes 3145728 | tf_op jit(solution)/shard_map/all_to_all | solution.py:407
  39.0 14.6 %collective-permute-start.6 = (bf16[32,32,256]{2,1,0:T(8,128)(2,1)S(1)}, bf16[32,32,256]{2,1,0:T(8,128)(2,1)S(1)}, u32[]{:S(2)}, u32[]{:S(2)}) collective-permute-start(bf16[32,32,256]{2,1,0:T(8,128)(2,1)S(1)} %combine.2.refs_5_.own), channel_id=1, source_target_pairs={{0,96},{32,0},{64,32},{96,64},{1,97},{33,1},{65,33},{97,65},{2,98}... | collective-permute-start | bytes 1572872 | tf_op jit(solution)/shard_map/ppermute | solution.py:404
  42.0 14.9 %collective-permute-start.7 = (bf16[32,32,256]{2,1,0:T(8,128)(2,1)S(1)}, bf16[32,32,256]{2,1,0:T(8,128)(2,1)S(1)}, u32[]{:S(2)}, u32[]{:S(2)}) collective-permute-start(bf16[32,32,256]{2,1,0:T(8,128)(2,1)S(1)} %combine.2.refs_5_.own), channel_id=1, source_target_pairs={{0,32},{32,64},{64,96},{96,0},{1,33},{33,65},{65,97},{97,1},{2,34}... | collective-permute-start | bytes 1572872 | tf_op jit(solution)/shard_map/ppermute | solution.py:401
  57.0 8.5 %collective-permute-start.8 = (bf16[16,32,256]{2,1,0:T(8,128)(2,1)S(1)}, bf16[16,32,256]{2,1,0:T(8,128)(2,1)S(1)}, u32[]{:S(2)}, u32[]{:S(2)}) collective-permute-start(bf16[16,32,256]{2,1,0:T(8,128)(2,1)S(1)} %get-tuple-element.23), channel_id=1, source_target_pairs={{0,32},{32,64},{64,96},{96,0},{1,33},{33,65},{65,97},{97,1},{2,34}... | collective-permute-start | bytes 786440 | tf_op jit(solution)/shard_map/ppermute | solution.py:401
  57.1 8.4 %collective-permute-start.9 = (bf16[16,32,256]{2,1,0:T(8,128)(2,1)S(1)}, bf16[16,32,256]{2,1,0:T(8,128)(2,1)S(1)}, u32[]{:S(2)}, u32[]{:S(2)}) collective-permute-start(bf16[16,32,256]{2,1,0:T(8,128)(2,1)S(1)} %get-tuple-element.24), channel_id=1, source_target_pairs={{0,96},{32,0},{64,32},{96,64},{1,97},{33,1},{65,33},{97,65},{2,98}... | collective-permute-start | bytes 786440 | tf_op jit(solution)/shard_map/ppermute | solution.py:404
  65.7 1.3 copy-start.6
  67.0 43.4 %all-to-all-start.1 = ((bf16[32,128,256]{2,1,0:T(8,128)(2,1)}), bf16[32,128,256]{2,1,0:T(8,128)(2,1)}, u32[]{:S(2)}, u32[]{:S(2)}) async-start(bf16[32,128,256]{2,1,0:T(8,128)(2,1)} %copy-done.6), calls=%async_computation.1 | async-start | bytes 4194304 | tf_op jit(solution)/shard_map/all_to_all | solution.py:407
  74.6 39.6 %copy-start = (bf16[32,64,256]{2,1,0:T(8,128)(2,1)}, bf16[32,64,256]{2,1,0:T(8,128)(2,1)S(1)}, u32[]{:S(2)}) copy-start(bf16[32,64,256]{2,1,0:T(8,128)(2,1)S(1)} %get-tuple-element.22.refs_1_.own) | copy-start | bytes 3145732
  74.6 26.5 %collective-permute-start.4 = (bf16[32,64,256]{2,1,0:T(8,128)(2,1)S(1)}, bf16[32,64,256]{2,1,0:T(8,128)(2,1)S(1)}, u32[]{:S(2)}, u32[]{:S(2)}) collective-permute-start(bf16[32,64,256]{2,1,0:T(8,128)(2,1)S(1)} %get-tuple-element.22.refs_1_.own), channel_id=1, source_target_pairs={{0,96},{32,0},{64,32},{96,64},{1,97},{33,1},{65,33},{97,65},{2,98}... | collective-permute-start | bytes 3145736 | tf_op jit(solution)/shard_map/ppermute | solution.py:404
  77.6 27.3 %collective-permute-start.5 = (bf16[32,64,256]{2,1,0:T(8,128)(2,1)S(1)}, bf16[32,64,256]{2,1,0:T(8,128)(2,1)S(1)}, u32[]{:S(2)}, u32[]{:S(2)}) collective-permute-start(bf16[32,64,256]{2,1,0:T(8,128)(2,1)S(1)} %get-tuple-element.22.refs_1_.own), channel_id=1, source_target_pairs={{0,32},{32,64},{64,96},{96,0},{1,33},{33,65},{65,97},{97,1},{2,34}... | collective-permute-start | bytes 3145736 | tf_op jit(solution)/shard_map/ppermute | solution.py:401
  77.6 40.3 %collective-permute-start.2 = (bf16[32,32,256]{2,1,0:T(8,128)(2,1)S(1)}, bf16[32,32,256]{2,1,0:T(8,128)(2,1)}, u32[]{:S(2)}, u32[]{:S(2)}) collective-permute-start(bf16[32,32,256]{2,1,0:T(8,128)(2,1)S(1)} %get-tuple-element.21.refs_1_), channel_id=1, source_target_pairs={{0,32},{32,64},{64,96},{96,0},{1,33},{33,65},{65,97},{97,1},{2,34}... | collective-permute-start | bytes 1572872 | tf_op jit(solution)/shard_map/ppermute | solution.py:401
  77.6 40.3 %collective-permute-start.3 = (bf16[32,32,256]{2,1,0:T(8,128)(2,1)S(1)}, bf16[32,32,256]{2,1,0:T(8,128)(2,1)}, u32[]{:S(2)}, u32[]{:S(2)}) collective-permute-start(bf16[32,32,256]{2,1,0:T(8,128)(2,1)S(1)} %get-tuple-element.21.refs_1_), channel_id=1, source_target_pairs={{0,96},{32,0},{64,32},{96,64},{1,97},{33,1},{65,33},{97,65},{2,98}... | collective-permute-start | bytes 1572872 | tf_op jit(solution)/shard_map/ppermute | solution.py:404
  104.9 1.3 copy-start.4
  106.2 1.0 copy-start.2
  107.2 21.4 %collective-permute-start.12 = (bf16[32,32,256]{2,1,0:T(8,128)(2,1)}, bf16[32,32,256]{2,1,0:T(8,128)(2,1)}, u32[]{:S(2)}, u32[]{:S(2)}) collective-permute-start(bf16[32,32,256]{2,1,0:T(8,128)(2,1)} %get-tuple-element.27), channel_id=1, source_target_pairs={{0,32},{32,64},{64,96},{96,0},{1,33},{33,65},{65,97},{97,1},{2,34}... | collective-permute-start | bytes 1572872 | tf_op jit(solution)/shard_map/ppermute | solution.py:401
  107.2 21.4 %collective-permute-start.13 = (bf16[32,32,256]{2,1,0:T(8,128)(2,1)}, bf16[32,32,256]{2,1,0:T(8,128)(2,1)}, u32[]{:S(2)}, u32[]{:S(2)}) collective-permute-start(bf16[32,32,256]{2,1,0:T(8,128)(2,1)} %get-tuple-element.28), channel_id=1, source_target_pairs={{0,96},{32,0},{64,32},{96,64},{1,97},{33,1},{65,33},{97,65},{2,98}... | collective-permute-start | bytes 1572872 | tf_op jit(solution)/shard_map/ppermute | solution.py:404
  117.9 4.6 %copy-start.1 = (bf16[32,64,256]{2,1,0:T(8,128)(2,1)S(1)}, bf16[32,64,256]{2,1,0:T(8,128)(2,1)}, u32[]{:S(2)}) copy-start(bf16[32,64,256]{2,1,0:T(8,128)(2,1)} %copy-done) | copy-start | bytes 3145732
  117.9 4.6 %copy-start.3 = (bf16[32,64,256]{2,1,0:T(8,128)(2,1)S(1)}, bf16[32,64,256]{2,1,0:T(8,128)(2,1)}, u32[]{:S(2)}) copy-start(bf16[32,64,256]{2,1,0:T(8,128)(2,1)} %copy-done.2) | copy-start | bytes 3145732
  117.9 4.6 %copy-start.5 = (bf16[32,64,256]{2,1,0:T(8,128)(2,1)S(1)}, bf16[32,64,256]{2,1,0:T(8,128)(2,1)}, u32[]{:S(2)}) copy-start(bf16[32,64,256]{2,1,0:T(8,128)(2,1)} %copy-done.4) | copy-start | bytes 3145732
  119.1 13.9 %collective-permute-start.10 = (bf16[16,32,256]{2,1,0:T(8,128)(2,1)S(1)}, bf16[16,32,256]{2,1,0:T(8,128)(2,1)S(1)}, u32[]{:S(2)}, u32[]{:S(2)}) collective-permute-start(bf16[16,32,256]{2,1,0:T(8,128)(2,1)S(1)} %get-tuple-element.25), channel_id=1, source_target_pairs={{0,32},{32,64},{64,96},{96,0},{1,33},{33,65},{65,97},{97,1},{2,34}... | collective-permute-start | bytes 786440 | tf_op jit(solution)/shard_map/ppermute | solution.py:401
  119.2 13.8 %collective-permute-start.11 = (bf16[16,32,256]{2,1,0:T(8,128)(2,1)S(1)}, bf16[16,32,256]{2,1,0:T(8,128)(2,1)S(1)}, u32[]{:S(2)}, u32[]{:S(2)}) collective-permute-start(bf16[16,32,256]{2,1,0:T(8,128)(2,1)S(1)} %get-tuple-element.26), channel_id=1, source_target_pairs={{0,96},{32,0},{64,32},{96,64},{1,97},{33,1},{65,33},{97,65},{2,98}... | collective-permute-start | bytes 786440 | tf_op jit(solution)/shard_map/ppermute | solution.py:404
